TPU v7x, 256 devices: a whole 4x4x8 slice. The times are simulated.
256 devices in a mesh: ctx: 16 (over x, y), dp: 16 (over z, core).
Axes of the slice: x: 4, y: 4, z: 8, core: 2. Of those that a mesh axis runs over, the one named last changes fastest.
Arguments:
- inputs: bfloat16 [32, 2048, 1024], P('dp', 'ctx'), may hold values from -6 to 6
- gate_in: bfloat16 [32, 2048, 1024], P('dp', 'ctx'), may hold values from -6 to 6
- cotangent: bfloat16 [32, 2048, 1024], P('dp', 'ctx'), may hold values from -6 to 6
- recon_mask: int32 [32, 2048], P('dp', 'ctx'), may hold values 0 or 1
- segment_starts: int32 [32, 3], P('dp'), may hold values from 1 to 2047
- weights: bfloat16 [1024, 2048], replicated, may hold values from -0.1875 to 0.1875
- gate_bias: float32 [2048], replicated, may hold values from -4 to 4
- decay_rate: float32 [1024], replicated, may hold values from 9.765625e-07 to 0.01
Outputs:
- input_grad: bfloat16 [32, 2048, 1024], P('dp', 'ctx')
- gate_grad: bfloat16 [32, 2048, 1024], P('dp', 'ctx')
- weight_grads: float32 [1024, 2048], P('ctx', 'dp')
Inputs may be any that keep to these rules, and one draw needn't show every extreme that they name: `segment_starts`: each entry is a position of its row at which a new packed sequence begins; entries may repeat and come in any order.
All inputs are finite; a program needn't handle non-finite values. No bound on the sum of `recon_mask` on one device may be relied on, other than what follows from the above.
Results may differ from a plain program's by a relative error of at most 0.0044.
Values sent between devices are 32-bit elements; how exact they have to be, the bound alone decides.
No kernel may reach another device: no remote copies, remote signals or barrier semaphores. Data moves between devices by JAX's collectives and lax.ppermute only.
A program may use at most 128 MiB of HBM per device.

v0:
```python
import math

import jax
import jax.numpy as jnp
from jax import lax
from jax.sharding import PartitionSpec as P


def entering(value, axis, combine, identity, reverse):
    peers, place = (lax.axis_size(axis), lax.axis_index(axis))
    everything = jax.tree.map(lambda part: lax.all_gather(part, axis), value)
    start = jax.tree.map(
        lambda part, zero: jnp.broadcast_to(jnp.asarray(zero, part.dtype), part.shape),
        value,
        identity,
    )

    def lap(k, before):
        at = peers - 1 - k if reverse else k
        reached = at > place if reverse else at < place
        new = combine(before, jax.tree.map(lambda part: part[at], everything))
        return jax.tree.map(lambda a, b: jnp.where(reached, a, b), new, before)

    return lax.fori_loop(0, peers, lap, start)


def combine(earlier, latter):
    return (earlier[0] * latter[0], latter[0] * earlier[1] + latter[1])


def per_device(
    inputs, gate_in, cotangent, recon_mask, segment_starts, weights, gate_bias, decay_rate
):
    rows_dev, slab_steps, model_width = inputs.shape
    ctx_count = lax.axis_size("ctx")
    ctx_index = lax.axis_index("ctx")
    preact = (
        jnp.einsum("rsd,de->rse", inputs, weights, preferred_element_type=jnp.float32) + gate_bias
    )
    gate_decay = jax.nn.sigmoid(preact[..., :model_width])
    gate_input = jax.nn.sigmoid(preact[..., model_width:])
    position = ctx_index * slab_steps + jnp.arange(slab_steps, dtype=jnp.int32)
    start_hit = (
        jnp.any(position[None, :, None] == segment_starts[:, None, :], axis=2)
        | (position == 0)[None, :]
    )
    reset_flag = start_hit.astype(jnp.float32)[..., None]
    carry_keep = 1.0 - reset_flag
    decay_arg = 8.0 * decay_rate * gate_decay
    decay_step = jnp.exp(-decay_arg)
    step_decay = carry_keep * decay_step
    norm_square = -jnp.expm1(-2.0 * decay_arg)
    input_norm = reset_flag + carry_keep * jnp.sqrt(norm_square)
    inputs_wide = inputs.astype(jnp.float32)
    drive_term = input_norm * gate_input * inputs_wide
    decay_local, hidden_local = lax.associative_scan(combine, (step_decay, drive_term), axis=1)
    grad_out = recon_mask.astype(jnp.float32)[..., None] * cotangent.astype(jnp.float32)
    gelu_value, gelu_back = jax.vjp(jax.nn.gelu, gate_in.astype(jnp.float32))
    grad_hidden = grad_out * gelu_value
    back_decay, back_local = lax.associative_scan(
        combine, (step_decay, step_decay * grad_hidden), axis=1, reverse=True
    )
    unit_scale = jnp.ones((rows_dev, model_width), jnp.float32)
    zero_state = jnp.zeros((rows_dev, model_width), jnp.float32)
    hidden_carry = entering(
        (decay_local[:, -1], hidden_local[:, -1]), "ctx", combine, (unit_scale, zero_state), False
    )[1]
    adjoint_carry = entering(
        (back_decay[:, 0], back_local[:, 0]), "ctx", combine, (unit_scale, zero_state), True
    )[1]
    hidden = hidden_local + decay_local * hidden_carry[:, None, :]
    hidden_prev = jnp.concatenate([hidden_carry[:, None, :], hidden[:, :-1]], axis=1)
    carried = back_local + back_decay * adjoint_carry[:, None, :]
    adjoint = grad_hidden + jnp.concatenate([carried[:, 1:], adjoint_carry[:, None, :]], axis=1)
    gate_grad = gelu_back(grad_out * hidden)[0].astype(jnp.bfloat16)
    ratio_term = decay_arg / norm_square
    grad_decay_gate = (
        (1.0 - gate_decay)
        * decay_arg
        * (
            carry_keep
            * decay_step
            * decay_step
            * input_norm
            * ratio_term
            * adjoint
            * gate_input
            * inputs_wide
            - step_decay * adjoint * hidden_prev
        )
    )
    grad_input_gate = adjoint * input_norm * inputs_wide * gate_input * (1.0 - gate_input)
    grad_preact = jnp.concatenate([grad_decay_gate, grad_input_gate], axis=-1).astype(jnp.bfloat16)
    back_term = jnp.einsum("rse,de->rsd", grad_preact, weights, preferred_element_type=jnp.float32)
    input_grad = (adjoint * input_norm * gate_input + back_term).astype(jnp.bfloat16)
    flat_inputs = inputs.reshape(rows_dev * slab_steps, model_width)
    flat_grads = grad_preact.reshape(rows_dev * slab_steps, 2 * model_width)
    scale_factor = 1.0 / math.sqrt(rows_dev * lax.axis_size("dp") * slab_steps * ctx_count)
    partial_grad = jnp.einsum(
        "td,te->de", flat_inputs, flat_grads, preferred_element_type=jnp.float32
    )
    column_sums = lax.psum_scatter(partial_grad, "dp", scatter_dimension=1, tiled=True)
    weight_sum = lax.psum_scatter(column_sums, "ctx", scatter_dimension=0, tiled=True)
    return (input_grad, gate_grad, weight_sum * scale_factor)


def solution(mesh):
    return jax.shard_map(
        per_device,
        mesh=mesh,
        in_specs=(
            P("dp", "ctx", None),
            P("dp", "ctx", None),
            P("dp", "ctx", None),
            P("dp", "ctx"),
            P("dp", None),
            P(),
            P(),
            P(),
        ),
        out_specs=(P("dp", "ctx", None), P("dp", "ctx", None), P("ctx", "dp")),
        check_vma=False,
    )
```

profile of v0, /device:TPU:8, one launch (start us, length us, event | category | flops | bytes accessed | tf_op | source)
XLA Modules:
  0.0 580.4 jit_solution(15532568391106494759)
XLA Ops:
  9.4 3.7 fusion.6
  16.2 3.3 slice.550
  19.5 3.3 slice.549
  84.7 3.3 slice.579
  148.2 23.6 %all-gather.2 = f32[32,1,1024]{2,1,0:T(1,128)S(1)} all-gather(f32[2,1,1024]{2,1,0:T(1,128)S(1)} %slice_add_fusion.4), channel_id=4, replica_groups=mesh['ctx'=16,'dp'=16] {'ctx'}, dimensions={0}, use_global_device_ids=true | all-gather | bytes 139264 | tf_op jit(solution)/shard_map/all_gather | solution.py:11
  180.9 22.1 %all-gather.3 = f32[32,1,1024]{2,1,0:T(1,128)S(1)} all-gather(f32[2,1,1024]{2,1,0:T(1,128)S(1)} %slice_add_fusion.1), channel_id=5, replica_groups=mesh['ctx'=16,'dp'=16] {'ctx'}, dimensions={0}, use_global_device_ids=true | all-gather | bytes 139264 | tf_op jit(solution)/shard_map/all_gather | solution.py:11
  204.2 4.7 fusion.18
  209.4 4.7 slice.447
  214.2 3.3 slice.450
  217.4 3.3 slice.448
  220.7 4.8 slice.454
  225.4 4.7 slice.451
  230.2 4.7 slice.449
  293.2 3.3 slice.498
  309.6 4.8 slice.499
  314.4 4.8 slice.445
  349.1 22.6 %all-gather = f32[32,1,1024]{2,1,0:T(1,128)S(1)} all-gather(f32[2,1,1024]{2,1,0:T(1,128)S(1)} %slice_add_fusion.6), channel_id=2, replica_groups=mesh['ctx'=16,'dp'=16] {'ctx'}, dimensions={0}, use_global_device_ids=true | all-gather | bytes 139264 | tf_op jit(solution)/shard_map/all_gather | solution.py:11
  372.1 22.1 %all-gather.1 = f32[32,1,1024]{2,1,0:T(1,128)S(1)} all-gather(f32[2,1,1024]{2,1,0:T(1,128)} %slice_add_fusion.5), channel_id=3, replica_groups=mesh['ctx'=16,'dp'=16] {'ctx'}, dimensions={0}, use_global_device_ids=true | all-gather | bytes 139264 | tf_op jit(solution)/shard_map/all_gather | solution.py:11
  395.4 5.3 rev.8
  400.7 8.9 %rev.9 = f32[2,128,1024]{2,1,0:T(8,128)} reverse(f32[2,128,1024]{2,1,0:T(8,128)} %add.436), dimensions={1} | reverse | bytes 2097152 | tf_op jit(solution)/shard_map/rev | solution.py:60
  415.7 4.6 convolution_bitcast_fusion
  420.3 72.4 %reduce-scatter.5.cloned.1.call-done = f32[1024,128]{0,1:T(8,128)} async-done(((f32[1024,2048]{0,1:T(8,128)}), f32[1024,128]{0,1:T(8,128)}) %reduce-scatter.5.cloned.1.call-update) | async-done | bytes 524304 | tf_op jit(solution)/shard_map/reduce_scatter | solution.py:102
  494.8 5.5 fusion.13
  500.3 71.6 %reduce-scatter.7.cloned.1.call-done = f32[64,128]{1,0:T(8,128)} async-done(((f32[1024,128]{1,0:T(8,128)}), f32[64,128]{1,0:T(8,128)}) %reduce-scatter.7.cloned.1.call-update) | async-done | bytes 32784
  (362 shorter events, 250.8 us)
Async XLA Ops:
  7.2 485.6 %reduce-scatter.5.cloned.1.call-start = ((), (), s32[]{:S(2)}) async-start(), calls=%async_computation.2 | async-start | bytes 8912896 | tf_op jit(solution)/shard_map/reduce_scatter | solution.py:102
  81.0 17.9 %copy-start.16 = (f32[2,7,1024]{2,1,0:T(8,128)S(1)}, f32[2,7,1024]{2,1,0:T(8,128)}, u32[]{:S(2)}) copy-start(f32[2,7,1024]{2,1,0:T(8,128)} %slice.573) | copy-start | bytes 172036
  81.1 17.9 %copy-start.17 = (f32[2,7,1024]{2,1,0:T(8,128)S(1)}, f32[2,7,1024]{2,1,0:T(8,128)}, u32[]{:S(2)}) copy-start(f32[2,7,1024]{2,1,0:T(8,128)} %slice.540) | copy-start | bytes 172036
  83.1 9.8 %copy-start.34 = (f32[2,1,1024]{2,1,0:T(1,128)S(1)}, f32[2,1,1024]{2,1,0:T(1,128)}, u32[]{:S(2)}) copy-start(f32[2,1,1024]{2,1,0:T(1,128)} %get-tuple-element.347) | copy-start | bytes 24580
  83.1 9.8 %copy-start.35 = (f32[2,1,1024]{2,1,0:T(1,128)S(1)}, f32[2,1,1024]{2,1,0:T(1,128)}, u32[]{:S(2)}) copy-start(f32[2,1,1024]{2,1,0:T(1,128)} %get-tuple-element.348) | copy-start | bytes 24580
  83.1 9.9 %copy-start.36 = (f32[2,1,1024]{2,1,0:T(1,128)S(1)}, f32[2,1,1024]{2,1,0:T(1,128)}, u32[]{:S(2)}) copy-start(f32[2,1,1024]{2,1,0:T(1,128)} %get-tuple-element.349) | copy-start | bytes 24580
  83.1 9.9 %copy-start.37 = (f32[2,1,1024]{2,1,0:T(1,128)S(1)}, f32[2,1,1024]{2,1,0:T(1,128)}, u32[]{:S(2)}) copy-start(f32[2,1,1024]{2,1,0:T(1,128)} %get-tuple-element.350) | copy-start | bytes 24580
  83.1 9.9 %copy-start.23 = (f32[2,2,1024]{2,1,0:T(2,128)S(1)}, f32[2,2,1024]{2,1,0:T(2,128)}, u32[]{:S(2)}) copy-start(f32[2,2,1024]{2,1,0:T(2,128)} %get-tuple-element.365) | copy-start | bytes 49156
  83.1 10.0 %copy-start.21 = (f32[2,2,1024]{2,1,0:T(2,128)S(1)}, f32[2,2,1024]{2,1,0:T(2,128)}, u32[]{:S(2)}) copy-start(f32[2,2,1024]{2,1,0:T(2,128)} %get-tuple-element.366) | copy-start | bytes 49156
  83.2 10.1 %copy-start.20 = (f32[2,3,1024]{2,1,0:T(4,128)S(1)}, f32[2,3,1024]{2,1,0:T(4,128)}, u32[]{:S(2)}) copy-start(f32[2,3,1024]{2,1,0:T(4,128)} %slice.571) | copy-start | bytes 73732
  126.5 7.6 %copy-start.14 = (f32[2,32,1024]{2,1,0:T(8,128)S(1)}, f32[2,32,1024]{2,1,0:T(8,128)}, u32[]{:S(2)}) copy-start(f32[2,32,1024]{2,1,0:T(8,128)} %add.464) | copy-start | bytes 786436
  129.0 6.7 %copy-start.26 = (f32[2,1,1024]{2,1,0:T(1,128)S(1)}, f32[2,1,1024]{2,1,0:T(1,128)}, u32[]{:S(2)}) copy-start(f32[2,1,1024]{2,1,0:T(1,128)} %slice.656) | copy-start | bytes 24580
  290.2 10.6 %copy-start.38 = (f32[2,1,1024]{2,1,0:T(1,128)S(1)}, f32[2,1,1024]{2,1,0:T(1,128)}, u32[]{:S(2)}) copy-start(f32[2,1,1024]{2,1,0:T(1,128)} %get-tuple-element.339) | copy-start | bytes 24580
  290.2 10.6 %copy-start.39 = (f32[2,1,1024]{2,1,0:T(1,128)S(1)}, f32[2,1,1024]{2,1,0:T(1,128)}, u32[]{:S(2)}) copy-start(f32[2,1,1024]{2,1,0:T(1,128)} %get-tuple-element.340) | copy-start | bytes 24580
  290.2 10.6 %copy-start.40 = (f32[2,1,1024]{2,1,0:T(1,128)S(1)}, f32[2,1,1024]{2,1,0:T(1,128)}, u32[]{:S(2)}) copy-start(f32[2,1,1024]{2,1,0:T(1,128)} %get-tuple-element.341) | copy-start | bytes 24580
  290.2 10.6 %copy-start.41 = (f32[2,1,1024]{2,1,0:T(1,128)S(1)}, f32[2,1,1024]{2,1,0:T(1,128)}, u32[]{:S(2)}) copy-start(f32[2,1,1024]{2,1,0:T(1,128)} %get-tuple-element.342) | copy-start | bytes 24580
  290.2 10.7 %copy-start.24 = (f32[2,2,1024]{2,1,0:T(2,128)S(1)}, f32[2,2,1024]{2,1,0:T(2,128)}, u32[]{:S(2)}) copy-start(f32[2,2,1024]{2,1,0:T(2,128)} %get-tuple-element.370) | copy-start | bytes 49156
  290.2 10.8 %copy-start.22 = (f32[2,2,1024]{2,1,0:T(2,128)S(1)}, f32[2,2,1024]{2,1,0:T(2,128)}, u32[]{:S(2)}) copy-start(f32[2,2,1024]{2,1,0:T(2,128)} %get-tuple-element.369) | copy-start | bytes 49156
  290.2 13.3 %copy-start.18 = (f32[2,7,1024]{2,1,0:T(8,128)S(1)}, f32[2,7,1024]{2,1,0:T(8,128)}, u32[]{:S(2)}) copy-start(f32[2,7,1024]{2,1,0:T(8,128)} %slice.492) | copy-start | bytes 172036
  290.2 13.3 %copy-start.19 = (f32[2,7,1024]{2,1,0:T(8,128)S(1)}, f32[2,7,1024]{2,1,0:T(8,128)}, u32[]{:S(2)}) copy-start(f32[2,7,1024]{2,1,0:T(8,128)} %slice.467) | copy-start | bytes 172036
  308.4 12.4 %copy-start.27 = (f32[2,1,1024]{2,1,0:T(1,128)S(1)}, f32[2,1,1024]{2,1,0:T(1,128)}, u32[]{:S(2)}) copy-start(f32[2,1,1024]{2,1,0:T(1,128)} %slice.584) | copy-start | bytes 24580
  349.1 46.3 %copy-start.7 = (f32[2,128,1024]{2,1,0:T(8,128)S(1)}, f32[2,128,1024]{2,1,0:T(8,128)}, u32[]{:S(2)}) copy-start(f32[2,128,1024]{2,1,0:T(8,128)} %add.429) | copy-start | bytes 3145732
  420.3 74.5 %copy-start.9 = (f32[2,128,1024]{2,1,0:T(8,128)S(1)}, f32[2,128,1024]{2,1,0:T(8,128)}, u32[]{:S(2)}) copy-start(f32[2,128,1024]{2,1,0:T(8,128)} %copy-done.8) | copy-start | bytes 3145732
  420.3 151.7 %reduce-scatter.7.cloned.1.call-start = ((), (), s32[]{:S(2)}) async-start(), calls=%async_computation.3 | async-start | bytes 557056
  (25 other events, 76.6 us)
Sparse Core Ops, SparseCore 0:
  420.4 72.2 reduce-scatter.4
  496.2 75.7 reduce-scatter.6
where the time goes:
time: 588 us; the launch traced here: 580 us
  local copies, waits for them, and re-layouts  220 us (37%)
  waiting for transfers between devices  144 us (24%)
  other arithmetic  96.7 us (16%)
  blocking collectives  90.4 us (15%)
  between operations  15 us (3%)
  matrix products  13.8 us (2%)
    slice x50, local copies, waits for them, and re-layouts, per_device(): lax.associative_scan(combine, (step_decay, step_decay * grad_hidden), axi...  92.1 us
    all_gather x4, blocking collectives, entering(): everything = jax.tree.map(lambda part: lax.all_gather(part, axis), value)  90.4 us
    reduce_scatter x1, waiting for transfers between devices, per_device(): lax.psum_scatter(partial_grad, 'dp', scatter_dimension=1, tiled=True)  72.4 us
    unnamed x3, waiting for transfers between devices  71.6 us
    slice x41, local copies, waits for them, and re-layouts, per_device(): lax.associative_scan(combine, (step_decay, drive_term), axis=1)  60.7 us
    add x22, other arithmetic, combine(): return (earlier[0] * latter[0], latter[0] * earlier[1] + latter[1])  34.7 us
    pad x24, local copies, waits for them, and re-layouts, per_device(): lax.associative_scan(combine, (step_decay, drive_term), axis=1)  31.6 us
    pad x24, local copies, waits for them, and re-layouts, per_device(): lax.associative_scan(combine, (step_decay, step_decay * grad_hidden), axi...  15.3 us
  transfers between devices with their start and end apart: 2, of which 2 were waited for; matrix products, arithmetic and copies ran while one was open for 1% of the time, Pallas kernels for 0%

commit v1 on v0

v1 whole, which is shorter than its diff:
```python
import math

import jax
import jax.numpy as jnp
from jax import lax
from jax.experimental import pallas as pl
from jax.experimental.pallas import tpu as pltpu
from jax.sharding import PartitionSpec as P

GROUPS = 8
LANES = 128
BLOCK = 256
F32 = jnp.float32
BF16 = jnp.bfloat16
ROOT = math.sqrt(2.0 / math.pi)
CUBIC = 0.044715


def dot(a, b, dims=((1,), (0,))):
    return lax.dot_general(a, b, (dims, ((), ())), preferred_element_type=F32)


def order(tokens, steps, transpose=False):
    inner = steps // GROUPS
    rho = lax.broadcasted_iota(jnp.int32, (tokens, tokens), 1 if transpose else 0)
    at = lax.broadcasted_iota(jnp.int32, (tokens, tokens), 0 if transpose else 1)
    place = rho % steps
    source = (rho - place) + (place % GROUPS) * inner + place // GROUPS
    return at == source


def wide(value, width):
    return jnp.concatenate([value] * (width // value.shape[1]), axis=1)


def logistic(value):
    return 0.5 * jnp.tanh(0.5 * value) + 0.5


def gates_kernel(
    starts, x, gin, cot, mask, w_decay, w_input, b_decay, b_input, rate,
    summary, grouped, a_out, c_out, f_out, ru_out, q_out, gh_out, gg_out, xp_out,
    move, move_masked, xb, p1, p2, gins, gos,
):
    tokens, steps = x.shape[0], mask.shape[1]
    rows, inner = tokens // steps, steps // GROUPS
    width = gin.shape[1]
    block = pl.program_id(0)
    base = lax.axis_index("ctx") * steps

    @pl.when(block == 0)
    def _():
        hit = order(tokens, steps)
        masks = mask[...].astype(F32)
        mask_row = jnp.concatenate([masks[r : r + 1] for r in range(rows)], axis=1)
        move[...] = jnp.where(hit, 1.0, 0.0).astype(BF16)
        move_masked[...] = jnp.where(hit, jnp.broadcast_to(mask_row, hit.shape), 0.0).astype(BF16)
        xp_out[...] = dot(move[...], x[...])
        xb[...] = xp_out[...].astype(BF16)

    p1[...] = dot(xb[...], w_decay[...]) + b_decay[...]
    p2[...] = dot(xb[...], w_input[...]) + b_input[...]
    gins[...] = dot(move[...], gin[...])
    gos[...] = dot(move_masked[...], cot[...])
    rate8 = jnp.broadcast_to(8.0 * rate[...], (GROUPS, width))
    spot = lax.broadcasted_iota(jnp.int32, (GROUPS, LANES), 0) * inner + base
    lanes = pl.ds(pl.multiple_of(block * width, width), width)

    def ahead(k, carry):
        new = []
        for r in range(rows):
            h, prod = carry[2 * r], carry[2 * r + 1]
            at = pl.ds(pl.multiple_of(r * steps + k * GROUPS, GROUPS), GROUPS)
            here = spot + k
            reset = here == 0
            for s in range(starts.shape[1]):
                reset = reset | (here == starts[r, s])
            keep = wide(jnp.where(reset, 0.0, 1.0), width)
            gate_decay = logistic(p1[at, :])
            gate_input = logistic(p2[at, :])
            xt = xp_out[at, lanes]
            arg = rate8 * gate_decay
            y = 2.0 * arg
            step = jnp.exp(-arg)
            square = y * (
                1.0 - y * (1 / 2 - y * (1 / 6 - y * (1 / 24 - y * (1 / 120 - y * (1 / 720)))))
            )
            a = keep * step
            c = ((1.0 - keep) + keep * jnp.sqrt(square)) * gate_input
            u = c * xt
            ratio = 0.5 + y * (0.25 + y * (1 / 24 - (y * y) * (1 / 1440)))
            a_out[at, :] = a
            c_out[at, :] = c
            f_out[at, :] = (1.0 - gate_decay) * arg * a
            ru_out[at, :] = a * ratio * u
            q_out[at, :] = u * (1.0 - gate_input)
            new += [a * h + u, a * prod]
            g, go = gins[at, :], gos[at, :]
            gsq = g * g
            th = jnp.tanh(ROOT * g * (1.0 + CUBIC * gsq))
            half = 0.5 * (1.0 + th)
            gh_out[at, :] = go * (g * half)
            gg_out[at, :] = go * (
                half + 0.5 * g * (1.0 - th * th) * (ROOT * (1.0 + (3.0 * CUBIC) * gsq))
            )
        return tuple(new)

    zero = jnp.zeros((GROUPS, width), F32)
    one = jnp.ones((GROUPS, width), F32)
    forward = lax.fori_loop(0, inner, ahead, (zero, one) * rows, unroll=2)

    def back(i, carry):
        k = inner - 1 - i
        new = []
        for r in range(rows):
            at = pl.ds(pl.multiple_of(r * steps + k * GROUPS, GROUPS), GROUPS)
            new.append(a_out[at, :] * (gh_out[at, :] + carry[r]))
        return tuple(new)

    backward = lax.fori_loop(0, inner, back, (zero,) * rows, unroll=4)

    for r in range(rows):
        hs, ps, bs = forward[2 * r], forward[2 * r + 1], backward[r]
        grouped[pl.ds((0 * rows + r) * GROUPS, GROUPS), :] = ps
        grouped[pl.ds((1 * rows + r) * GROUPS, GROUPS), :] = hs
        grouped[pl.ds((2 * rows + r) * GROUPS, GROUPS), :] = bs
        qs = ps
        for d in (1, 2, 4):
            hs = ps * pltpu.roll(hs, d, 0) + hs
            ps = ps * pltpu.roll(ps, d, 0)
            bs = qs * pltpu.roll(bs, GROUPS - d, 0) + bs
            qs = qs * pltpu.roll(qs, GROUPS - d, 0)
        summary[0 * rows + r : 0 * rows + r + 1, :] = ps[GROUPS - 1 :]
        summary[1 * rows + r : 1 * rows + r + 1, :] = hs[GROUPS - 1 :]
        summary[2 * rows + r : 2 * rows + r + 1, :] = bs[:1]


def grads_kernel(
    slabs, grouped, a_in, c_in, f_in, ru_in, q_in, gh_in, gg_in, xp,
    gate_grad, grads, sent, direct,
    prev, ggs, gds, gis,
):
    count = slabs.shape[0]
    rows = slabs.shape[1] // 3
    tokens, width = a_in.shape
    steps = tokens // rows
    inner = steps // GROUPS
    me = lax.axis_index("ctx")
    sub = lax.broadcasted_iota(jnp.int32, (GROUPS, width), 0)

    def spread(i, row):
        return jnp.broadcast_to(slabs[i, row : row + 1, :], (GROUPS, width))

    enter, enter_back = [], []
    for r in range(rows):
        h = jnp.zeros((GROUPS, width), F32)
        for i in range(count - 1):
            h = jnp.where(i < me, spread(i, r) * h + spread(i, rows + r), h)
        b = jnp.zeros((GROUPS, width), F32)
        for i in range(count - 1, 0, -1):
            b = jnp.where(i > me, spread(i, r) * b + spread(i, 2 * rows + r), b)
        ps = grouped[pl.ds((0 * rows + r) * GROUPS, GROUPS), :]
        hs = grouped[pl.ds((1 * rows + r) * GROUPS, GROUPS), :]
        bs = grouped[pl.ds((2 * rows + r) * GROUPS, GROUPS), :]
        hs = jnp.where(sub == 0, ps * h + hs, hs)
        bs = jnp.where(sub == GROUPS - 1, ps * b + bs, bs)
        qs = ps
        for d in (1, 2, 4):
            hs = jnp.where(sub >= d, ps * pltpu.roll(hs, d, 0) + hs, hs)
            ps = jnp.where(sub >= d, ps * pltpu.roll(ps, d, 0), ps)
            bs = jnp.where(sub < GROUPS - d, qs * pltpu.roll(bs, GROUPS - d, 0) + bs, bs)
            qs = jnp.where(sub < GROUPS - d, qs * pltpu.roll(qs, GROUPS - d, 0), qs)
        enter.append(jnp.where(sub == 0, h, pltpu.roll(hs, 1, 0)))
        enter_back.append(jnp.where(sub == GROUPS - 1, b, pltpu.roll(bs, GROUPS - 1, 0)))

    def ahead(k, carry):
        new = []
        for r in range(rows):
            at = pl.ds(pl.multiple_of(r * steps + k * GROUPS, GROUPS), GROUPS)
            prev[at, :] = carry[r]
            h = a_in[at, :] * carry[r] + c_in[at, :] * xp[at, :]
            ggs[at, :] = gg_in[at, :] * h
            new.append(h)
        return tuple(new)

    lax.fori_loop(0, inner, ahead, tuple(enter), unroll=4)

    def back(i, carry):
        k = inner - 1 - i
        new = []
        for r in range(rows):
            at = pl.ds(pl.multiple_of(r * steps + k * GROUPS, GROUPS), GROUPS)
            adjoint = gh_in[at, :] + carry[r]
            new.append(a_in[at, :] * adjoint)
            gds[at, :] = adjoint * f_in[at, :] * (ru_in[at, :] - prev[at, :])
            gis[at, :] = adjoint * q_in[at, :]
            direct[at, :] = adjoint * c_in[at, :]
        return tuple(new)

    lax.fori_loop(0, inner, back, tuple(enter_back), unroll=4)
    unmove = jnp.where(order(tokens, steps, True), 1.0, 0.0).astype(BF16)
    gate_grad[...] = dot(unmove, ggs[...].astype(BF16)).astype(BF16)
    other = lax.axis_index("dp") % 2 == 0
    for half, value in enumerate((gds, gis)):
        grads[half] = value[...].astype(BF16)
        sent[half] = jnp.where(other, value[:, LANES:], value[:, :LANES])


def weights_kernel(x_own, x_other, grads, received, out, held):
    tokens = x_own.shape[0]

    @pl.when(pl.program_id(0) == 0)
    def _():
        core = lax.axis_index("dp") % 2
        parts = grads.shape[2] // (2 * LANES)
        for half in range(2):
            for z in range(parts):
                to = pl.ds((half * parts + z) * LANES, LANES)
                came = pl.ds(z * LANES, LANES)
                own = jnp.where(
                    core == 0,
                    grads[half, :, pl.ds(2 * z * LANES, LANES)].astype(F32),
                    grads[half, :, pl.ds((2 * z + 1) * LANES, LANES)].astype(F32),
                )
                held[pl.ds(0, tokens), to] = own.astype(BF16)
                held[pl.ds(tokens, tokens), to] = received[half, :, came].astype(BF16)

    both = jnp.concatenate([x_own[...].astype(BF16), x_other[...].astype(BF16)], axis=0)
    out[...] = dot(both, held[...], ((0,), (0,)))


def inputs_kernel(steps, grads, direct, weights, out):
    width = grads.shape[2]
    tokens = direct.shape[0]
    total = direct[...]
    for half in range(2):
        total = total + dot(
            grads[half], weights[:, half * width : (half + 1) * width], ((1,), (1,))
        )
    unmove = jnp.where(order(tokens, steps, True), 1.0, 0.0).astype(BF16)
    out[...] = dot(unmove, total.astype(BF16)).astype(BF16)


def sum_kernel(at, parts, out):
    total = parts[0]
    for i in range(1, parts.shape[0]):
        total = total + parts[i]
    out[0] = total


def params(mib):
    return pltpu.CompilerParams(vmem_limit_bytes=mib << 20)


def full(shape):
    return pl.BlockSpec(shape, lambda j: (0,) * len(shape))


def columns(rows, width=BLOCK, first=0):
    return pl.BlockSpec((rows, width), lambda j: (0, j + first))


def shaped(shape, dtype=F32):
    return jax.ShapeDtypeStruct(shape, dtype)


def per_device(
    inputs, gate_in, cotangent, recon_mask, segment_starts, weights, gate_bias, decay_rate
):
    rows, steps, model = inputs.shape
    tokens = rows * steps
    peers, pairs = lax.axis_size("ctx"), lax.axis_size("dp")
    chips = pairs // 2
    blocks = model // BLOCK
    flat = lambda value: value.reshape(tokens, model)
    bias = gate_bias.reshape(1, 2 * model)
    big = shaped((tokens, model))
    tile = columns(tokens)
    outs = pl.pallas_call(
        gates_kernel,
        grid=(blocks,),
        in_specs=[
            pl.BlockSpec(memory_space=pltpu.SMEM),
            full((tokens, model)),
            tile,
            tile,
            full((rows, steps)),
            columns(model),
            columns(model, first=blocks),
            columns(1),
            columns(1, first=blocks),
            columns(1),
        ],
        out_specs=[columns(3 * rows), columns(3 * rows * GROUPS)] + [tile] * 7 + [full((tokens, model))],
        out_shape=[shaped((3 * rows, model)), shaped((3 * rows * GROUPS, model))] + [big] * 8,
        scratch_shapes=[
            pltpu.VMEM((tokens, tokens), BF16),
            pltpu.VMEM((tokens, tokens), BF16),
            pltpu.VMEM((tokens, model), BF16),
        ]
        + [pltpu.VMEM((tokens, BLOCK), F32)] * 4,
        compiler_params=params(32),
        name="gates",
    )(
        segment_starts, flat(inputs), flat(gate_in), flat(cotangent), recon_mask,
        weights, weights, bias, bias, decay_rate.reshape(1, model),
    )
    summary, grouped, *middle, xp = outs
    swap = [(i, i ^ 1) for i in range(pairs)]
    x_other = lax.ppermute(xp, "dp", swap)
    slabs = lax.all_to_all(
        jnp.broadcast_to(summary, (peers,) + summary.shape), "ctx", 0, 0, tiled=True
    )
    pair_tile = pl.BlockSpec((2, tokens, BLOCK), lambda j: (0, 0, j))
    gate_grad, grads, sent, direct = pl.pallas_call(
        grads_kernel,
        grid=(blocks,),
        in_specs=[
            pl.BlockSpec((peers, 3 * rows, BLOCK), lambda j: (0, 0, j)),
            columns(3 * rows * GROUPS),
        ]
        + [tile] * 8,
        out_specs=[
            tile,
            pair_tile,
            pl.BlockSpec((2, tokens, LANES), lambda j: (0, 0, j)),
            tile,
        ],
        out_shape=[
            shaped((tokens, model), BF16),
            shaped((2, tokens, model), BF16),
            shaped((2, tokens, model // 2)),
            big,
        ],
        scratch_shapes=[pltpu.VMEM((tokens, BLOCK), F32)] * 4,
        compiler_params=params(32),
        name="grads",
    )(slabs, grouped, *middle, xp)
    received = lax.ppermute(sent, "dp", swap)
    partial = pl.pallas_call(
        weights_kernel,
        grid=(blocks,),
        in_specs=[tile, tile, full((2, tokens, model)), full((2, tokens, model // 2))],
        out_specs=pl.BlockSpec((BLOCK, model), lambda j: (j, 0)),
        out_shape=shaped((model, model)),
        scratch_shapes=[pltpu.VMEM((2 * tokens, model), BF16)],
        compiler_params=params(24),
        name="weights",
    )(xp, x_other, grads, received)
    part = model // peers
    slices = lax.all_to_all(partial.reshape(peers, part, model), "ctx", 0, 0, tiled=True)
    chip = lax.axis_index("dp") // 2
    by_chip = pl.pallas_call(
        sum_kernel,
        grid_spec=pltpu.PrefetchScalarGridSpec(
            num_scalar_prefetch=1,
            grid=(chips,),
            in_specs=[
                pl.BlockSpec((peers, part, LANES), lambda j, at: (0, 0, lax.rem(j + at[0], chips)))
            ],
            out_specs=pl.BlockSpec((1, part, LANES), lambda j, at: (j, 0, 0)),
        ),
        out_shape=shaped((chips, part, LANES)),
        compiler_params=params(16),
        name="slab_sum",
    )(chip.reshape(1), slices)
    total = by_chip[0]
    for d in range(1, chips):
        hop = [(i, ((i // 2 + d) % chips) * 2 + i % 2) for i in range(pairs)]
        total = total + lax.ppermute(by_chip[d], "dp", hop)
    scale = 1.0 / math.sqrt(rows * pairs * steps * peers)
    input_grad = pl.pallas_call(
        lambda *refs: inputs_kernel(steps, *refs),
        grid=(blocks,),
        in_specs=[
            full((2, tokens, model)),
            tile,
            pl.BlockSpec((BLOCK, 2 * model), lambda j: (j, 0)),
        ],
        out_specs=tile,
        out_shape=shaped((tokens, model), BF16),
        compiler_params=params(24),
        name="inputs",
    )(grads, direct, weights)
    return (
        input_grad.reshape(inputs.shape),
        gate_grad.reshape(inputs.shape),
        total * scale,
    )


def solution(mesh):
    return jax.shard_map(
        per_device,
        mesh=mesh,
        in_specs=(
            P("dp", "ctx", None),
            P("dp", "ctx", None),
            P("dp", "ctx", None),
            P("dp", "ctx"),
            P("dp", None),
            P(),
            P(),
            P(),
        ),
        out_specs=(P("dp", "ctx", None), P("dp", "ctx", None), P("ctx", "dp")),
        check_vma=False,
    )
```

time: 588 us -> 159 us (0.27)
  the two profiles are of different devices: /device:TPU:8 before, /device:TPU:28 now
where the time goes in v1:
time: 159 us; the launch traced here: 158 us
  waiting for transfers between devices  71.9 us (45%)
  starting transfers between devices  34.2 us (22%)
  local copies, waits for them, and re-layouts  26.5 us (17%)
  Pallas kernels  24 us (15%)
    all_to_all x1, waiting for transfers between devices, per_device(): lax.all_to_all(partial.reshape(peers, part, model), 'ctx', 0, 0, tiled=True)  61.7 us
    unnamed x52, local copies, waits for them, and re-layouts  25.7 us
    ppermute x7, starting transfers between devices, per_device(): total = total + lax.ppermute(by_chip[d], 'dp', hop)  18.5 us
    all_to_all x1, starting transfers between devices, per_device(): lax.all_to_all(partial.reshape(peers, part, model), 'ctx', 0, 0, tiled=True)  8.59 us
    pallas_call x1, Pallas kernels, per_device(): pl.pallas_call(gates_kernel, grid=(blocks,), in_specs=[pl.BlockSpec(memor...  7.71 us
    all_to_all x1, waiting for transfers between devices, per_device(): lax.all_to_all(jnp.broadcast_to(summary, (peers,) + summary.shape), 'ctx'...  7.45 us
    all_to_all x1, starting transfers between devices, per_device(): lax.all_to_all(jnp.broadcast_to(summary, (peers,) + summary.shape), 'ctx'...  7.11 us
    pallas_call x1, Pallas kernels, per_device(): pl.pallas_call(sum_kernel, grid_spec=pltpu.PrefetchScalarGridSpec(num_sca...  4.96 us
  transfers between devices with their start and end apart: 11, of which 3 were waited for; matrix products, arithmetic and copies ran while one was open for 0% of the time, Pallas kernels for 5%

profile of v1, /device:TPU:28, one launch (start us, length us, event | category | flops | bytes accessed | tf_op | source)
XLA Modules:
  0.0 158.0 jit_solution(10900516289620989369)
XLA Ops:
  0.6 2.2 %copy-done = bf16[1024,2048]{1,0:T(8,128)(2,1)S(1)} copy-done((bf16[1024,2048]{1,0:T(8,128)(2,1)S(1)}, bf16[1024,2048]{1,0:T(8,128)(2,1)}, u32[]{:S(2)}) %copy-start) | copy-done | bytes 4194328
  8.7 7.7 %gates.1 = (f32[6,1024]{1,0:T(8,128)S(1)}, f32[48,1024]{1,0:T(8,128)S(1)}, f32[256,1024]{1,0:T(8,128)S(1)}, f32[256,1024]{1,0:T(8,128)S(1)}, f32[256,1024]{1,0:T...) custom-call(s32[2,3]{1,0:T(2,128)S(1)} %copy-done.24, ...), custom_call_target="tpu_custom_call" | custom-call | tf_op jit(solution)/shard_map/gates/pallas_call | solution.py:279
  24.3 7.1 %all-to-all-start = ((f32[16,6,1024]{2,1,0:T(8,128)}), f32[16,6,1024]{2,1,0:T(8,128)S(1)}, u32[]{:S(2)}, u32[]{:S(2)}) async-start(f32[16,6,1024]{2,1,0:T(8,128)} %broadcast_in_dim.3), calls=%async_computation | async-start | bytes 1048576 | tf_op jit(solution)/shard_map/all_to_all | solution.py:311
  31.4 7.5 %all-to-all-done.slabs = f32[16,6,1024]{2,1,0:T(8,128)S(1)} async-done(((f32[16,6,1024]{2,1,0:T(8,128)}), f32[16,6,1024]{2,1,0:T(8,128)S(1)}, u32[]{:S(2)}, u32[]{:S(2)}) %all-to-all-start) | async-done | bytes 393248 | tf_op jit(solution)/shard_map/all_to_all | solution.py:311
  38.9 1.2 copy-done.4
  40.1 1.2 copy-done.6
  41.3 1.2 copy-done.8
  42.5 1.2 copy-done.10
  43.8 1.2 copy-done.12
  45.0 1.2 copy-done.14
  46.2 1.2 copy-done.16
  47.4 4.1 %grads.1 = (bf16[256,1024]{1,0:T(8,128)(2,1)}, bf16[2,256,1024]{2,1,0:T(8,128)(2,1)S(1)}, f32[2,256,512]{2,1,0:T(8,128)S(1)}, f32[256,1024]{1,0:T(8,128)S(1)}) custom-call(f32[16,6,1024]{2,1,0:T(8,128)S(1)} %all-to-all-done.slabs, f32[48,1024]{1,0:T(8,128)S(1)} %get-tuple-element.18.grouped, f32[256,1024]{1,0:T(8,128)S(1)} %copy-done.4, ...), custom_call_target="tpu_custom_call" | custom-call | tf_op jit(solution)/shard_map/grads/pallas_call | solution.py:315
  51.5 2.7 %collective-permute-done.1.received = f32[2,256,512]{2,1,0:T(8,128)S(1)} collective-permute-done((f32[2,256,512]{2,1,0:T(8,128)S(1)}, f32[2,256,512]{2,1,0:T(8,128)S(1)}, u32[]{:S(2)}, u32[]{:S(2)}) %collective-permute-start.1) | collective-permute-done | bytes 1048608 | tf_op jit(solution)/shard_map/ppermute | solution.py:339
  54.2 3.7 %weights.1 = f32[1024,1024]{1,0:T(8,128)S(1)} custom-call(f32[256,1024]{1,0:T(8,128)S(1)} %get-tuple-element.26.xp.x_own, f32[256,1024]{1,0:T(8,128)} %collective-permute-done.x_other, bf16[2,256,1024]{2,1,0:T(8,128)(2,1)S(1)} %get-tuple-element.27.refs_0_.grads, f32[2,256,512]{2,1,0:T(8,128)S(1)} %collective-permute-done.1.received), custom_call_target="tpu_custom_call" | custom-call | tf_op jit(solution)/shard_map/weights/pallas_call | solution.py:340
  57.9 2.0 %copy-done.2 = f32[1024,1024]{1,0:T(8,128)} copy-done((f32[1024,1024]{1,0:T(8,128)}, f32[1024,1024]{1,0:T(8,128)S(1)}, u32[]{:S(2)}) %copy-start.2) | copy-done | bytes 4194328
  59.9 8.6 %all-to-all-start.1 = ((f32[16,64,1024]{2,1,0:T(8,128)}), f32[16,64,1024]{2,1,0:T(8,128)}, u32[]{:S(2)}, u32[]{:S(2)}) async-start(f32[16,64,1024]{2,1,0:T(8,128)} %bitcast.41), calls=%async_computation.1 | async-start | bytes 8388608 | tf_op jit(solution)/shard_map/all_to_all | solution.py:351
  68.5 61.7 %all-to-all-done.1.parts = f32[16,64,1024]{2,1,0:T(8,128)} async-done(((f32[16,64,1024]{2,1,0:T(8,128)}), f32[16,64,1024]{2,1,0:T(8,128)}, u32[]{:S(2)}, u32[]{:S(2)}) %all-to-all-start.1) | async-done | bytes 4194336 | tf_op jit(solution)/shard_map/all_to_all | solution.py:351
  130.2 5.0 %slab_sum.1 = f32[8,64,128]{2,1,0:T(8,128)S(1)} custom-call(s32[1]{0:T(128)} %bitcast.7.at, f32[16,64,1024]{2,1,0:T(8,128)} %all-to-all-done.1.parts), custom_call_target="tpu_custom_call" | custom-call | tf_op jit(solution)/shard_map/slab_sum/pallas_call | solution.py:353
  135.2 2.0 %collective-permute-start.2 = (f32[64,128]{1,0:T(8,128)S(1)}, f32[64,128]{1,0:T(8,128)S(1)}, u32[]{:S(2)}, u32[]{:S(2)}) collective-permute-start(f32[64,128]{1,0:T(8,128)S(1)} %get-tuple-element.31), channel_id=1, source_target_pairs={{0,2},{1,3},{2,4},{3,5},{4,6},{5,7},{6,8},{7,9},{8,10},{9,11},{10,... | collective-permute-start | bytes 98312 | tf_op jit(solution)/shard_map/ppermute | solution.py:370
  137.2 3.3 %collective-permute-start.3 = (f32[64,128]{1,0:T(8,128)S(1)}, f32[64,128]{1,0:T(8,128)S(1)}, u32[]{:S(2)}, u32[]{:S(2)}) collective-permute-start(f32[64,128]{1,0:T(8,128)S(1)} %get-tuple-element.37), channel_id=1, source_target_pairs={{0,4},{1,5},{2,6},{3,7},{4,8},{5,9},{6,10},{7,11},{8,12},{9,13},{1... | collective-permute-start | bytes 98312 | tf_op jit(solution)/shard_map/ppermute | solution.py:370
  140.5 4.0 %collective-permute-start.4 = (f32[64,128]{1,0:T(8,128)S(1)}, f32[64,128]{1,0:T(8,128)S(1)}, u32[]{:S(2)}, u32[]{:S(2)}) collective-permute-start(f32[64,128]{1,0:T(8,128)S(1)} %get-tuple-element.36), channel_id=1, source_target_pairs={{0,6},{1,7},{2,8},{3,9},{4,10},{5,11},{6,12},{7,13},{8,14},{9,15},... | collective-permute-start | bytes 98312 | tf_op jit(solution)/shard_map/ppermute | solution.py:370
  145.1 4.9 %collective-permute-start.6 = (f32[64,128]{1,0:T(8,128)S(1)}, f32[64,128]{1,0:T(8,128)S(1)}, u32[]{:S(2)}, u32[]{:S(2)}) collective-permute-start(f32[64,128]{1,0:T(8,128)S(1)} %get-tuple-element.34), channel_id=1, source_target_pairs={{0,10},{1,11},{2,12},{3,13},{4,14},{5,15},{6,0},{7,1},{8,2},{9,3},... | collective-permute-start | bytes 98312 | tf_op jit(solution)/shard_map/ppermute | solution.py:370
  150.0 2.7 %collective-permute-start.7 = (f32[64,128]{1,0:T(8,128)S(1)}, f32[64,128]{1,0:T(8,128)S(1)}, u32[]{:S(2)}, u32[]{:S(2)}) collective-permute-start(f32[64,128]{1,0:T(8,128)S(1)} %get-tuple-element.33), channel_id=1, source_target_pairs={{0,12},{1,13},{2,14},{3,15},{4,0},{5,1},{6,2},{7,3},{8,4},{9,5},{1... | collective-permute-start | bytes 98312 | tf_op jit(solution)/shard_map/ppermute | solution.py:370
  153.7 3.6 %inputs.1 = bf16[256,1024]{1,0:T(8,128)(2,1)} custom-call(bf16[2,256,1024]{2,1,0:T(8,128)(2,1)S(1)} %get-tuple-element.27.refs_0_.grads, f32[256,1024]{1,0:T(8,128)S(1)} %copy-done.18, bf16[1024,2048]{1,0:T(8,128)(2,1)S(1)} %copy-done.1), custom_call_target="tpu_custom_call" | custom-call | tf_op jit(solution)/shard_map/inputs/pallas_call | solution.py:372
  (58 shorter events, 16.0 us)
Async XLA Ops:
  0.6 2.2 %copy-start = (bf16[1024,2048]{1,0:T(8,128)(2,1)S(1)}, bf16[1024,2048]{1,0:T(8,128)(2,1)}, u32[]{:S(2)}) copy-start(bf16[1024,2048]{1,0:T(8,128)(2,1)} %refs_2_.1) | copy-start | bytes 12582916
  22.3 1.1 copy-start.15
  24.3 14.6 %all-to-all-start = ((f32[16,6,1024]{2,1,0:T(8,128)}), f32[16,6,1024]{2,1,0:T(8,128)S(1)}, u32[]{:S(2)}, u32[]{:S(2)}) async-start(f32[16,6,1024]{2,1,0:T(8,128)} %broadcast_in_dim.3), calls=%async_computation | async-start | bytes 1048576 | tf_op jit(solution)/shard_map/all_to_all | solution.py:311
  31.4 20.1 %collective-permute-start = (f32[256,1024]{1,0:T(8,128)S(1)}, f32[256,1024]{1,0:T(8,128)}, u32[]{:S(2)}, u32[]{:S(2)}) collective-permute-start(f32[256,1024]{1,0:T(8,128)S(1)} %get-tuple-element.26.xp.x_own), channel_id=1, source_target_pairs={{0,1},{1,0},{2,3},{3,2},{4,5},{5,4},{6,7},{7,6},{8,9},{9,8},{10,11... | collective-permute-start | bytes 3145736 | tf_op jit(solution)/shard_map/ppermute | solution.py:310
  38.9 1.2 copy-start.4
  40.1 1.2 copy-start.6
  41.3 1.2 copy-start.8
  42.5 1.2 copy-start.10
  43.8 1.2 copy-start.12
  45.0 1.2 copy-start.14
  46.2 1.2 copy-start.16
  51.5 6.3 %copy-start.17 = (f32[256,1024]{1,0:T(8,128)}, f32[256,1024]{1,0:T(8,128)S(1)}, u32[]{:S(2)}) copy-start(f32[256,1024]{1,0:T(8,128)S(1)} %get-tuple-element.28.refs_1_) | copy-start | bytes 3145732
  51.5 2.7 %collective-permute-start.1 = (f32[2,256,512]{2,1,0:T(8,128)S(1)}, f32[2,256,512]{2,1,0:T(8,128)S(1)}, u32[]{:S(2)}, u32[]{:S(2)}) collective-permute-start(f32[2,256,512]{2,1,0:T(8,128)S(1)} %get-tuple-element.30), channel_id=1, source_target_pairs={{0,1},{1,0},{2,3},{3,2},{4,5},{5,4},{6,7},{7,6},{8,9},{9,8},{10,11... | collective-permute-start | bytes 3145736 | tf_op jit(solution)/shard_map/ppermute | solution.py:339
  57.9 2.0 %copy-start.2 = (f32[1024,1024]{1,0:T(8,128)}, f32[1024,1024]{1,0:T(8,128)S(1)}, u32[]{:S(2)}) copy-start(f32[1024,1024]{1,0:T(8,128)S(1)} %weights.1) | copy-start | bytes 12582916
  59.9 93.8 %copy-start.18 = (f32[256,1024]{1,0:T(8,128)S(1)}, f32[256,1024]{1,0:T(8,128)}, u32[]{:S(2)}) copy-start(f32[256,1024]{1,0:T(8,128)} %copy-done.17) | copy-start | bytes 3145732
  59.9 70.3 %all-to-all-start.1 = ((f32[16,64,1024]{2,1,0:T(8,128)}), f32[16,64,1024]{2,1,0:T(8,128)}, u32[]{:S(2)}, u32[]{:S(2)}) async-start(f32[16,64,1024]{2,1,0:T(8,128)} %bitcast.41), calls=%async_computation.1 | async-start | bytes 8388608 | tf_op jit(solution)/shard_map/all_to_all | solution.py:351
  130.2 23.5 %copy-start.1 = (bf16[1024,2048]{1,0:T(8,128)(2,1)S(1)}, bf16[1024,2048]{1,0:T(8,128)(2,1)}, u32[]{:S(2)}) copy-start(bf16[1024,2048]{1,0:T(8,128)(2,1)} %refs_2_.1) | copy-start | bytes 12582916
  135.2 14.8 %collective-permute-start.2 = (f32[64,128]{1,0:T(8,128)S(1)}, f32[64,128]{1,0:T(8,128)S(1)}, u32[]{:S(2)}, u32[]{:S(2)}) collective-permute-start(f32[64,128]{1,0:T(8,128)S(1)} %get-tuple-element.31), channel_id=1, source_target_pairs={{0,2},{1,3},{2,4},{3,5},{4,6},{5,7},{6,8},{7,9},{8,10},{9,11},{10,... | collective-permute-start | bytes 98312 | tf_op jit(solution)/shard_map/ppermute | solution.py:370
  137.2 15.5 %collective-permute-start.3 = (f32[64,128]{1,0:T(8,128)S(1)}, f32[64,128]{1,0:T(8,128)S(1)}, u32[]{:S(2)}, u32[]{:S(2)}) collective-permute-start(f32[64,128]{1,0:T(8,128)S(1)} %get-tuple-element.37), channel_id=1, source_target_pairs={{0,4},{1,5},{2,6},{3,7},{4,8},{5,9},{6,10},{7,11},{8,12},{9,13},{1... | collective-permute-start | bytes 98312 | tf_op jit(solution)/shard_map/ppermute | solution.py:370
  140.5 16.8 %collective-permute-start.4 = (f32[64,128]{1,0:T(8,128)S(1)}, f32[64,128]{1,0:T(8,128)S(1)}, u32[]{:S(2)}, u32[]{:S(2)}) collective-permute-start(f32[64,128]{1,0:T(8,128)S(1)} %get-tuple-element.36), channel_id=1, source_target_pairs={{0,6},{1,7},{2,8},{3,9},{4,10},{5,11},{6,12},{7,13},{8,14},{9,15},... | collective-permute-start | bytes 98312 | tf_op jit(solution)/shard_map/ppermute | solution.py:370
  144.5 12.8 %collective-permute-start.5 = (f32[64,128]{1,0:T(8,128)S(1)}, f32[64,128]{1,0:T(8,128)S(1)}, u32[]{:S(2)}, u32[]{:S(2)}) collective-permute-start(f32[64,128]{1,0:T(8,128)S(1)} %get-tuple-element.35), channel_id=1, source_target_pairs={{0,8},{1,9},{2,10},{3,11},{4,12},{5,13},{6,14},{7,15},{8,0},{9,1},... | collective-permute-start | bytes 98312 | tf_op jit(solution)/shard_map/ppermute | solution.py:370
  145.1 12.2 %collective-permute-start.6 = (f32[64,128]{1,0:T(8,128)S(1)}, f32[64,128]{1,0:T(8,128)S(1)}, u32[]{:S(2)}, u32[]{:S(2)}) collective-permute-start(f32[64,128]{1,0:T(8,128)S(1)} %get-tuple-element.34), channel_id=1, source_target_pairs={{0,10},{1,11},{2,12},{3,13},{4,14},{5,15},{6,0},{7,1},{8,2},{9,3},... | collective-permute-start | bytes 98312 | tf_op jit(solution)/shard_map/ppermute | solution.py:370
  150.0 7.3 %collective-permute-start.7 = (f32[64,128]{1,0:T(8,128)S(1)}, f32[64,128]{1,0:T(8,128)S(1)}, u32[]{:S(2)}, u32[]{:S(2)}) collective-permute-start(f32[64,128]{1,0:T(8,128)S(1)} %get-tuple-element.33), channel_id=1, source_target_pairs={{0,12},{1,13},{2,14},{3,15},{4,0},{5,1},{6,2},{7,3},{8,4},{9,5},{1... | collective-permute-start | bytes 98312 | tf_op jit(solution)/shard_map/ppermute | solution.py:370
  152.7 4.6 %collective-permute-start.8 = (f32[64,128]{1,0:T(8,128)S(1)}, f32[64,128]{1,0:T(8,128)S(1)}, u32[]{:S(2)}, u32[]{:S(2)}) collective-permute-start(f32[64,128]{1,0:T(8,128)S(1)} %get-tuple-element.32), channel_id=1, source_target_pairs={{0,14},{1,15},{2,0},{3,1},{4,2},{5,3},{6,4},{7,5},{8,6},{9,7},{10,... | collective-permute-start | bytes 98312 | tf_op jit(solution)/shard_map/ppermute | solution.py:370
  (13 other events, 11.8 us)

commit v2 on v1

--- a/solution.py
+++ b/solution.py
@@ -14,6 +14,8 @@
 BF16 = jnp.bfloat16
 ROOT = math.sqrt(2.0 / math.pi)
 CUBIC = 0.044715
+SIDE = 4
+PIECES = (8, 10, 6, 12, 4, 14, 0)
 
 
 def dot(a, b, dims=((1,), (0,))):
@@ -130,9 +132,9 @@
             ps = ps * pltpu.roll(ps, d, 0)
             bs = qs * pltpu.roll(bs, GROUPS - d, 0) + bs
             qs = qs * pltpu.roll(qs, GROUPS - d, 0)
-        summary[0 * rows + r : 0 * rows + r + 1, :] = ps[GROUPS - 1 :]
-        summary[1 * rows + r : 1 * rows + r + 1, :] = hs[GROUPS - 1 :]
-        summary[2 * rows + r : 2 * rows + r + 1, :] = bs[:1]
+        for i, value in enumerate((ps[GROUPS - 1 :], hs[GROUPS - 1 :], bs[:1])):
+            at = pl.ds(i * rows + r, 1)
+            summary[:, at, :] = jnp.broadcast_to(value[None], (summary.shape[0], 1, width))
 
 
 def grads_kernel(
@@ -206,27 +208,49 @@
         sent[half] = jnp.where(other, value[:, LANES:], value[:, :LANES])
 
 
-def weights_kernel(x_own, x_other, grads, received, out, held):
-    tokens = x_own.shape[0]
-
-    @pl.when(pl.program_id(0) == 0)
-    def _():
-        core = lax.axis_index("dp") % 2
-        parts = grads.shape[2] // (2 * LANES)
-        for half in range(2):
-            for z in range(parts):
-                to = pl.ds((half * parts + z) * LANES, LANES)
-                came = pl.ds(z * LANES, LANES)
-                own = jnp.where(
-                    core == 0,
-                    grads[half, :, pl.ds(2 * z * LANES, LANES)].astype(F32),
-                    grads[half, :, pl.ds((2 * z + 1) * LANES, LANES)].astype(F32),
-                )
-                held[pl.ds(0, tokens), to] = own.astype(BF16)
-                held[pl.ds(tokens, tokens), to] = received[half, :, came].astype(BF16)
-
-    both = jnp.concatenate([x_own[...].astype(BF16), x_other[...].astype(BF16)], axis=0)
-    out[...] = dot(both, held[...], ((0,), (0,)))
+def turn_kernel(x_own, x_other, out):
+    tokens, model = x_own.shape
+    part = model // (SIDE * SIDE)
+    core = lax.axis_index("dp") % 2
+    my_x, my_y = lax.axis_index("ctx") // SIDE, lax.axis_index("ctx") % SIDE
+    for s, value in enumerate((x_own, x_other)):
+        for bx in range(SIDE):
+            turned = value[:, pl.ds(bx * SIDE * part, SIDE * part)].T.astype(BF16)
+            for by in range(SIDE):
+                dx, dy = (bx - my_x + SIDE) % SIDE, (by - my_y + SIDE) % SIDE
+                place = jnp.where(core == 0, dx * SIDE + dy, dy * SIDE + dx)
+                to = pl.ds(pl.multiple_of(place * part, part), part)
+                out[to, pl.ds(s * tokens, tokens)] = turned[by * part : (by + 1) * part]
+
+
+def weights_kernel(x_turned, grads, received, *rest):
+    *outs, held = rest
+    tokens = grads.shape[1]
+    part = outs[0].shape[1]
+    core = lax.axis_index("dp") % 2
+    parts = grads.shape[2] // (2 * LANES)
+    for half in range(2):
+        for z in range(parts):
+            to = pl.ds((half * parts + z) * LANES, LANES)
+            own = jnp.where(
+                core == 0,
+                grads[half, :, pl.ds(2 * z * LANES, LANES)].astype(F32),
+                grads[half, :, pl.ds((2 * z + 1) * LANES, LANES)].astype(F32),
+            )
+            held[pl.ds(0, tokens), to] = own.astype(BF16)
+            held[pl.ds(tokens, tokens), to] = received[
+                half, :, pl.ds(z * LANES, LANES)
+            ].astype(BF16)
+    for out, start in zip(outs, PIECES):
+        span = out.shape[0] * part
+        value = dot(x_turned[pl.ds(start * part, span), :], held[...])
+        out[...] = value.reshape(out.shape)
+
+
+def fold_kernel(own, low, low_more, high, high_more, *outs):
+    for i, out in enumerate(outs):
+        first, second = (low, low_more) if i < 2 else (high, high_more)
+        out[...] = own[i] + first[i % 2] + second[i % 2]
 
 
 def inputs_kernel(steps, grads, direct, weights, out):
@@ -241,11 +265,16 @@
     out[...] = dot(unmove, total.astype(BF16)).astype(BF16)
 
 
-def sum_kernel(at, parts, out):
-    total = parts[0]
-    for i in range(1, parts.shape[0]):
-        total = total + parts[i]
-    out[0] = total
+def sum_kernel(*refs):
+    parts, outs = refs[:SIDE], refs[SIDE:]
+    chips = len(outs)
+    chip = lax.axis_index("dp") // 2
+    for j, out in enumerate(outs):
+        at = pl.ds(pl.multiple_of(lax.rem(chip + j, chips) * LANES, LANES), LANES)
+        total = parts[0][:, at]
+        for value in parts[1:]:
+            total = total + value[:, at]
+        out[...] = total
 
 
 def params(mib):
@@ -258,6 +287,10 @@
 
 def columns(rows, width=BLOCK, first=0):
     return pl.BlockSpec((rows, width), lambda j: (0, j + first))
+
+
+def far(value):
+    return pltpu.with_memory_space_constraint(value, pltpu.HBM)
 
 
 def shaped(shape, dtype=F32):
@@ -291,26 +324,38 @@
             columns(1, first=blocks),
             columns(1),
         ],
-        out_specs=[columns(3 * rows), columns(3 * rows * GROUPS)] + [tile] * 7 + [full((tokens, model))],
-        out_shape=[shaped((3 * rows, model)), shaped((3 * rows * GROUPS, model))] + [big] * 8,
+        out_specs=[
+            pl.BlockSpec((peers, 3 * rows, BLOCK), lambda j: (0, 0, j)),
+            columns(3 * rows * GROUPS),
+        ]
+        + [tile] * 7
+        + [full((tokens, model))],
+        out_shape=[shaped((peers, 3 * rows, model)), shaped((3 * rows * GROUPS, model))] + [pltpu.HBM((tokens, model), F32)] * 7 + [big],
         scratch_shapes=[
             pltpu.VMEM((tokens, tokens), BF16),
             pltpu.VMEM((tokens, tokens), BF16),
             pltpu.VMEM((tokens, model), BF16),
         ]
         + [pltpu.VMEM((tokens, BLOCK), F32)] * 4,
-        compiler_params=params(32),
+        compiler_params=params(16),
         name="gates",
     )(
-        segment_starts, flat(inputs), flat(gate_in), flat(cotangent), recon_mask,
-        weights, weights, bias, bias, decay_rate.reshape(1, model),
+        segment_starts, far(flat(inputs)), far(flat(gate_in)), far(flat(cotangent)), far(recon_mask),
+        far(weights), far(weights), far(bias), far(bias), far(decay_rate.reshape(1, model)),
     )
     summary, grouped, *middle, xp = outs
+    middle = [far(v) for v in middle]
     swap = [(i, i ^ 1) for i in range(pairs)]
     x_other = lax.ppermute(xp, "dp", swap)
-    slabs = lax.all_to_all(
-        jnp.broadcast_to(summary, (peers,) + summary.shape), "ctx", 0, 0, tiled=True
-    )
+    slabs = lax.all_to_all(summary, "ctx", 0, 0, tiled=True)
+    part = model // peers
+    x_turned = pl.pallas_call(
+        turn_kernel,
+        out_shape=shaped((model, 2 * tokens), BF16),
+        compiler_params=params(8),
+        name="turn",
+    )(xp, x_other)
+    slabs, x_turned = lax.optimization_barrier((slabs, x_turned))
     pair_tile = pl.BlockSpec((2, tokens, BLOCK), lambda j: (0, 0, j))
     gate_grad, grads, sent, direct = pl.pallas_call(
         grads_kernel,
@@ -330,45 +375,36 @@
             shaped((tokens, model), BF16),
             shaped((2, tokens, model), BF16),
             shaped((2, tokens, model // 2)),
-            big,
+            pltpu.HBM((tokens, model), F32),
         ],
         scratch_shapes=[pltpu.VMEM((tokens, BLOCK), F32)] * 4,
-        compiler_params=params(32),
+        compiler_params=params(12),
         name="grads",
     )(slabs, grouped, *middle, xp)
+    direct = far(direct)
     received = lax.ppermute(sent, "dp", swap)
-    partial = pl.pallas_call(
+    piece = shaped((2, part, model))
+    on2, back2, on1, back1, on_last, back_last, stay = pl.pallas_call(
         weights_kernel,
-        grid=(blocks,),
-        in_specs=[tile, tile, full((2, tokens, model)), full((2, tokens, model // 2))],
-        out_specs=pl.BlockSpec((BLOCK, model), lambda j: (j, 0)),
-        out_shape=shaped((model, model)),
+        out_shape=[piece] * 6 + [shaped((SIDE, part, model))],
         scratch_shapes=[pltpu.VMEM((2 * tokens, model), BF16)],
-        compiler_params=params(24),
+        compiler_params=params(16),
         name="weights",
-    )(xp, x_other, grads, received)
-    part = model // peers
-    slices = lax.all_to_all(partial.reshape(peers, part, model), "ctx", 0, 0, tiled=True)
-    chip = lax.axis_index("dp") // 2
-    by_chip = pl.pallas_call(
-        sum_kernel,
-        grid_spec=pltpu.PrefetchScalarGridSpec(
-            num_scalar_prefetch=1,
-            grid=(chips,),
-            in_specs=[
-                pl.BlockSpec((peers, part, LANES), lambda j, at: (0, 0, lax.rem(j + at[0], chips)))
-            ],
-            out_specs=pl.BlockSpec((1, part, LANES), lambda j, at: (j, 0, 0)),
-        ),
-        out_shape=shaped((chips, part, LANES)),
-        compiler_params=params(16),
-        name="slab_sum",
-    )(chip.reshape(1), slices)
-    total = by_chip[0]
-    for d in range(1, chips):
-        hop = [(i, ((i // 2 + d) % chips) * 2 + i % 2) for i in range(pairs)]
-        total = total + lax.ppermute(by_chip[d], "dp", hop)
-    scale = 1.0 / math.sqrt(rows * pairs * steps * peers)
+    )(x_turned, grads, received)
+
+    def move(value, step, first):
+        pairs_of = []
+        for i in range(peers * pairs):
+            x, y, d = i // pairs // SIDE, i // pairs % SIDE, i % pairs
+            if (d % 2 == 0) == first:
+                x = (x + step) % SIDE
+            else:
+                y = (y + step) % SIDE
+            pairs_of.append((i, (x * SIDE + y) * pairs + d))
+        return lax.ppermute(value, ("ctx", "dp"), pairs_of)
+
+    came_on2, came_back2 = move(on2, 1, True), move(back2, -1, True)
+    came_on1, came_back1 = move(on1, 1, True), move(back1, -1, True)
     input_grad = pl.pallas_call(
         lambda *refs: inputs_kernel(steps, *refs),
         grid=(blocks,),
@@ -379,9 +415,34 @@
         ],
         out_specs=tile,
         out_shape=shaped((tokens, model), BF16),
-        compiler_params=params(24),
+        compiler_params=params(12),
+        cost_estimate=pl.CostEstimate(
+            flops=4 * tokens * model * model, bytes_accessed=6 * model * model, transcendentals=0
+        ),
         name="inputs",
-    )(grads, direct, weights)
+    )(grads, direct, far(weights))
+    came_on2, came_back2, input_grad = lax.optimization_barrier((came_on2, came_back2, input_grad))
+    came_on = move(on_last + came_on2, 1, True)
+    came_back = move(back_last + came_back2, -1, True)
+    near = shaped((part, model))
+    quarters = pl.pallas_call(
+        fold_kernel,
+        out_shape=[near] * SIDE,
+        compiler_params=params(8),
+        name="fold",
+    )(stay, came_back1, came_on, came_on1, came_back)
+    others = [move(quarters[d], d, False) for d in (2, 1, 3)]
+    by_chip = pl.pallas_call(
+        sum_kernel,
+        out_shape=[shaped((part, LANES))] * chips,
+        compiler_params=params(4),
+        name="slab_sum",
+    )(quarters[0], *others)
+    total = by_chip[0]
+    for d in range(1, chips):
+        hop = [(i, ((i // 2 + d) % chips) * 2 + i % 2) for i in range(pairs)]
+        total = total + lax.ppermute(by_chip[d], "dp", hop)
+    scale = 1.0 / math.sqrt(rows * pairs * steps * peers)
     return (
         input_grad.reshape(inputs.shape),
         gate_grad.reshape(inputs.shape),

time: 159 us -> 97.8 us (0.62)
  the two profiles are of different devices: /device:TPU:28 before, /device:TPU:8 now
where the time goes in v2:
time: 97.8 us; the launch traced here: 96.9 us
  starting transfers between devices  36.7 us (38%)
  waiting for transfers between devices  32.5 us (33%)
  Pallas kernels  23.3 us (24%)
  local copies, waits for them, and re-layouts  2.96 us (3%)
    ppermute x9, waiting for transfers between devices, move(): return lax.ppermute(value, ('ctx', 'dp'), pairs_of)  18.2 us
    ppermute x7, starting transfers between devices, per_device(): total = total + lax.ppermute(by_chip[d], 'dp', hop)  17.4 us
    ppermute x9, starting transfers between devices, move(): return lax.ppermute(value, ('ctx', 'dp'), pairs_of)  11.7 us
    pallas_call x1, Pallas kernels, per_device(): pl.pallas_call(gates_kernel, grid=(blocks,), in_specs=[pl.BlockSpec(memor...  9.81 us
    all_to_all x1, waiting for transfers between devices, per_device(): slabs = lax.all_to_all(summary, 'ctx', 0, 0, tiled=True)  8.12 us
    all_to_all x1, starting transfers between devices, per_device(): slabs = lax.all_to_all(summary, 'ctx', 0, 0, tiled=True)  7.41 us
    pallas_call x1, Pallas kernels, per_device(): pl.pallas_call(grads_kernel, grid=(blocks,), in_specs=[pl.BlockSpec((peer...  5.84 us
    pallas_call x1, Pallas kernels, per_device(): pl.pallas_call(lambda *refs: inputs_kernel(steps, *refs), grid=(blocks,),...  5.57 us
  transfers between devices with their start and end apart: 19, of which 11 were waited for; matrix products, arithmetic and copies ran while one was open for 0% of the time, Pallas kernels for 6%

profile of v2, /device:TPU:8, one launch (start us, length us, event | category | flops | bytes accessed | tf_op | source)
XLA Modules:
  0.0 96.9 jit_solution(15368478371284513621)
XLA Ops:
  1.3 9.8 %gates.1 = (f32[16,6,1024]{2,1,0:T(8,128)}, f32[48,1024]{1,0:T(8,128)S(1)}, f32[256,1024]{1,0:T(8,128)}, f32[256,1024]{1,0:T(8,128)}, f32[256,1024]{1,0:T(8,128)...) custom-call(s32[2,3]{1,0:T(2,128)S(1)} %copy-done.2, ...), custom_call_target="tpu_custom_call" | custom-call | tf_op jit(solution)/shard_map/gates/pallas_call | solution.py:312
  11.2 7.4 %all-to-all-start = ((f32[16,6,1024]{2,1,0:T(8,128)}), f32[16,6,1024]{2,1,0:T(8,128)S(1)}, u32[]{:S(2)}, u32[]{:S(2)}) async-start(f32[16,6,1024]{2,1,0:T(8,128)} %get-tuple-element.41), calls=%async_computation | async-start | bytes 1048576 | tf_op jit(solution)/shard_map/all_to_all | solution.py:350
  18.7 1.1 %copy-done = f32[256,1024]{1,0:T(8,128)} copy-done((f32[256,1024]{1,0:T(8,128)}, f32[256,1024]{1,0:T(8,128)S(1)}, u32[]{:S(2)}) %copy-start) | copy-done | bytes 1048600
  19.7 1.2 %copy-done.1 = f32[256,1024]{1,0:T(8,128)S(1)} copy-done((f32[256,1024]{1,0:T(8,128)S(1)}, f32[256,1024]{1,0:T(8,128)}, u32[]{:S(2)}) %copy-start.1) | copy-done | bytes 1048600
  21.3 8.1 %all-to-all-done.slabs = f32[16,6,1024]{2,1,0:T(8,128)S(1)} async-done(((f32[16,6,1024]{2,1,0:T(8,128)}), f32[16,6,1024]{2,1,0:T(8,128)S(1)}, u32[]{:S(2)}, u32[]{:S(2)}) %all-to-all-start) | async-done | bytes 393248 | tf_op jit(solution)/shard_map/all_to_all | solution.py:350
  29.4 5.8 %grads.1 = (bf16[256,1024]{1,0:T(8,128)(2,1)}, bf16[2,256,1024]{2,1,0:T(8,128)(2,1)S(1)}, f32[2,256,512]{2,1,0:T(8,128)S(1)}, f32[256,1024]{1,0:T(8,128)}) custom-call(f32[16,6,1024]{2,1,0:T(8,128)S(1)} %all-to-all-done.slabs, f32[48,1024]{1,0:T(8,128)S(1)} %get-tuple-element.45.grouped, f32[256,1024]{1,0:T(8,128)} %get-tuple-element.46.a_in, ...), custom_call_target="tpu_custom_call" | custom-call | tf_op jit(solution)/shard_map/grads/pallas_call | solution.py:360
  35.3 2.7 %collective-permute-done.1.received = f32[2,256,512]{2,1,0:T(8,128)S(1)} collective-permute-done((f32[2,256,512]{2,1,0:T(8,128)S(1)}, f32[2,256,512]{2,1,0:T(8,128)S(1)}, u32[]{:S(2)}, u32[]{:S(2)}) %collective-permute-start.1) | collective-permute-done | bytes 1048608 | tf_op jit(solution)/shard_map/ppermute | solution.py:385
  37.9 1.5 %weights.1 = (f32[2,64,1024]{2,1,0:T(8,128)S(1)}, f32[2,64,1024]{2,1,0:T(8,128)S(1)}, f32[2,64,1024]{2,1,0:T(8,128)S(1)}, f32[2,64,1024]{2,1,0:T(8,128)S(1)}, f3...) custom-call(bf16[1024,512]{1,0:T(8,128)(2,1)S(1)} %turn.1.x_turned, ...), custom_call_target="tpu_custom_call" | custom-call | tf_op jit(solution)/shard_map/weights/pallas_call | solution.py:387
  39.5 3.2 %collective-permute-start.3 = (f32[2,64,1024]{2,1,0:T(8,128)S(1)}, f32[2,64,1024]{2,1,0:T(8,128)S(1)}, u32[]{:S(2)}, u32[]{:S(2)}) collective-permute-start(f32[2,64,1024]{2,1,0:T(8,128)S(1)} %get-tuple-element.56), channel_id=1, source_target_pairs={{0,192},{1,49},{2,194},{3,51},{4,196},{5,53},{6,198},{7,55},{8,200... | collective-permute-start | bytes 1572872 | tf_op jit(solution)/shard_map/ppermute | solution.py:404
  42.7 5.6 %inputs.1 = bf16[256,1024]{1,0:T(8,128)(2,1)} custom-call(bf16[2,256,1024]{2,1,0:T(8,128)(2,1)S(1)} %get-tuple-element.53.grads.refs_0_, f32[256,1024]{1,0:T(8,128)} %get-tuple-element.57.refs_1_, bf16[1024,2048]{1,0:T(8,128)(2,1)} %refs_2_.1), custom_call_target="tpu_custom_call" | custom-call | flops 1073741824 | bytes 6291456 | tf_op jit(solution)/shard_map/inputs/pallas_call | solution.py:408
  48.3 2.0 %collective-permute-start.6 = (f32[2,64,1024]{2,1,0:T(8,128)S(1)}, f32[2,64,1024]{2,1,0:T(8,128)S(1)}, u32[]{:S(2)}, u32[]{:S(2)}) collective-permute-start(f32[2,64,1024]{2,1,0:T(8,128)S(1)} %get-tuple-element.64), channel_id=1, source_target_pairs={{0,64},{1,17},{2,66},{3,19},{4,68},{5,21},{6,70},{7,23},{8,72},{9,... | collective-permute-start | bytes 1572872 | tf_op jit(solution)/shard_map/ppermute | solution.py:404
  50.6 3.3 %collective-permute-start.7 = (f32[2,64,1024]{2,1,0:T(8,128)S(1)}, f32[2,64,1024]{2,1,0:T(8,128)S(1)}, u32[]{:S(2)}, u32[]{:S(2)}) collective-permute-start(f32[2,64,1024]{2,1,0:T(8,128)S(1)} %add.28), channel_id=1, source_target_pairs={{0,192},{1,49},{2,194},{3,51},{4,196},{5,53},{6,198},{7,55},{8,200... | collective-permute-start | bytes 1572872 | tf_op jit(solution)/shard_map/ppermute | solution.py:404
  53.9 3.6 %collective-permute-done.4.low = f32[2,64,1024]{2,1,0:T(8,128)S(1)} collective-permute-done((f32[2,64,1024]{2,1,0:T(8,128)S(1)}, f32[2,64,1024]{2,1,0:T(8,128)S(1)}, u32[]{:S(2)}, u32[]{:S(2)}) %collective-permute-start.4) | collective-permute-done | bytes 524320 | tf_op jit(solution)/shard_map/ppermute | solution.py:404
  57.5 1.2 %collective-permute-done.6.high = f32[2,64,1024]{2,1,0:T(8,128)S(1)} collective-permute-done((f32[2,64,1024]{2,1,0:T(8,128)S(1)}, f32[2,64,1024]{2,1,0:T(8,128)S(1)}, u32[]{:S(2)}, u32[]{:S(2)}) %collective-permute-start.6) | collective-permute-done | bytes 524320 | tf_op jit(solution)/shard_map/ppermute | solution.py:404
  58.7 5.6 %collective-permute-done.5.low_more = f32[2,64,1024]{2,1,0:T(8,128)S(1)} collective-permute-done((f32[2,64,1024]{2,1,0:T(8,128)S(1)}, f32[2,64,1024]{2,1,0:T(8,128)S(1)}, u32[]{:S(2)}, u32[]{:S(2)}) %collective-permute-start.5) | collective-permute-done | bytes 524320 | tf_op jit(solution)/shard_map/ppermute | solution.py:404
  65.4 2.1 %collective-permute-start.9 = (f32[64,1024]{1,0:T(8,128)S(1)}, f32[64,1024]{1,0:T(8,128)S(1)}, u32[]{:S(2)}, u32[]{:S(2)}) collective-permute-start(f32[64,1024]{1,0:T(8,128)S(1)} %get-tuple-element.69), channel_id=1, source_target_pairs={{0,16},{1,65},{2,18},{3,67},{4,20},{5,69},{6,22},{7,71},{8,24},{9,... | collective-permute-start | bytes 786440 | tf_op jit(solution)/shard_map/ppermute | solution.py:404
  67.5 5.1 %collective-permute-done.8.refs_1_ = f32[64,1024]{1,0:T(8,128)S(1)} collective-permute-done((f32[64,1024]{1,0:T(8,128)S(1)}, f32[64,1024]{1,0:T(8,128)S(1)}, u32[]{:S(2)}, u32[]{:S(2)}) %collective-permute-start.8) | collective-permute-done | bytes 262176 | tf_op jit(solution)/shard_map/ppermute | solution.py:404
  72.5 1.8 %collective-permute-done.9.refs_2_ = f32[64,1024]{1,0:T(8,128)S(1)} collective-permute-done((f32[64,1024]{1,0:T(8,128)S(1)}, f32[64,1024]{1,0:T(8,128)S(1)}, u32[]{:S(2)}, u32[]{:S(2)}) %collective-permute-start.9) | collective-permute-done | bytes 262176 | tf_op jit(solution)/shard_map/ppermute | solution.py:404
  75.4 6.1 %collective-permute-start.17 = (f32[64,128]{1,0:T(8,128)S(1)}, f32[64,128]{1,0:T(8,128)S(1)}, u32[]{:S(2)}, u32[]{:S(2)}) collective-permute-start(f32[64,128]{1,0:T(8,128)S(1)} %get-tuple-element.78), channel_id=1, source_target_pairs={{0,14},{1,15},{2,0},{3,1},{4,2},{5,3},{6,4},{7,5},{8,6},{9,7},{10,... | collective-permute-start | bytes 98312 | tf_op jit(solution)/shard_map/ppermute | solution.py:444
  81.5 1.4 %collective-permute-start.16 = (f32[64,128]{1,0:T(8,128)S(1)}, f32[64,128]{1,0:T(8,128)S(1)}, u32[]{:S(2)}, u32[]{:S(2)}) collective-permute-start(f32[64,128]{1,0:T(8,128)S(1)} %get-tuple-element.77), channel_id=1, source_target_pairs={{0,12},{1,13},{2,14},{3,15},{4,0},{5,1},{6,2},{7,3},{8,4},{9,5},{1... | collective-permute-start | bytes 98312 | tf_op jit(solution)/shard_map/ppermute | solution.py:444
  83.4 5.0 %collective-permute-start.14 = (f32[64,128]{1,0:T(8,128)S(1)}, f32[64,128]{1,0:T(8,128)S(1)}, u32[]{:S(2)}, u32[]{:S(2)}) collective-permute-start(f32[64,128]{1,0:T(8,128)S(1)} %get-tuple-element.75), channel_id=1, source_target_pairs={{0,8},{1,9},{2,10},{3,11},{4,12},{5,13},{6,14},{7,15},{8,0},{9,1},... | collective-permute-start | bytes 98312 | tf_op jit(solution)/shard_map/ppermute | solution.py:444
  88.4 2.5 %collective-permute-start.12 = (f32[64,128]{1,0:T(8,128)S(1)}, f32[64,128]{1,0:T(8,128)S(1)}, u32[]{:S(2)}, u32[]{:S(2)}) collective-permute-start(f32[64,128]{1,0:T(8,128)S(1)} %get-tuple-element.73), channel_id=1, source_target_pairs={{0,4},{1,5},{2,6},{3,7},{4,8},{5,9},{6,10},{7,11},{8,12},{9,13},{1... | collective-permute-start | bytes 98312 | tf_op jit(solution)/shard_map/ppermute | solution.py:444
  90.9 1.9 %collective-permute-start.11 = (f32[64,128]{1,0:T(8,128)S(1)}, f32[64,128]{1,0:T(8,128)S(1)}, u32[]{:S(2)}, u32[]{:S(2)}) collective-permute-start(f32[64,128]{1,0:T(8,128)S(1)} %get-tuple-element.72), channel_id=1, source_target_pairs={{0,2},{1,3},{2,4},{3,5},{4,6},{5,7},{6,8},{7,9},{8,10},{9,11},{10,... | collective-permute-start | bytes 98312 | tf_op jit(solution)/shard_map/ppermute | solution.py:444
  92.8 2.5 %collective-permute-done.13 = f32[64,128]{1,0:T(8,128)S(1)} collective-permute-done((f32[64,128]{1,0:T(8,128)S(1)}, f32[64,128]{1,0:T(8,128)S(1)}, u32[]{:S(2)}, u32[]{:S(2)}) %collective-permute-start.13) | collective-permute-done | bytes 32800 | tf_op jit(solution)/shard_map/ppermute | solution.py:444
  (30 shorter events, 5.6 us)
Async XLA Ops:
  0.6 0.7 copy-start.2
  11.1 7.5 %collective-permute-start = (f32[256,1024]{1,0:T(8,128)S(1)}, f32[256,1024]{1,0:T(8,128)S(1)}, u32[]{:S(2)}, u32[]{:S(2)}) collective-permute-start(f32[256,1024]{1,0:T(8,128)S(1)} %get-tuple-element.42.x_own.xp), channel_id=1, source_target_pairs={{0,1},{1,0},{2,3},{3,2},{4,5},{5,4},{6,7},{7,6},{8,9},{9,8},{10,11... | collective-permute-start | bytes 3145736 | tf_op jit(solution)/shard_map/ppermute | solution.py:349
  11.2 18.2 %all-to-all-start = ((f32[16,6,1024]{2,1,0:T(8,128)}), f32[16,6,1024]{2,1,0:T(8,128)S(1)}, u32[]{:S(2)}, u32[]{:S(2)}) async-start(f32[16,6,1024]{2,1,0:T(8,128)} %get-tuple-element.41), calls=%async_computation | async-start | bytes 1048576 | tf_op jit(solution)/shard_map/all_to_all | solution.py:350
  18.6 1.1 %copy-start = (f32[256,1024]{1,0:T(8,128)}, f32[256,1024]{1,0:T(8,128)S(1)}, u32[]{:S(2)}) copy-start(f32[256,1024]{1,0:T(8,128)S(1)} %collective-permute-done.x_other) | copy-start | bytes 3145732
  19.7 1.2 %copy-start.1 = (f32[256,1024]{1,0:T(8,128)S(1)}, f32[256,1024]{1,0:T(8,128)}, u32[]{:S(2)}) copy-start(f32[256,1024]{1,0:T(8,128)} %copy-done) | copy-start | bytes 3145732
  35.3 2.7 %collective-permute-start.1 = (f32[2,256,512]{2,1,0:T(8,128)S(1)}, f32[2,256,512]{2,1,0:T(8,128)S(1)}, u32[]{:S(2)}, u32[]{:S(2)}) collective-permute-start(f32[2,256,512]{2,1,0:T(8,128)S(1)} %get-tuple-element.54), channel_id=1, source_target_pairs={{0,1},{1,0},{2,3},{3,2},{4,5},{5,4},{6,7},{7,6},{8,9},{9,8},{10,11... | collective-permute-start | bytes 3145736 | tf_op jit(solution)/shard_map/ppermute | solution.py:385
  39.4 10.9 %collective-permute-start.2 = (f32[2,64,1024]{2,1,0:T(8,128)S(1)}, f32[2,64,1024]{2,1,0:T(8,128)S(1)}, u32[]{:S(2)}, u32[]{:S(2)}) collective-permute-start(f32[2,64,1024]{2,1,0:T(8,128)S(1)} %get-tuple-element.55), channel_id=1, source_target_pairs={{0,64},{1,17},{2,66},{3,19},{4,68},{5,21},{6,70},{7,23},{8,72},{9,... | collective-permute-start | bytes 1572872 | tf_op jit(solution)/shard_map/ppermute | solution.py:404
  39.5 10.8 %collective-permute-start.3 = (f32[2,64,1024]{2,1,0:T(8,128)S(1)}, f32[2,64,1024]{2,1,0:T(8,128)S(1)}, u32[]{:S(2)}, u32[]{:S(2)}) collective-permute-start(f32[2,64,1024]{2,1,0:T(8,128)S(1)} %get-tuple-element.56), channel_id=1, source_target_pairs={{0,192},{1,49},{2,194},{3,51},{4,196},{5,53},{6,198},{7,55},{8,200... | collective-permute-start | bytes 1572872 | tf_op jit(solution)/shard_map/ppermute | solution.py:404
  48.3 9.2 %collective-permute-start.4 = (f32[2,64,1024]{2,1,0:T(8,128)S(1)}, f32[2,64,1024]{2,1,0:T(8,128)S(1)}, u32[]{:S(2)}, u32[]{:S(2)}) collective-permute-start(f32[2,64,1024]{2,1,0:T(8,128)S(1)} %get-tuple-element.61), channel_id=1, source_target_pairs={{0,192},{1,49},{2,194},{3,51},{4,196},{5,53},{6,198},{7,55},{8,200... | collective-permute-start | bytes 1572872 | tf_op jit(solution)/shard_map/ppermute | solution.py:404
  48.3 10.4 %collective-permute-start.6 = (f32[2,64,1024]{2,1,0:T(8,128)S(1)}, f32[2,64,1024]{2,1,0:T(8,128)S(1)}, u32[]{:S(2)}, u32[]{:S(2)}) collective-permute-start(f32[2,64,1024]{2,1,0:T(8,128)S(1)} %get-tuple-element.64), channel_id=1, source_target_pairs={{0,64},{1,17},{2,66},{3,19},{4,68},{5,21},{6,70},{7,23},{8,72},{9,... | collective-permute-start | bytes 1572872 | tf_op jit(solution)/shard_map/ppermute | solution.py:404
  50.4 13.9 %collective-permute-start.5 = (f32[2,64,1024]{2,1,0:T(8,128)S(1)}, f32[2,64,1024]{2,1,0:T(8,128)S(1)}, u32[]{:S(2)}, u32[]{:S(2)}) collective-permute-start(f32[2,64,1024]{2,1,0:T(8,128)S(1)} %add.27), channel_id=1, source_target_pairs={{0,64},{1,17},{2,66},{3,19},{4,68},{5,21},{6,70},{7,23},{8,72},{9,... | collective-permute-start | bytes 1572872 | tf_op jit(solution)/shard_map/ppermute | solution.py:404
  50.6 13.7 %collective-permute-start.7 = (f32[2,64,1024]{2,1,0:T(8,128)S(1)}, f32[2,64,1024]{2,1,0:T(8,128)S(1)}, u32[]{:S(2)}, u32[]{:S(2)}) collective-permute-start(f32[2,64,1024]{2,1,0:T(8,128)S(1)} %add.28), channel_id=1, source_target_pairs={{0,192},{1,49},{2,194},{3,51},{4,196},{5,53},{6,198},{7,55},{8,200... | collective-permute-start | bytes 1572872 | tf_op jit(solution)/shard_map/ppermute | solution.py:404
  64.4 8.1 %collective-permute-start.8 = (f32[64,1024]{1,0:T(8,128)S(1)}, f32[64,1024]{1,0:T(8,128)S(1)}, u32[]{:S(2)}, u32[]{:S(2)}) collective-permute-start(f32[64,1024]{1,0:T(8,128)S(1)} %get-tuple-element.68), channel_id=1, source_target_pairs={{0,32},{1,129},{2,34},{3,131},{4,36},{5,133},{6,38},{7,135},{8,40}... | collective-permute-start | bytes 786440 | tf_op jit(solution)/shard_map/ppermute | solution.py:404
  65.4 8.9 %collective-permute-start.9 = (f32[64,1024]{1,0:T(8,128)S(1)}, f32[64,1024]{1,0:T(8,128)S(1)}, u32[]{:S(2)}, u32[]{:S(2)}) collective-permute-start(f32[64,1024]{1,0:T(8,128)S(1)} %get-tuple-element.69), channel_id=1, source_target_pairs={{0,16},{1,65},{2,18},{3,67},{4,20},{5,69},{6,22},{7,71},{8,24},{9,... | collective-permute-start | bytes 786440 | tf_op jit(solution)/shard_map/ppermute | solution.py:404
  67.5 7.8 %collective-permute-start.10 = (f32[64,1024]{1,0:T(8,128)S(1)}, f32[64,1024]{1,0:T(8,128)S(1)}, u32[]{:S(2)}, u32[]{:S(2)}) collective-permute-start(f32[64,1024]{1,0:T(8,128)S(1)} %get-tuple-element.70), channel_id=1, source_target_pairs={{0,48},{1,193},{2,50},{3,195},{4,52},{5,197},{6,54},{7,199},{8,56}... | collective-permute-start | bytes 786440 | tf_op jit(solution)/shard_map/ppermute | solution.py:404
  75.4 13.1 %collective-permute-start.17 = (f32[64,128]{1,0:T(8,128)S(1)}, f32[64,128]{1,0:T(8,128)S(1)}, u32[]{:S(2)}, u32[]{:S(2)}) collective-permute-start(f32[64,128]{1,0:T(8,128)S(1)} %get-tuple-element.78), channel_id=1, source_target_pairs={{0,14},{1,15},{2,0},{3,1},{4,2},{5,3},{6,4},{7,5},{8,6},{9,7},{10,... | collective-permute-start | bytes 98312 | tf_op jit(solution)/shard_map/ppermute | solution.py:444
  81.5 9.4 %collective-permute-start.16 = (f32[64,128]{1,0:T(8,128)S(1)}, f32[64,128]{1,0:T(8,128)S(1)}, u32[]{:S(2)}, u32[]{:S(2)}) collective-permute-start(f32[64,128]{1,0:T(8,128)S(1)} %get-tuple-element.77), channel_id=1, source_target_pairs={{0,12},{1,13},{2,14},{3,15},{4,0},{5,1},{6,2},{7,3},{8,4},{9,5},{1... | collective-permute-start | bytes 98312 | tf_op jit(solution)/shard_map/ppermute | solution.py:444
  82.9 9.9 %collective-permute-start.15 = (f32[64,128]{1,0:T(8,128)S(1)}, f32[64,128]{1,0:T(8,128)S(1)}, u32[]{:S(2)}, u32[]{:S(2)}) collective-permute-start(f32[64,128]{1,0:T(8,128)S(1)} %get-tuple-element.76), channel_id=1, source_target_pairs={{0,10},{1,11},{2,12},{3,13},{4,14},{5,15},{6,0},{7,1},{8,2},{9,3},... | collective-permute-start | bytes 98312 | tf_op jit(solution)/shard_map/ppermute | solution.py:444
  83.4 9.4 %collective-permute-start.14 = (f32[64,128]{1,0:T(8,128)S(1)}, f32[64,128]{1,0:T(8,128)S(1)}, u32[]{:S(2)}, u32[]{:S(2)}) collective-permute-start(f32[64,128]{1,0:T(8,128)S(1)} %get-tuple-element.75), channel_id=1, source_target_pairs={{0,8},{1,9},{2,10},{3,11},{4,12},{5,13},{6,14},{7,15},{8,0},{9,1},... | collective-permute-start | bytes 98312 | tf_op jit(solution)/shard_map/ppermute | solution.py:444
  88.4 6.9 %collective-permute-start.13 = (f32[64,128]{1,0:T(8,128)S(1)}, f32[64,128]{1,0:T(8,128)S(1)}, u32[]{:S(2)}, u32[]{:S(2)}) collective-permute-start(f32[64,128]{1,0:T(8,128)S(1)} %get-tuple-element.74), channel_id=1, source_target_pairs={{0,6},{1,7},{2,8},{3,9},{4,10},{5,11},{6,12},{7,13},{8,14},{9,15},... | collective-permute-start | bytes 98312 | tf_op jit(solution)/shard_map/ppermute | solution.py:444
  88.4 7.7 %collective-permute-start.12 = (f32[64,128]{1,0:T(8,128)S(1)}, f32[64,128]{1,0:T(8,128)S(1)}, u32[]{:S(2)}, u32[]{:S(2)}) collective-permute-start(f32[64,128]{1,0:T(8,128)S(1)} %get-tuple-element.73), channel_id=1, source_target_pairs={{0,4},{1,5},{2,6},{3,7},{4,8},{5,9},{6,10},{7,11},{8,12},{9,13},{1... | collective-permute-start | bytes 98312 | tf_op jit(solution)/shard_map/ppermute | solution.py:444
  90.9 5.4 %collective-permute-start.11 = (f32[64,128]{1,0:T(8,128)S(1)}, f32[64,128]{1,0:T(8,128)S(1)}, u32[]{:S(2)}, u32[]{:S(2)}) collective-permute-start(f32[64,128]{1,0:T(8,128)S(1)} %get-tuple-element.72), channel_id=1, source_target_pairs={{0,2},{1,3},{2,4},{3,5},{4,6},{5,7},{6,8},{7,9},{8,10},{9,11},{10,... | collective-permute-start | bytes 98312 | tf_op jit(solution)/shard_map/ppermute | solution.py:444

commit v3 on v2

v3 whole, which is shorter than its diff:
```python
import math

import jax
import jax.numpy as jnp
from jax import lax
from jax.experimental import pallas as pl
from jax.experimental.pallas import tpu as pltpu
from jax.sharding import PartitionSpec as P

GROUPS = 8
LANES = 128
BLOCK = 256
F32 = jnp.float32
BF16 = jnp.bfloat16
ROOT = math.sqrt(2.0 / math.pi)
CUBIC = 0.044715
SIDE = 4
UNROLL = (16, 16, 16, 16)
PARAMS = (28, 28)
PIECES = (8, 10, 6, 12, 4, 14, 0)


def dot(a, b, dims=((1,), (0,))):
    return lax.dot_general(a, b, (dims, ((), ())), preferred_element_type=F32)


def order(tokens, steps, transpose=False):
    inner = steps // GROUPS
    rho = lax.broadcasted_iota(jnp.int32, (tokens, tokens), 1 if transpose else 0)
    at = lax.broadcasted_iota(jnp.int32, (tokens, tokens), 0 if transpose else 1)
    place = rho % steps
    source = (rho - place) + (place % GROUPS) * inner + place // GROUPS
    return at == source


def wide(value, width):
    return jnp.concatenate([value] * (width // value.shape[1]), axis=1)


def logistic(value):
    return 0.5 * jnp.tanh(0.5 * value) + 0.5


def gates_kernel(
    starts, x, gin, cot, mask, w_decay, w_input, bias, rate,
    summary, grouped, middle, xp_out,
    move, move_masked, xb, p1, p2, gins, gos,
):
    tokens, steps = x.shape[0], mask.shape[1]
    rows, inner = tokens // steps, steps // GROUPS
    width = gin.shape[1]
    block = pl.program_id(0)
    me = lax.axis_index("ctx")
    base = me * steps
    lanes = pl.ds(pl.multiple_of(block * width, width), width)
    lanes_input = pl.ds(pl.multiple_of(x.shape[1] + block * width, width), width)

    @pl.when(block == 0)
    def _():
        hit = order(tokens, steps)
        masks = mask[...].astype(F32)
        mask_row = jnp.concatenate([masks[r : r + 1] for r in range(rows)], axis=1)
        move[...] = jnp.where(hit, 1.0, 0.0).astype(BF16)
        move_masked[...] = jnp.where(hit, jnp.broadcast_to(mask_row, hit.shape), 0.0).astype(BF16)
        xp_out[...] = dot(move[...], x[...])
        xb[...] = xp_out[...].astype(BF16)

    p1[...] = dot(xb[...], w_decay[...]) + bias[:, lanes]
    p2[...] = dot(xb[...], w_input[...]) + bias[:, lanes_input]
    gins[...] = dot(move[...], gin[...])
    gos[...] = dot(move_masked[...], cot[...])
    rate8 = jnp.broadcast_to(8.0 * rate[:, lanes], (GROUPS, width))
    spot = lax.broadcasted_iota(jnp.int32, (GROUPS, LANES), 0) * inner + base
    spots = [
        [jnp.broadcast_to(starts[r : r + 1, s : s + 1], spot.shape) for s in range(starts.shape[1])]
        for r in range(rows)
    ]

    def ahead(k, carry):
        new = []
        for r in range(rows):
            h, prod = carry[2 * r], carry[2 * r + 1]
            at = pl.ds(pl.multiple_of(r * steps + k * GROUPS, GROUPS), GROUPS)
            here = spot + k
            reset = here == 0
            for s in range(starts.shape[1]):
                reset = reset | (here == spots[r][s])
            keep = wide(jnp.where(reset, 0.0, 1.0), width)
            gate_decay = logistic(p1[at, :])
            gate_input = logistic(p2[at, :])
            xt = xp_out[at, lanes]
            arg = rate8 * gate_decay
            y = 2.0 * arg
            step = jnp.exp(-arg)
            square = y * (
                1.0 - y * (1 / 2 - y * (1 / 6 - y * (1 / 24 - y * (1 / 120 - y * (1 / 720)))))
            )
            a = keep * step
            c = ((1.0 - keep) + keep * jnp.sqrt(square)) * gate_input
            u = c * xt
            ratio = 0.5 + y * (0.25 + y * (1 / 24 - (y * y) * (1 / 1440)))
            middle[0, at, lanes] = a
            middle[1, at, lanes] = c
            middle[2, at, lanes] = (1.0 - gate_decay) * arg * a
            middle[3, at, lanes] = a * ratio * u
            middle[4, at, lanes] = u * (1.0 - gate_input)
            new += [a * h + u, a * prod]
            g, go = gins[at, :], gos[at, :]
            gsq = g * g
            th = jnp.tanh(ROOT * g * (1.0 + CUBIC * gsq))
            half = 0.5 * (1.0 + th)
            middle[5, at, lanes] = go * (g * half)
            middle[6, at, lanes] = go * (
                half + 0.5 * g * (1.0 - th * th) * (ROOT * (1.0 + (3.0 * CUBIC) * gsq))
            )
        return tuple(new)

    zero = jnp.zeros((GROUPS, width), F32)
    one = jnp.ones((GROUPS, width), F32)
    forward = lax.fori_loop(0, inner, ahead, (zero, one) * rows, unroll=UNROLL[0])

    def back(i, carry):
        k = inner - 1 - i
        new = []
        for r in range(rows):
            at = pl.ds(pl.multiple_of(r * steps + k * GROUPS, GROUPS), GROUPS)
            new.append(middle[0, at, lanes] * (middle[5, at, lanes] + carry[r]))
        return tuple(new)

    backward = lax.fori_loop(0, inner, back, (zero,) * rows, unroll=UNROLL[1])

    for r in range(rows):
        hs, ps, bs = forward[2 * r], forward[2 * r + 1], backward[r]
        grouped[pl.ds((0 * rows + r) * GROUPS, GROUPS), lanes] = ps
        grouped[pl.ds((1 * rows + r) * GROUPS, GROUPS), lanes] = hs
        grouped[pl.ds((2 * rows + r) * GROUPS, GROUPS), lanes] = bs
        qs = ps
        for d in (1, 2, 4):
            hs = ps * pltpu.roll(hs, d, 0) + hs
            ps = ps * pltpu.roll(ps, d, 0)
            bs = qs * pltpu.roll(bs, GROUPS - d, 0) + bs
            qs = qs * pltpu.roll(qs, GROUPS - d, 0)
        for i in range(summary.shape[0]):
            summary[i, r : r + 1, :] = ps[GROUPS - 1 :]
            summary[i, rows + r : rows + r + 1, :] = jnp.where(me < i, hs[GROUPS - 1 :], bs[:1])


def grads_kernel(
    slabs, grouped, middle, xp,
    gate_grad, grads, sent, direct,
    prev, ggs, gds, gis,
):
    count = slabs.shape[0]
    rows = slabs.shape[1] // 2
    tokens, width = gate_grad.shape
    lanes = pl.ds(pl.multiple_of(pl.program_id(0) * width, width), width)
    to_send = pl.ds(pl.multiple_of(pl.program_id(0) * LANES, LANES), LANES)
    steps = tokens // rows
    inner = steps // GROUPS
    me = lax.axis_index("ctx")
    sub = lax.broadcasted_iota(jnp.int32, (GROUPS, width), 0)

    def spread(i, row):
        return jnp.broadcast_to(slabs[i, row : row + 1, lanes], (GROUPS, width))

    enter, enter_back = [], []
    for r in range(rows):
        h = jnp.zeros((GROUPS, width), F32)
        for i in range(count - 1):
            h = jnp.where(i < me, spread(i, r) * h + spread(i, rows + r), h)
        b = jnp.zeros((GROUPS, width), F32)
        for i in range(count - 1, 0, -1):
            b = jnp.where(i > me, spread(i, r) * b + spread(i, rows + r), b)
        ps = grouped[pl.ds((0 * rows + r) * GROUPS, GROUPS), lanes]
        hs = grouped[pl.ds((1 * rows + r) * GROUPS, GROUPS), lanes]
        bs = grouped[pl.ds((2 * rows + r) * GROUPS, GROUPS), lanes]
        hs = jnp.where(sub == 0, ps * h + hs, hs)
        bs = jnp.where(sub == GROUPS - 1, ps * b + bs, bs)
        qs = ps
        for d in (1, 2, 4):
            hs = jnp.where(sub >= d, ps * pltpu.roll(hs, d, 0) + hs, hs)
            ps = jnp.where(sub >= d, ps * pltpu.roll(ps, d, 0), ps)
            bs = jnp.where(sub < GROUPS - d, qs * pltpu.roll(bs, GROUPS - d, 0) + bs, bs)
            qs = jnp.where(sub < GROUPS - d, qs * pltpu.roll(qs, GROUPS - d, 0), qs)
        enter.append(jnp.where(sub == 0, h, pltpu.roll(hs, 1, 0)))
        enter_back.append(jnp.where(sub == GROUPS - 1, b, pltpu.roll(bs, GROUPS - 1, 0)))

    def ahead(k, carry):
        new = []
        for r in range(rows):
            at = pl.ds(pl.multiple_of(r * steps + k * GROUPS, GROUPS), GROUPS)
            prev[at, :] = carry[r]
            h = middle[0, at, lanes] * carry[r] + middle[1, at, lanes] * xp[at, lanes]
            ggs[at, :] = middle[6, at, lanes] * h
            new.append(h)
        return tuple(new)

    lax.fori_loop(0, inner, ahead, tuple(enter), unroll=UNROLL[2])

    def back(i, carry):
        k = inner - 1 - i
        new = []
        for r in range(rows):
            at = pl.ds(pl.multiple_of(r * steps + k * GROUPS, GROUPS), GROUPS)
            adjoint = middle[5, at, lanes] + carry[r]
            new.append(middle[0, at, lanes] * adjoint)
            gds[at, :] = adjoint * middle[2, at, lanes] * (middle[3, at, lanes] - prev[at, :])
            gis[at, :] = adjoint * middle[4, at, lanes]
            direct[at, lanes] = adjoint * middle[1, at, lanes]
        return tuple(new)

    lax.fori_loop(0, inner, back, tuple(enter_back), unroll=UNROLL[3])
    unmove = jnp.where(order(tokens, steps, True), 1.0, 0.0).astype(BF16)
    gate_grad[...] = dot(unmove, ggs[...].astype(BF16)).astype(BF16)
    other = lax.axis_index("dp") % 2 == 0
    for half, value in enumerate((gds, gis)):
        grads[half, :, lanes] = value[...].astype(BF16)
        sent[half, :, to_send] = jnp.where(other, value[:, LANES:], value[:, :LANES])


def turn_kernel(steps, x_own, x_other, out):
    tokens, model = x_own.shape
    part = model // (SIDE * SIDE)
    core = lax.axis_index("dp") % 2
    my_x, my_y = lax.axis_index("ctx") // SIDE, lax.axis_index("ctx") % SIDE
    place = jnp.where(order(tokens, steps), 1.0, 0.0).astype(BF16)
    for s, value in enumerate((x_own, x_other)):
        for bx in range(SIDE):
            turned = value[:, pl.ds(bx * SIDE * part, SIDE * part)]
            if s == 1:
                turned = dot(place, turned.astype(BF16))
            turned = turned.T.astype(BF16)
            for by in range(SIDE):
                dx, dy = (bx - my_x + SIDE) % SIDE, (by - my_y + SIDE) % SIDE
                block = jnp.where(core == 0, dx * SIDE + dy, dy * SIDE + dx)
                to = pl.ds(pl.multiple_of(block * part, part), part)
                out[to, pl.ds(s * tokens, tokens)] = turned[by * part : (by + 1) * part]


def pieces(x_turned, held, outs, starts):
    part = outs[0].shape[1]
    for out, start in zip(outs, starts):
        value = dot(x_turned[pl.ds(start * part, out.shape[0] * part), :], held[...])
        out[...] = value.reshape(out.shape)


def first_weights_kernel(x_turned, grads, received, held, *outs):
    tokens = grads.shape[1]
    core = lax.axis_index("dp") % 2
    parts = grads.shape[2] // (2 * LANES)
    for half in range(2):
        for z in range(parts):
            to = pl.ds((half * parts + z) * LANES, LANES)
            own = jnp.where(
                core == 0,
                grads[half, :, pl.ds(2 * z * LANES, LANES)].astype(F32),
                grads[half, :, pl.ds((2 * z + 1) * LANES, LANES)].astype(F32),
            )
            held[pl.ds(0, tokens), to] = own.astype(BF16)
            held[pl.ds(tokens, tokens), to] = received[
                half, :, pl.ds(z * LANES, LANES)
            ].astype(BF16)
    pieces(x_turned, held, outs, PIECES[:2])


def more_weights_kernel(x_turned, held, *outs):
    pieces(x_turned, held, outs, PIECES[2:])


def fold_kernel(own, low, low_more, high, high_more, *outs):
    for i, out in enumerate(outs):
        first, second = (low, low_more) if i < 2 else (high, high_more)
        out[...] = own[i] + first[i % 2] + second[i % 2]


def inputs_kernel(steps, grads, direct, weights, out):
    width = grads.shape[2]
    tokens = direct.shape[0]
    total = direct[...]
    for half in range(2):
        total = total + dot(
            grads[half], weights[:, half * width : (half + 1) * width], ((1,), (1,))
        )
    unmove = jnp.where(order(tokens, steps, True), 1.0, 0.0).astype(BF16)
    out[...] = dot(unmove, total.astype(BF16)).astype(BF16)


def sum_kernel(scale, *refs):
    *parts, out = refs
    for z in range(out.shape[0]):
        at = pl.ds(z * LANES, LANES)
        total = parts[0][:, at]
        for value in parts[1:]:
            total = total + value[:, at]
        out[z] = total * scale


def params(mib):
    return pltpu.CompilerParams(vmem_limit_bytes=mib << 20)


def full(shape):
    return pl.BlockSpec(shape, lambda j: (0,) * len(shape))


def columns(rows, width=BLOCK, first=0):
    return pl.BlockSpec((rows, width), lambda j: (0, j + first))


def far(value):
    return pltpu.with_memory_space_constraint(value, pltpu.HBM)


def shaped(shape, dtype=F32):
    return jax.ShapeDtypeStruct(shape, dtype)


def gates(
    inputs, gate_in, cotangent, recon_mask, segment_starts, weights, gate_bias, decay_rate, peers
):
    rows, steps, model = inputs.shape
    tokens = rows * steps
    blocks = model // BLOCK
    flat = lambda value: value.reshape(tokens, model)
    bias = gate_bias.reshape(1, 2 * model)
    tile = columns(tokens)
    near = pl.BlockSpec(memory_space=pltpu.VMEM)
    return pl.pallas_call(
        gates_kernel,
        grid=(blocks,),
        in_specs=[
            full(segment_starts.shape),
            full((tokens, model)),
            tile,
            tile,
            full((rows, steps)),
            columns(model),
            columns(model, first=blocks),
            full((1, 2 * model)),
            full((1, model)),
        ],
        out_specs=[pl.BlockSpec((peers, 2 * rows, BLOCK), lambda j: (0, 0, j)), near, near, near],
        out_shape=[
            shaped((peers, 2 * rows, model)),
            pltpu.VMEM((3 * rows * GROUPS, model), F32),
            pltpu.VMEM((7, tokens, model), F32),
            pltpu.VMEM((tokens, model), F32),
        ],
        scratch_shapes=[
            pltpu.VMEM((tokens, tokens), BF16),
            pltpu.VMEM((tokens, tokens), BF16),
            pltpu.VMEM((tokens, model), BF16),
        ]
        + [pltpu.VMEM((tokens, BLOCK), F32)] * 4,
        compiler_params=params(PARAMS[0]),
        name="gates",
    )(
        far(segment_starts), far(flat(inputs)), far(flat(gate_in)), far(flat(cotangent)), far(recon_mask),
        far(weights), far(weights), far(bias), far(decay_rate.reshape(1, model)),
    )


def gradients(slabs, grouped, middle, xp):
    tokens, model = xp.shape
    near = pl.BlockSpec(memory_space=pltpu.VMEM)
    return pl.pallas_call(
        grads_kernel,
        grid=(model // BLOCK,),
        in_specs=[near] * 4,
        out_specs=[columns(tokens), near, near, near],
        out_shape=[
            shaped((tokens, model), BF16),
            pltpu.VMEM((2, tokens, model), BF16),
            pltpu.VMEM((2, tokens, model // 2), F32),
            pltpu.VMEM((tokens, model), F32),
        ],
        scratch_shapes=[pltpu.VMEM((tokens, BLOCK), F32)] * 4,
        compiler_params=params(PARAMS[1]),
        name="grads",
    )(slabs, grouped, middle, xp)


def input_gradient(grads, direct, weights, steps):
    tokens, model = direct.shape
    return pl.pallas_call(
        lambda *refs: inputs_kernel(steps, *refs),
        grid=(model // BLOCK,),
        in_specs=[
            full((2, tokens, model)),
            columns(tokens),
            pl.BlockSpec((BLOCK, 2 * model), lambda j: (j, 0)),
        ],
        out_specs=columns(tokens),
        out_shape=shaped((tokens, model), BF16),
        compiler_params=params(12),
        cost_estimate=pl.CostEstimate(
            flops=4 * tokens * model * model, bytes_accessed=6 * model * model, transcendentals=0
        ),
        name="inputs",
    )(grads, direct, far(weights))


def per_device(
    inputs, gate_in, cotangent, recon_mask, segment_starts, weights, gate_bias, decay_rate
):
    rows, steps, model = inputs.shape
    tokens = rows * steps
    peers, pairs = lax.axis_size("ctx"), lax.axis_size("dp")
    chips = pairs // 2
    swap = [(i, i ^ 1) for i in range(pairs)]
    x_other = lax.ppermute(inputs.reshape(tokens, model).astype(F32), "dp", swap)
    summary, grouped, middle, xp = gates(
        inputs, gate_in, cotangent, recon_mask, segment_starts, weights, gate_bias, decay_rate, peers
    )
    summary, x_other = lax.optimization_barrier((summary, x_other))
    slabs = lax.all_to_all(summary, "ctx", 0, 0, tiled=True)
    part = model // peers
    gate_grad, grads, sent, direct = gradients(slabs, grouped, middle, xp)
    received = lax.ppermute(sent, "dp", swap)
    x_turned = pl.pallas_call(
        lambda *refs: turn_kernel(steps, *refs),
        out_shape=shaped((model, 2 * tokens), BF16),
        compiler_params=params(8),
        name="turn",
    )(xp, x_other)
    piece = shaped((2, part, model))
    held, on2, back2 = pl.pallas_call(
        first_weights_kernel,
        out_shape=[shaped((2 * tokens, model), BF16), piece, piece],
        compiler_params=params(12),
        name="first_weights",
    )(x_turned, grads, received)
    on1, back1, on_last, back_last, stay = pl.pallas_call(
        more_weights_kernel,
        out_shape=[piece] * 4 + [shaped((SIDE, part, model))],
        compiler_params=params(12),
        name="more_weights",
    )(x_turned, held)

    def move(value, step, first):
        pairs_of = []
        for i in range(peers * pairs):
            x, y, d = i // pairs // SIDE, i // pairs % SIDE, i % pairs
            if (d % 2 == 0) == first:
                x = (x + step) % SIDE
            else:
                y = (y + step) % SIDE
            pairs_of.append((i, (x * SIDE + y) * pairs + d))
        return lax.ppermute(value, ("ctx", "dp"), pairs_of)

    came_on2, came_back2 = move(on2, 1, True), move(back2, -1, True)
    came_on1, came_back1 = move(on1, 1, True), move(back1, -1, True)
    came_on1, came_back1, direct = lax.optimization_barrier((came_on1, came_back1, direct))
    came_on = move(on_last + came_on2, 1, True)
    came_back = move(back_last + came_back2, -1, True)
    input_grad = input_gradient(grads, direct, weights, steps)
    came_on, came_back, input_grad = lax.optimization_barrier((came_on, came_back, input_grad))
    scale = 1.0 / math.sqrt(rows * pairs * steps * peers)
    near = shaped((part, model))
    quarters = pl.pallas_call(
        fold_kernel,
        out_shape=[near] * SIDE,
        compiler_params=params(8),
        name="fold",
    )(stay, came_back1, came_on, came_on1, came_back)
    others = [move(quarters[d], d, False) for d in (2, 1, 3)]
    by_chip = pl.pallas_call(
        lambda *refs: sum_kernel(scale, *refs),
        out_shape=shaped((chips, part, LANES)),
        compiler_params=params(4),
        name="slab_sum",
    )(quarters[0], *others)
    same_core = [list(range(core, pairs, 2)) for core in range(2)]
    by_chip = lax.all_to_all(
        by_chip, "dp", 0, 0, axis_index_groups=same_core, tiled=True
    )
    total = jnp.sum(by_chip, axis=0)
    return (
        input_grad.reshape(inputs.shape),
        gate_grad.reshape(inputs.shape),
        total,
    )


def solution(mesh):
    return jax.shard_map(
        per_device,
        mesh=mesh,
        in_specs=(
            P("dp", "ctx", None),
            P("dp", "ctx", None),
            P("dp", "ctx", None),
            P("dp", "ctx"),
            P("dp", None),
            P(),
            P(),
            P(),
        ),
        out_specs=(P("dp", "ctx", None), P("dp", "ctx", None), P("ctx", "dp")),
        check_vma=False,
    )
```

time: 97.8 us -> 83.6 us (0.85)
  blocking collectives: 0 us -> 33.5 us
  starting transfers between devices: 36.7 us -> 11.3 us
  waiting for transfers between devices: 32.5 us -> 18.2 us
  Pallas kernels: 23.3 us -> 17.6 us
  local copies, waits for them, and re-layouts: 2.96 us -> 0 us
  other arithmetic: 0.79 us -> 1.9 us
    all_to_all x0 -> x2, blocking collectives: none -> 33.5 us  [the longest x1 18.7 us: per_device(): lax.all_to_all(by_chip, 'dp', 0, 0, axis_index_groups=same_core, tiled=True)]
    ppermute x8 -> x1, starting transfers between devices: 17.5 us -> 0.09 us  [per_device(): lax.ppermute(inputs.reshape(tokens, model).astype(F32), 'dp', swap)]
    all_to_all x1 -> x0, waiting for transfers between devices: 8.12 us -> none  [per_device(): slabs = lax.all_to_all(summary, 'ctx', 0, 0, tiled=True)]
    all_to_all x1 -> x0, starting transfers between devices: 7.41 us -> none  [per_device(): slabs = lax.all_to_all(summary, 'ctx', 0, 0, tiled=True)]
    pallas_call x6 -> x7, Pallas kernels: 23.2 us -> 17.5 us  [the longest x1 7.05 us: gates(): pl.pallas_call(gates_kernel, grid=(blocks,), in_specs=[full(segment_start...]
    ppermute x8 -> x1, waiting for transfers between devices: 3.52 us -> 0.01 us  [per_device(): lax.ppermute(inputs.reshape(tokens, model).astype(F32), 'dp', swap)]
    unnamed x6 -> x0, local copies, waits for them, and re-layouts: 2.96 us -> none
    ppermute x9, waiting for transfers between devices: 18.2 us -> 15.9 us  [move(): return lax.ppermute(value, ('ctx', 'dp'), pairs_of)]
  transfers between devices with their start and end apart: 19 -> 11, of which waited for: 11 -> 7; matrix products, arithmetic and copies ran while one was open for 0% -> 0% of each run, Pallas kernels for 6% -> 17%
where the time goes in v3:
time: 83.6 us; the launch traced here: 83.2 us
  blocking collectives  33.5 us (40%)
  waiting for transfers between devices  18.2 us (22%)
  Pallas kernels  17.6 us (21%)
  starting transfers between devices  11.3 us (14%)
  other arithmetic  1.9 us (2%)
    all_to_all x1, blocking collectives, per_device(): lax.all_to_all(by_chip, 'dp', 0, 0, axis_index_groups=same_core, tiled=True)  18.7 us
    ppermute x9, waiting for transfers between devices, move(): return lax.ppermute(value, ('ctx', 'dp'), pairs_of)  15.9 us
    all_to_all x1, blocking collectives, per_device(): slabs = lax.all_to_all(summary, 'ctx', 0, 0, tiled=True)  14.8 us
    ppermute x9, starting transfers between devices, move(): return lax.ppermute(value, ('ctx', 'dp'), pairs_of)  11.2 us
    pallas_call x1, Pallas kernels, gates(): pl.pallas_call(gates_kernel, grid=(blocks,), in_specs=[full(segment_start...  7.05 us
    pallas_call x1, Pallas kernels, input_gradient(): pl.pallas_call(lambda *refs: inputs_kernel(steps, *refs), grid=(model //...  5.43 us
    pallas_call x1, Pallas kernels, gradients(): pl.pallas_call(grads_kernel, grid=(model // BLOCK,), in_specs=[near] * 4,...  2.94 us
    ppermute x1, waiting for transfers between devices, per_device(): received = lax.ppermute(sent, 'dp', swap)  2.25 us
  transfers between devices with their start and end apart: 11, of which 7 were waited for; matrix products, arithmetic and copies ran while one was open for 0% of the time, Pallas kernels for 17%

profile of v3, /device:TPU:8, one launch (start us, length us, event | category | flops | bytes accessed | tf_op | source)
XLA Modules:
  0.0 83.2 jit_solution(8056593508213668835)
XLA Ops:
  0.6 1.1 %bitcast_convert_fusion = f32[256,1024]{1,0:T(8,128)S(1)} fusion(bf16[2,128,1024]{2,1,0:T(8,128)(2,1)} %param.8), kind=kLoop, calls=%fused_computation | loop fusion | flops 262144 | bytes 1572864 | tf_op jit(solution)/shard_map/convert_element_type | solution.py:411
  1.9 7.1 %gates.1 = (f32[16,4,1024]{2,1,0:T(4,128)S(1)}, f32[48,1024]{1,0:T(8,128)S(1)}, f32[7,256,1024]{2,1,0:T(8,128)S(1)}, f32[256,1024]{1,0:T(8,128)S(1)}) custom-call(s32[2,3]{1,0:T(2,128)} %starts.1, bf16[256,1024]{1,0:T(8,128)(2,1)} %bitcast.8, bf16[256,1024]{1,0:T(8,128)(2,1)} %bitcast.9, bf16[256,1024]{1,0:T(8,128)(2,1)} %bitcast.10, s32[2,128]{1,0:T(2,128)} %mask.1, ...), custom_call_target="tpu_custom_call" | custom-call | tf_op jit(solution)/shard_map/gates/pallas_call | solution.py:328
  9.0 14.8 %all_to_all.10.slabs = f32[16,4,1024]{2,1,0:T(4,128)S(1)} all-to-all(f32[16,4,1024]{2,1,0:T(4,128)S(1)} %get-tuple-element.34), channel_id=1, replica_groups=mesh['ctx'=16,'dp'=16] {'ctx'}, dimensions={0} | all-to-all | bytes 524288 | tf_op jit(solution)/shard_map/all_to_all | solution.py:416
  23.7 2.9 %grads.1 = (bf16[256,1024]{1,0:T(8,128)(2,1)}, bf16[2,256,1024]{2,1,0:T(8,128)(2,1)S(1)}, f32[2,256,512]{2,1,0:T(8,128)S(1)}, f32[256,1024]{1,0:T(8,128)S(1)}) custom-call(f32[16,4,1024]{2,1,0:T(4,128)S(1)} %all_to_all.10.slabs, f32[48,1024]{1,0:T(8,128)S(1)} %get-tuple-element.35.grouped, f32[7,256,1024]{2,1,0:T(8,128)S(1)} %get-tuple-element.36.middle, ...), custom_call_target="tpu_custom_call" | custom-call | tf_op jit(solution)/shard_map/grads/pallas_call | solution.py:366
  26.7 0.4 turn.1.x_turned
  27.1 2.3 %collective-permute-done.1.received = f32[2,256,512]{2,1,0:T(8,128)S(1)} collective-permute-done((f32[2,256,512]{2,1,0:T(8,128)S(1)}, f32[2,256,512]{2,1,0:T(8,128)S(1)}, u32[]{:S(2)}, u32[]{:S(2)}) %collective-permute-start.1) | collective-permute-done | bytes 1048608 | tf_op jit(solution)/shard_map/ppermute | solution.py:419
  29.3 0.6 first_weights.1
  30.0 1.3 %collective-permute-start.4 = (f32[2,64,1024]{2,1,0:T(8,128)S(1)}, f32[2,64,1024]{2,1,0:T(8,128)S(1)}, u32[]{:S(2)}, u32[]{:S(2)}) collective-permute-start(f32[2,64,1024]{2,1,0:T(8,128)S(1)} %get-tuple-element.43), channel_id=1, source_target_pairs={{0,192},{1,49},{2,194},{3,51},{4,196},{5,53},{6,198},{7,55},{8,200... | collective-permute-start | bytes 1572872 | tf_op jit(solution)/shard_map/ppermute | solution.py:449
  31.2 0.8 %collective-permute-start.2 = (f32[2,64,1024]{2,1,0:T(8,128)S(1)}, f32[2,64,1024]{2,1,0:T(8,128)S(1)}, u32[]{:S(2)}, u32[]{:S(2)}) collective-permute-start(f32[2,64,1024]{2,1,0:T(8,128)S(1)} %get-tuple-element.41), channel_id=1, source_target_pairs={{0,64},{1,17},{2,66},{3,19},{4,68},{5,21},{6,70},{7,23},{8,72},{9,... | collective-permute-start | bytes 1572872 | tf_op jit(solution)/shard_map/ppermute | solution.py:449
  32.1 1.0 %more_weights.1 = (f32[2,64,1024]{2,1,0:T(8,128)S(1)}, f32[2,64,1024]{2,1,0:T(8,128)S(1)}, f32[2,64,1024]{2,1,0:T(8,128)S(1)}, f32[2,64,1024]{2,1,0:T(8,128)S(1)}, f32[4,64,1024]{2,1,0:T(8,128)S(1)}) custom-call(bf16[1024,512]{1,0:T(8,128)(2,1)S(1)} %turn.1.x_turned, bf16[512,1024]{1,0:T(8,128)(2,1)S(1)} %get-tuple-element.39.held), custom_call_target="tpu_custom_call" | custom-call | tf_op jit(solution)/shard_map/more_weights/pallas_call | solution.py:433
  33.2 3.2 %collective-permute-start.7 = (f32[2,64,1024]{2,1,0:T(8,128)S(1)}, f32[2,64,1024]{2,1,0:T(8,128)S(1)}, u32[]{:S(2)}, u32[]{:S(2)}) collective-permute-start(f32[2,64,1024]{2,1,0:T(8,128)S(1)} %get-tuple-element.45), channel_id=1, source_target_pairs={{0,192},{1,49},{2,194},{3,51},{4,196},{5,53},{6,198},{7,55},{8,200... | collective-permute-start | bytes 1572872 | tf_op jit(solution)/shard_map/ppermute | solution.py:449
  36.4 2.8 %collective-permute-done.4 = f32[2,64,1024]{2,1,0:T(8,128)S(1)} collective-permute-done((f32[2,64,1024]{2,1,0:T(8,128)S(1)}, f32[2,64,1024]{2,1,0:T(8,128)S(1)}, u32[]{:S(2)}, u32[]{:S(2)}) %collective-permute-start.4) | collective-permute-done | bytes 524320 | tf_op jit(solution)/shard_map/ppermute | solution.py:449
  39.3 2.5 %collective-permute-start.5 = (f32[2,64,1024]{2,1,0:T(8,128)S(1)}, f32[2,64,1024]{2,1,0:T(8,128)S(1)}, u32[]{:S(2)}, u32[]{:S(2)}) collective-permute-start(f32[2,64,1024]{2,1,0:T(8,128)S(1)} %add.7), channel_id=1, source_target_pairs={{0,192},{1,49},{2,194},{3,51},{4,196},{5,53},{6,198},{7,55},{8,200... | collective-permute-start | bytes 1572872 | tf_op jit(solution)/shard_map/ppermute | solution.py:449
  41.9 5.3 %collective-permute-done.6.high = f32[2,64,1024]{2,1,0:T(8,128)S(1)} collective-permute-done((f32[2,64,1024]{2,1,0:T(8,128)S(1)}, f32[2,64,1024]{2,1,0:T(8,128)S(1)}, u32[]{:S(2)}, u32[]{:S(2)}) %collective-permute-start.6) | collective-permute-done | bytes 524320 | tf_op jit(solution)/shard_map/ppermute | solution.py:449
  47.3 5.4 %inputs.1 = bf16[256,1024]{1,0:T(8,128)(2,1)} custom-call(bf16[2,256,1024]{2,1,0:T(8,128)(2,1)S(1)} %get-tuple-element.37.grads.refs_0_, f32[256,1024]{1,0:T(8,128)S(1)} %get-tuple-element.47.refs_1_, bf16[1024,2048]{1,0:T(8,128)(2,1)} %refs_2_.1), custom_call_target="tpu_custom_call" | custom-call | flops 1073741824 | bytes 6291456 | tf_op jit(solution)/shard_map/inputs/pallas_call | solution.py:385
  52.7 0.2 collective-permute-done.3.low_more
  53.0 1.2 %collective-permute-start.8 = (f32[64,1024]{1,0:T(8,128)S(1)}, f32[64,1024]{1,0:T(8,128)S(1)}, u32[]{:S(2)}, u32[]{:S(2)}) collective-permute-start(f32[64,1024]{1,0:T(8,128)S(1)} %get-tuple-element.56), channel_id=1, source_target_pairs={{0,32},{1,129},{2,34},{3,131},{4,36},{5,133},{6,38},{7,135},{8,40}... | collective-permute-start | bytes 786440 | tf_op jit(solution)/shard_map/ppermute | solution.py:449
  54.2 1.8 %collective-permute-start.9 = (f32[64,1024]{1,0:T(8,128)S(1)}, f32[64,1024]{1,0:T(8,128)S(1)}, u32[]{:S(2)}, u32[]{:S(2)}) collective-permute-start(f32[64,1024]{1,0:T(8,128)S(1)} %get-tuple-element.57), channel_id=1, source_target_pairs={{0,16},{1,65},{2,18},{3,67},{4,20},{5,69},{6,22},{7,71},{8,24},{9,... | collective-permute-start | bytes 786440 | tf_op jit(solution)/shard_map/ppermute | solution.py:449
  56.0 0.2 collective-permute-start.10
  56.3 4.8 %collective-permute-done.8.refs_1_ = f32[64,1024]{1,0:T(8,128)S(1)} collective-permute-done((f32[64,1024]{1,0:T(8,128)S(1)}, f32[64,1024]{1,0:T(8,128)S(1)}, u32[]{:S(2)}, u32[]{:S(2)}) %collective-permute-start.8) | collective-permute-done | bytes 262176 | tf_op jit(solution)/shard_map/ppermute | solution.py:449
  61.1 2.1 %collective-permute-done.9.refs_2_ = f32[64,1024]{1,0:T(8,128)S(1)} collective-permute-done((f32[64,1024]{1,0:T(8,128)S(1)}, f32[64,1024]{1,0:T(8,128)S(1)}, u32[]{:S(2)}, u32[]{:S(2)}) %collective-permute-start.9) | collective-permute-done | bytes 262176 | tf_op jit(solution)/shard_map/ppermute | solution.py:449
  63.2 0.6 collective-permute-done.10.refs_3_
  63.9 18.7 %all_to_all.11 = f32[8,64,128]{2,1,0:T(8,128)S(1)} all-to-all(f32[8,64,128]{2,1,0:T(8,128)S(1)} %slab_sum.1), channel_id=1, replica_groups={{0,2,4,6,8,10,12,14},{1,3,5,7,9,11,13,15},{16,18,20,22,24,26,28,30},{17..., dimensions={0} | all-to-all | bytes 524288 | tf_op jit(solution)/shard_map/all_to_all | solution.py:474
  82.6 0.6 reduce_sum.9
  (12 shorter events, 0.7 us)
Async XLA Ops:
  1.8 7.2 %collective-permute-start = (f32[256,1024]{1,0:T(8,128)S(1)}, f32[256,1024]{1,0:T(8,128)S(1)}, u32[]{:S(2)}, u32[]{:S(2)}) collective-permute-start(f32[256,1024]{1,0:T(8,128)S(1)} %bitcast_convert_fusion), channel_id=1, source_target_pairs={{0,1},{1,0},{2,3},{3,2},{4,5},{5,4},{6,7},{7,6},{8,9},{9,8},{10,11... | collective-permute-start | bytes 3145736 | tf_op jit(solution)/shard_map/ppermute | solution.py:411
  26.7 2.7 %collective-permute-start.1 = (f32[2,256,512]{2,1,0:T(8,128)S(1)}, f32[2,256,512]{2,1,0:T(8,128)S(1)}, u32[]{:S(2)}, u32[]{:S(2)}) collective-permute-start(f32[2,256,512]{2,1,0:T(8,128)S(1)} %get-tuple-element.38), channel_id=1, source_target_pairs={{0,1},{1,0},{2,3},{3,2},{4,5},{5,4},{6,7},{7,6},{8,9},{9,8},{10,11... | collective-permute-start | bytes 3145736 | tf_op jit(solution)/shard_map/ppermute | solution.py:419
  30.0 9.3 %collective-permute-start.4 = (f32[2,64,1024]{2,1,0:T(8,128)S(1)}, f32[2,64,1024]{2,1,0:T(8,128)S(1)}, u32[]{:S(2)}, u32[]{:S(2)}) collective-permute-start(f32[2,64,1024]{2,1,0:T(8,128)S(1)} %get-tuple-element.43), channel_id=1, source_target_pairs={{0,192},{1,49},{2,194},{3,51},{4,196},{5,53},{6,198},{7,55},{8,200... | collective-permute-start | bytes 1572872 | tf_op jit(solution)/shard_map/ppermute | solution.py:449
  31.2 10.5 %collective-permute-start.2 = (f32[2,64,1024]{2,1,0:T(8,128)S(1)}, f32[2,64,1024]{2,1,0:T(8,128)S(1)}, u32[]{:S(2)}, u32[]{:S(2)}) collective-permute-start(f32[2,64,1024]{2,1,0:T(8,128)S(1)} %get-tuple-element.41), channel_id=1, source_target_pairs={{0,64},{1,17},{2,66},{3,19},{4,68},{5,21},{6,70},{7,23},{8,72},{9,... | collective-permute-start | bytes 1572872 | tf_op jit(solution)/shard_map/ppermute | solution.py:449
  33.1 14.2 %collective-permute-start.6 = (f32[2,64,1024]{2,1,0:T(8,128)S(1)}, f32[2,64,1024]{2,1,0:T(8,128)S(1)}, u32[]{:S(2)}, u32[]{:S(2)}) collective-permute-start(f32[2,64,1024]{2,1,0:T(8,128)S(1)} %get-tuple-element.44), channel_id=1, source_target_pairs={{0,64},{1,17},{2,66},{3,19},{4,68},{5,21},{6,70},{7,23},{8,72},{9,... | collective-permute-start | bytes 1572872 | tf_op jit(solution)/shard_map/ppermute | solution.py:449
  33.2 14.0 %collective-permute-start.7 = (f32[2,64,1024]{2,1,0:T(8,128)S(1)}, f32[2,64,1024]{2,1,0:T(8,128)S(1)}, u32[]{:S(2)}, u32[]{:S(2)}) collective-permute-start(f32[2,64,1024]{2,1,0:T(8,128)S(1)} %get-tuple-element.45), channel_id=1, source_target_pairs={{0,192},{1,49},{2,194},{3,51},{4,196},{5,53},{6,198},{7,55},{8,200... | collective-permute-start | bytes 1572872 | tf_op jit(solution)/shard_map/ppermute | solution.py:449
  39.3 13.4 %collective-permute-start.5 = (f32[2,64,1024]{2,1,0:T(8,128)S(1)}, f32[2,64,1024]{2,1,0:T(8,128)S(1)}, u32[]{:S(2)}, u32[]{:S(2)}) collective-permute-start(f32[2,64,1024]{2,1,0:T(8,128)S(1)} %add.7), channel_id=1, source_target_pairs={{0,192},{1,49},{2,194},{3,51},{4,196},{5,53},{6,198},{7,55},{8,200... | collective-permute-start | bytes 1572872 | tf_op jit(solution)/shard_map/ppermute | solution.py:449
  41.9 11.0 %collective-permute-start.3 = (f32[2,64,1024]{2,1,0:T(8,128)S(1)}, f32[2,64,1024]{2,1,0:T(8,128)S(1)}, u32[]{:S(2)}, u32[]{:S(2)}) collective-permute-start(f32[2,64,1024]{2,1,0:T(8,128)S(1)} %add.6), channel_id=1, source_target_pairs={{0,64},{1,17},{2,66},{3,19},{4,68},{5,21},{6,70},{7,23},{8,72},{9,... | collective-permute-start | bytes 1572872 | tf_op jit(solution)/shard_map/ppermute | solution.py:449
  53.0 8.1 %collective-permute-start.8 = (f32[64,1024]{1,0:T(8,128)S(1)}, f32[64,1024]{1,0:T(8,128)S(1)}, u32[]{:S(2)}, u32[]{:S(2)}) collective-permute-start(f32[64,1024]{1,0:T(8,128)S(1)} %get-tuple-element.56), channel_id=1, source_target_pairs={{0,32},{1,129},{2,34},{3,131},{4,36},{5,133},{6,38},{7,135},{8,40}... | collective-permute-start | bytes 786440 | tf_op jit(solution)/shard_map/ppermute | solution.py:449
  54.2 9.0 %collective-permute-start.9 = (f32[64,1024]{1,0:T(8,128)S(1)}, f32[64,1024]{1,0:T(8,128)S(1)}, u32[]{:S(2)}, u32[]{:S(2)}) collective-permute-start(f32[64,1024]{1,0:T(8,128)S(1)} %get-tuple-element.57), channel_id=1, source_target_pairs={{0,16},{1,65},{2,18},{3,67},{4,20},{5,69},{6,22},{7,71},{8,24},{9,... | collective-permute-start | bytes 786440 | tf_op jit(solution)/shard_map/ppermute | solution.py:449
  56.0 7.8 %collective-permute-start.10 = (f32[64,1024]{1,0:T(8,128)S(1)}, f32[64,1024]{1,0:T(8,128)S(1)}, u32[]{:S(2)}, u32[]{:S(2)}) collective-permute-start(f32[64,1024]{1,0:T(8,128)S(1)} %get-tuple-element.58), channel_id=1, source_target_pairs={{0,48},{1,193},{2,50},{3,195},{4,52},{5,197},{6,54},{7,199},{8,56}... | collective-permute-start | bytes 786440 | tf_op jit(solution)/shard_map/ppermute | solution.py:449

commit v4 on v3

--- a/solution.py
+++ b/solution.py
@@ -15,6 +15,8 @@
 ROOT = math.sqrt(2.0 / math.pi)
 CUBIC = 0.044715
 SIDE = 4
+WIDE = 512
+WIDTH = 512
 UNROLL = (16, 16, 16, 16)
 PARAMS = (28, 28)
 PIECES = (8, 10, 6, 12, 4, 14, 0)
@@ -26,10 +28,11 @@
 
 def order(tokens, steps, transpose=False):
     inner = steps // GROUPS
+    shift, mask = GROUPS.bit_length() - 1, steps - 1
     rho = lax.broadcasted_iota(jnp.int32, (tokens, tokens), 1 if transpose else 0)
     at = lax.broadcasted_iota(jnp.int32, (tokens, tokens), 0 if transpose else 1)
-    place = rho % steps
-    source = (rho - place) + (place % GROUPS) * inner + place // GROUPS
+    place = rho & mask
+    source = (rho - place) + (place & (GROUPS - 1)) * inner + (place >> shift)
     return at == source
 
 
@@ -210,6 +213,7 @@
         return tuple(new)
 
     lax.fori_loop(0, inner, back, tuple(enter_back), unroll=UNROLL[3])
+
     unmove = jnp.where(order(tokens, steps, True), 1.0, 0.0).astype(BF16)
     gate_grad[...] = dot(unmove, ggs[...].astype(BF16)).astype(BF16)
     other = lax.axis_index("dp") % 2 == 0
@@ -218,18 +222,14 @@
         sent[half, :, to_send] = jnp.where(other, value[:, LANES:], value[:, :LANES])
 
 
-def turn_kernel(steps, x_own, x_other, out):
+def turn_kernel(x_own, x_other, out):
     tokens, model = x_own.shape
     part = model // (SIDE * SIDE)
     core = lax.axis_index("dp") % 2
     my_x, my_y = lax.axis_index("ctx") // SIDE, lax.axis_index("ctx") % SIDE
-    place = jnp.where(order(tokens, steps), 1.0, 0.0).astype(BF16)
     for s, value in enumerate((x_own, x_other)):
         for bx in range(SIDE):
-            turned = value[:, pl.ds(bx * SIDE * part, SIDE * part)]
-            if s == 1:
-                turned = dot(place, turned.astype(BF16))
-            turned = turned.T.astype(BF16)
+            turned = value[:, pl.ds(bx * SIDE * part, SIDE * part)].T.astype(BF16)
             for by in range(SIDE):
                 dx, dy = (bx - my_x + SIDE) % SIDE, (by - my_y + SIDE) % SIDE
                 block = jnp.where(core == 0, dx * SIDE + dy, dy * SIDE + dx)
@@ -274,12 +274,13 @@
 
 
 def inputs_kernel(steps, grads, direct, weights, out):
-    width = grads.shape[2]
-    tokens = direct.shape[0]
-    total = direct[...]
+    model = direct.shape[1]
+    tokens, width = out.shape
+    at = pl.ds(pl.multiple_of(pl.program_id(0) * width, width), width)
+    total = direct[:, at]
     for half in range(2):
         total = total + dot(
-            grads[half], weights[:, half * width : (half + 1) * width], ((1,), (1,))
+            grads[half], weights[at, pl.ds(half * model, model)], ((1,), (1,))
         )
     unmove = jnp.where(order(tokens, steps, True), 1.0, 0.0).astype(BF16)
     out[...] = dot(unmove, total.astype(BF16)).astype(BF16)
@@ -320,10 +321,10 @@
 ):
     rows, steps, model = inputs.shape
     tokens = rows * steps
-    blocks = model // BLOCK
+    blocks = model // WIDTH
     flat = lambda value: value.reshape(tokens, model)
     bias = gate_bias.reshape(1, 2 * model)
-    tile = columns(tokens)
+    tile = columns(tokens, WIDTH)
     near = pl.BlockSpec(memory_space=pltpu.VMEM)
     return pl.pallas_call(
         gates_kernel,
@@ -334,12 +335,12 @@
             tile,
             tile,
             full((rows, steps)),
-            columns(model),
-            columns(model, first=blocks),
+            columns(model, WIDTH),
+            columns(model, WIDTH, blocks),
             full((1, 2 * model)),
             full((1, model)),
         ],
-        out_specs=[pl.BlockSpec((peers, 2 * rows, BLOCK), lambda j: (0, 0, j)), near, near, near],
+        out_specs=[pl.BlockSpec((peers, 2 * rows, WIDTH), lambda j: (0, 0, j)), near, near, near],
         out_shape=[
             shaped((peers, 2 * rows, model)),
             pltpu.VMEM((3 * rows * GROUPS, model), F32),
@@ -351,7 +352,7 @@
             pltpu.VMEM((tokens, tokens), BF16),
             pltpu.VMEM((tokens, model), BF16),
         ]
-        + [pltpu.VMEM((tokens, BLOCK), F32)] * 4,
+        + [pltpu.VMEM((tokens, WIDTH), F32)] * 4,
         compiler_params=params(PARAMS[0]),
         name="gates",
     )(
@@ -382,22 +383,19 @@
 
 def input_gradient(grads, direct, weights, steps):
     tokens, model = direct.shape
+    near = pl.BlockSpec(memory_space=pltpu.VMEM)
     return pl.pallas_call(
         lambda *refs: inputs_kernel(steps, *refs),
-        grid=(model // BLOCK,),
-        in_specs=[
-            full((2, tokens, model)),
-            columns(tokens),
-            pl.BlockSpec((BLOCK, 2 * model), lambda j: (j, 0)),
-        ],
-        out_specs=columns(tokens),
+        grid=(model // WIDE,),
+        in_specs=[near] * 3,
+        out_specs=columns(tokens, WIDE),
         out_shape=shaped((tokens, model), BF16),
-        compiler_params=params(12),
+        compiler_params=params(16),
         cost_estimate=pl.CostEstimate(
             flops=4 * tokens * model * model, bytes_accessed=6 * model * model, transcendentals=0
         ),
         name="inputs",
-    )(grads, direct, far(weights))
+    )(grads, direct, weights)
 
 
 def per_device(
@@ -407,18 +405,18 @@
     tokens = rows * steps
     peers, pairs = lax.axis_size("ctx"), lax.axis_size("dp")
     chips = pairs // 2
-    swap = [(i, i ^ 1) for i in range(pairs)]
-    x_other = lax.ppermute(inputs.reshape(tokens, model).astype(F32), "dp", swap)
     summary, grouped, middle, xp = gates(
         inputs, gate_in, cotangent, recon_mask, segment_starts, weights, gate_bias, decay_rate, peers
     )
-    summary, x_other = lax.optimization_barrier((summary, x_other))
     slabs = lax.all_to_all(summary, "ctx", 0, 0, tiled=True)
+    slabs, xp = lax.optimization_barrier((slabs, xp))
+    swap = [(i, i ^ 1) for i in range(pairs)]
+    x_other = lax.ppermute(xp, "dp", swap)
     part = model // peers
     gate_grad, grads, sent, direct = gradients(slabs, grouped, middle, xp)
     received = lax.ppermute(sent, "dp", swap)
     x_turned = pl.pallas_call(
-        lambda *refs: turn_kernel(steps, *refs),
+        turn_kernel,
         out_shape=shaped((model, 2 * tokens), BF16),
         compiler_params=params(8),
         name="turn",

time: 83.6 us -> 81.1 us (0.970)
  Pallas kernels: 17.6 us -> 14.2 us
  waiting for transfers between devices: 18.2 us -> 20.6 us
  other arithmetic: 1.9 us -> 0.77 us
    pallas_call x1, Pallas kernels: 5.43 us -> 2.6 us  [input_gradient(): pl.pallas_call(lambda *refs: inputs_kernel(steps, *refs), grid=(model //...]
    ppermute x9, waiting for transfers between devices: 15.9 us -> 18.6 us  [move(): return lax.ppermute(value, ('ctx', 'dp'), pairs_of)]
    convert_element_type x1 -> x0, other arithmetic: 1.15 us -> none  [per_device(): inputs.reshape(tokens, model).astype(F32)]
  transfers between devices with their start and end apart: 11 -> 11, of which waited for: 7 -> 8; matrix products, arithmetic and copies ran while one was open for 0% -> 0% of each run, Pallas kernels for 17% -> 8%
where the time goes in v4:
time: 81.1 us; the launch traced here: 81 us
  blocking collectives  33 us (41%)
  waiting for transfers between devices  20.6 us (25%)
  Pallas kernels  14.2 us (18%)
  starting transfers between devices  11.7 us (14%)
    all_to_all x1, blocking collectives, per_device(): lax.all_to_all(by_chip, 'dp', 0, 0, axis_index_groups=same_core, tiled=True)  18.7 us
    ppermute x9, waiting for transfers between devices, move(): return lax.ppermute(value, ('ctx', 'dp'), pairs_of)  18.6 us
    all_to_all x1, blocking collectives, per_device(): slabs = lax.all_to_all(summary, 'ctx', 0, 0, tiled=True)  14.3 us
    ppermute x9, starting transfers between devices, move(): return lax.ppermute(value, ('ctx', 'dp'), pairs_of)  11.2 us
    pallas_call x1, Pallas kernels, gates(): pl.pallas_call(gates_kernel, grid=(blocks,), in_specs=[full(segment_start...  6.52 us
    pallas_call x1, Pallas kernels, gradients(): pl.pallas_call(grads_kernel, grid=(model // BLOCK,), in_specs=[near] * 4,...  2.92 us
    pallas_call x1, Pallas kernels, input_gradient(): pl.pallas_call(lambda *refs: inputs_kernel(steps, *refs), grid=(model //...  2.6 us
    ppermute x1, waiting for transfers between devices, per_device(): received = lax.ppermute(sent, 'dp', swap)  1.94 us
  transfers between devices with their start and end apart: 11, of which 8 were waited for; matrix products, arithmetic and copies ran while one was open for 0% of the time, Pallas kernels for 8%

profile of v4, /device:TPU:8, one launch (start us, length us, event | category | flops | bytes accessed | tf_op | source)
XLA Modules:
  0.0 81.0 jit_solution(18419763118762514492)
XLA Ops:
  0.6 6.5 %gates.1 = (f32[16,4,1024]{2,1,0:T(4,128)S(1)}, f32[48,1024]{1,0:T(8,128)S(1)}, f32[7,256,1024]{2,1,0:T(8,128)S(1)}, f32[256,1024]{1,0:T(8,128)S(1)}) custom-call(s32[2,3]{1,0:T(2,128)} %starts.1, bf16[256,1024]{1,0:T(8,128)(2,1)} %bitcast.7, bf16[256,1024]{1,0:T(8,128)(2,1)} %bitcast.8, bf16[256,1024]{1,0:T(8,128)(2,1)} %bitcast.9, s32[2,128]{1,0:T(2,128)} %mask.1, ...), custom_call_target="tpu_custom_call" | custom-call | tf_op jit(solution)/shard_map/gates/pallas_call | solution.py:329
  7.2 14.3 %all_to_all.10.slabs = f32[16,4,1024]{2,1,0:T(4,128)S(1)} all-to-all(f32[16,4,1024]{2,1,0:T(4,128)S(1)} %get-tuple-element.31), channel_id=1, replica_groups=mesh['ctx'=16,'dp'=16] {'ctx'}, dimensions={0} | all-to-all | bytes 524288 | tf_op jit(solution)/shard_map/all_to_all | solution.py:411
  21.4 2.9 %grads.1 = (bf16[256,1024]{1,0:T(8,128)(2,1)}, bf16[2,256,1024]{2,1,0:T(8,128)(2,1)S(1)}, f32[2,256,512]{2,1,0:T(8,128)S(1)}, f32[256,1024]{1,0:T(8,128)S(1)}) custom-call(f32[16,4,1024]{2,1,0:T(4,128)S(1)} %all_to_all.10.slabs, f32[48,1024]{1,0:T(8,128)S(1)} %get-tuple-element.35.grouped, f32[7,256,1024]{2,1,0:T(8,128)S(1)} %get-tuple-element.36.middle, ...), custom_call_target="tpu_custom_call" | custom-call | tf_op jit(solution)/shard_map/grads/pallas_call | solution.py:367
  24.4 0.5 collective-permute-start.1
  24.9 0.3 turn.1.x_turned
  25.2 1.9 %collective-permute-done.1.received = f32[2,256,512]{2,1,0:T(8,128)S(1)} collective-permute-done((f32[2,256,512]{2,1,0:T(8,128)S(1)}, f32[2,256,512]{2,1,0:T(8,128)S(1)}, u32[]{:S(2)}, u32[]{:S(2)}) %collective-permute-start.1) | collective-permute-done | bytes 1048608 | tf_op jit(solution)/shard_map/ppermute | solution.py:417
  27.1 0.6 first_weights.1
  27.8 1.2 %collective-permute-start.4 = (f32[2,64,1024]{2,1,0:T(8,128)S(1)}, f32[2,64,1024]{2,1,0:T(8,128)S(1)}, u32[]{:S(2)}, u32[]{:S(2)}) collective-permute-start(f32[2,64,1024]{2,1,0:T(8,128)S(1)} %get-tuple-element.43), channel_id=1, source_target_pairs={{0,192},{1,49},{2,194},{3,51},{4,196},{5,53},{6,198},{7,55},{8,200... | collective-permute-start | bytes 1572872 | tf_op jit(solution)/shard_map/ppermute | solution.py:447
  29.0 0.9 %collective-permute-start.2 = (f32[2,64,1024]{2,1,0:T(8,128)S(1)}, f32[2,64,1024]{2,1,0:T(8,128)S(1)}, u32[]{:S(2)}, u32[]{:S(2)}) collective-permute-start(f32[2,64,1024]{2,1,0:T(8,128)S(1)} %get-tuple-element.41), channel_id=1, source_target_pairs={{0,64},{1,17},{2,66},{3,19},{4,68},{5,21},{6,70},{7,23},{8,72},{9,... | collective-permute-start | bytes 1572872 | tf_op jit(solution)/shard_map/ppermute | solution.py:447
  29.9 1.0 %more_weights.1 = (f32[2,64,1024]{2,1,0:T(8,128)S(1)}, f32[2,64,1024]{2,1,0:T(8,128)S(1)}, f32[2,64,1024]{2,1,0:T(8,128)S(1)}, f32[2,64,1024]{2,1,0:T(8,128)S(1)}, f32[4,64,1024]{2,1,0:T(8,128)S(1)}) custom-call(bf16[1024,512]{1,0:T(8,128)(2,1)S(1)} %turn.1.x_turned, bf16[512,1024]{1,0:T(8,128)(2,1)S(1)} %get-tuple-element.39.held), custom_call_target="tpu_custom_call" | custom-call | tf_op jit(solution)/shard_map/more_weights/pallas_call | solution.py:431
  31.2 3.0 %collective-permute-start.7 = (f32[2,64,1024]{2,1,0:T(8,128)S(1)}, f32[2,64,1024]{2,1,0:T(8,128)S(1)}, u32[]{:S(2)}, u32[]{:S(2)}) collective-permute-start(f32[2,64,1024]{2,1,0:T(8,128)S(1)} %get-tuple-element.45), channel_id=1, source_target_pairs={{0,192},{1,49},{2,194},{3,51},{4,196},{5,53},{6,198},{7,55},{8,200... | collective-permute-start | bytes 1572872 | tf_op jit(solution)/shard_map/ppermute | solution.py:447
  34.2 2.8 %collective-permute-done.4 = f32[2,64,1024]{2,1,0:T(8,128)S(1)} collective-permute-done((f32[2,64,1024]{2,1,0:T(8,128)S(1)}, f32[2,64,1024]{2,1,0:T(8,128)S(1)}, u32[]{:S(2)}, u32[]{:S(2)}) %collective-permute-start.4) | collective-permute-done | bytes 524320 | tf_op jit(solution)/shard_map/ppermute | solution.py:447
  37.1 2.4 %collective-permute-start.5 = (f32[2,64,1024]{2,1,0:T(8,128)S(1)}, f32[2,64,1024]{2,1,0:T(8,128)S(1)}, u32[]{:S(2)}, u32[]{:S(2)}) collective-permute-start(f32[2,64,1024]{2,1,0:T(8,128)S(1)} %add.7), channel_id=1, source_target_pairs={{0,192},{1,49},{2,194},{3,51},{4,196},{5,53},{6,198},{7,55},{8,200... | collective-permute-start | bytes 1572872 | tf_op jit(solution)/shard_map/ppermute | solution.py:447
  39.7 5.3 %collective-permute-done.6.high = f32[2,64,1024]{2,1,0:T(8,128)S(1)} collective-permute-done((f32[2,64,1024]{2,1,0:T(8,128)S(1)}, f32[2,64,1024]{2,1,0:T(8,128)S(1)}, u32[]{:S(2)}, u32[]{:S(2)}) %collective-permute-start.6) | collective-permute-done | bytes 524320 | tf_op jit(solution)/shard_map/ppermute | solution.py:447
  45.0 2.6 %inputs.1 = bf16[256,1024]{1,0:T(8,128)(2,1)} custom-call(bf16[2,256,1024]{2,1,0:T(8,128)(2,1)S(1)} %get-tuple-element.37.grads.refs_0_, f32[256,1024]{1,0:T(8,128)S(1)} %get-tuple-element.47.refs_1_, bf16[1024,2048]{1,0:T(8,128)(2,1)S(1)} %copy-done), custom_call_target="tpu_custom_call" | custom-call | flops 1073741824 | bytes 6291456 | tf_op jit(solution)/shard_map/inputs/pallas_call | solution.py:387
  47.6 0.7 collective-permute-done.5.high_more
  48.3 2.3 %collective-permute-done.3.low_more = f32[2,64,1024]{2,1,0:T(8,128)S(1)} collective-permute-done((f32[2,64,1024]{2,1,0:T(8,128)S(1)}, f32[2,64,1024]{2,1,0:T(8,128)S(1)}, u32[]{:S(2)}, u32[]{:S(2)}) %collective-permute-start.3) | collective-permute-done | bytes 524320 | tf_op jit(solution)/shard_map/ppermute | solution.py:447
  50.8 1.3 %collective-permute-start.8 = (f32[64,1024]{1,0:T(8,128)S(1)}, f32[64,1024]{1,0:T(8,128)S(1)}, u32[]{:S(2)}, u32[]{:S(2)}) collective-permute-start(f32[64,1024]{1,0:T(8,128)S(1)} %get-tuple-element.56), channel_id=1, source_target_pairs={{0,32},{1,129},{2,34},{3,131},{4,36},{5,133},{6,38},{7,135},{8,40}... | collective-permute-start | bytes 786440 | tf_op jit(solution)/shard_map/ppermute | solution.py:447
  52.0 1.7 %collective-permute-start.9 = (f32[64,1024]{1,0:T(8,128)S(1)}, f32[64,1024]{1,0:T(8,128)S(1)}, u32[]{:S(2)}, u32[]{:S(2)}) collective-permute-start(f32[64,1024]{1,0:T(8,128)S(1)} %get-tuple-element.57), channel_id=1, source_target_pairs={{0,16},{1,65},{2,18},{3,67},{4,20},{5,69},{6,22},{7,71},{8,24},{9,... | collective-permute-start | bytes 786440 | tf_op jit(solution)/shard_map/ppermute | solution.py:447
  54.1 4.8 %collective-permute-done.8.refs_1_ = f32[64,1024]{1,0:T(8,128)S(1)} collective-permute-done((f32[64,1024]{1,0:T(8,128)S(1)}, f32[64,1024]{1,0:T(8,128)S(1)}, u32[]{:S(2)}, u32[]{:S(2)}) %collective-permute-start.8) | collective-permute-done | bytes 262176 | tf_op jit(solution)/shard_map/ppermute | solution.py:447
  58.8 2.1 %collective-permute-done.9.refs_2_ = f32[64,1024]{1,0:T(8,128)S(1)} collective-permute-done((f32[64,1024]{1,0:T(8,128)S(1)}, f32[64,1024]{1,0:T(8,128)S(1)}, u32[]{:S(2)}, u32[]{:S(2)}) %collective-permute-start.9) | collective-permute-done | bytes 262176 | tf_op jit(solution)/shard_map/ppermute | solution.py:447
  60.9 0.6 collective-permute-done.10.refs_3_
  61.6 18.7 %all_to_all.11 = f32[8,64,128]{2,1,0:T(8,128)S(1)} all-to-all(f32[8,64,128]{2,1,0:T(8,128)S(1)} %slab_sum.1), channel_id=1, replica_groups={{0,2,4,6,8,10,12,14},{1,3,5,7,9,11,13,15},{16,18,20,22,24,26,28,30},{17..., dimensions={0} | all-to-all | bytes 524288 | tf_op jit(solution)/shard_map/all_to_all | solution.py:472
  80.3 0.6 reduce_sum.9
  (13 shorter events, 1.0 us)
Async XLA Ops:
  21.4 3.4 %collective-permute-start = (f32[256,1024]{1,0:T(8,128)S(1)}, f32[256,1024]{1,0:T(8,128)S(1)}, u32[]{:S(2)}, u32[]{:S(2)}) collective-permute-start(f32[256,1024]{1,0:T(8,128)S(1)} %get-tuple-element.33.x_own.xp), channel_id=1, source_target_pairs={{0,1},{1,0},{2,3},{3,2},{4,5},{5,4},{6,7},{7,6},{8,9},{9,8},{10,11... | collective-permute-start | bytes 3145736 | tf_op jit(solution)/shard_map/ppermute | solution.py:414
  24.4 20.6 %copy-start = (bf16[1024,2048]{1,0:T(8,128)(2,1)S(1)}, bf16[1024,2048]{1,0:T(8,128)(2,1)}, u32[]{:S(2)}) copy-start(bf16[1024,2048]{1,0:T(8,128)(2,1)} %refs_2_.1) | copy-start | bytes 12582916
  24.4 2.8 %collective-permute-start.1 = (f32[2,256,512]{2,1,0:T(8,128)S(1)}, f32[2,256,512]{2,1,0:T(8,128)S(1)}, u32[]{:S(2)}, u32[]{:S(2)}) collective-permute-start(f32[2,256,512]{2,1,0:T(8,128)S(1)} %get-tuple-element.38), channel_id=1, source_target_pairs={{0,1},{1,0},{2,3},{3,2},{4,5},{5,4},{6,7},{7,6},{8,9},{9,8},{10,11... | collective-permute-start | bytes 3145736 | tf_op jit(solution)/shard_map/ppermute | solution.py:417
  27.8 9.3 %collective-permute-start.4 = (f32[2,64,1024]{2,1,0:T(8,128)S(1)}, f32[2,64,1024]{2,1,0:T(8,128)S(1)}, u32[]{:S(2)}, u32[]{:S(2)}) collective-permute-start(f32[2,64,1024]{2,1,0:T(8,128)S(1)} %get-tuple-element.43), channel_id=1, source_target_pairs={{0,192},{1,49},{2,194},{3,51},{4,196},{5,53},{6,198},{7,55},{8,200... | collective-permute-start | bytes 1572872 | tf_op jit(solution)/shard_map/ppermute | solution.py:447
  29.0 10.5 %collective-permute-start.2 = (f32[2,64,1024]{2,1,0:T(8,128)S(1)}, f32[2,64,1024]{2,1,0:T(8,128)S(1)}, u32[]{:S(2)}, u32[]{:S(2)}) collective-permute-start(f32[2,64,1024]{2,1,0:T(8,128)S(1)} %get-tuple-element.41), channel_id=1, source_target_pairs={{0,64},{1,17},{2,66},{3,19},{4,68},{5,21},{6,70},{7,23},{8,72},{9,... | collective-permute-start | bytes 1572872 | tf_op jit(solution)/shard_map/ppermute | solution.py:447
  30.9 14.1 %collective-permute-start.6 = (f32[2,64,1024]{2,1,0:T(8,128)S(1)}, f32[2,64,1024]{2,1,0:T(8,128)S(1)}, u32[]{:S(2)}, u32[]{:S(2)}) collective-permute-start(f32[2,64,1024]{2,1,0:T(8,128)S(1)} %get-tuple-element.44), channel_id=1, source_target_pairs={{0,64},{1,17},{2,66},{3,19},{4,68},{5,21},{6,70},{7,23},{8,72},{9,... | collective-permute-start | bytes 1572872 | tf_op jit(solution)/shard_map/ppermute | solution.py:447
  31.2 13.8 %collective-permute-start.7 = (f32[2,64,1024]{2,1,0:T(8,128)S(1)}, f32[2,64,1024]{2,1,0:T(8,128)S(1)}, u32[]{:S(2)}, u32[]{:S(2)}) collective-permute-start(f32[2,64,1024]{2,1,0:T(8,128)S(1)} %get-tuple-element.45), channel_id=1, source_target_pairs={{0,192},{1,49},{2,194},{3,51},{4,196},{5,53},{6,198},{7,55},{8,200... | collective-permute-start | bytes 1572872 | tf_op jit(solution)/shard_map/ppermute | solution.py:447
  37.1 11.2 %collective-permute-start.5 = (f32[2,64,1024]{2,1,0:T(8,128)S(1)}, f32[2,64,1024]{2,1,0:T(8,128)S(1)}, u32[]{:S(2)}, u32[]{:S(2)}) collective-permute-start(f32[2,64,1024]{2,1,0:T(8,128)S(1)} %add.7), channel_id=1, source_target_pairs={{0,192},{1,49},{2,194},{3,51},{4,196},{5,53},{6,198},{7,55},{8,200... | collective-permute-start | bytes 1572872 | tf_op jit(solution)/shard_map/ppermute | solution.py:447
  39.6 11.0 %collective-permute-start.3 = (f32[2,64,1024]{2,1,0:T(8,128)S(1)}, f32[2,64,1024]{2,1,0:T(8,128)S(1)}, u32[]{:S(2)}, u32[]{:S(2)}) collective-permute-start(f32[2,64,1024]{2,1,0:T(8,128)S(1)} %add.6), channel_id=1, source_target_pairs={{0,64},{1,17},{2,66},{3,19},{4,68},{5,21},{6,70},{7,23},{8,72},{9,... | collective-permute-start | bytes 1572872 | tf_op jit(solution)/shard_map/ppermute | solution.py:447
  50.8 8.1 %collective-permute-start.8 = (f32[64,1024]{1,0:T(8,128)S(1)}, f32[64,1024]{1,0:T(8,128)S(1)}, u32[]{:S(2)}, u32[]{:S(2)}) collective-permute-start(f32[64,1024]{1,0:T(8,128)S(1)} %get-tuple-element.56), channel_id=1, source_target_pairs={{0,32},{1,129},{2,34},{3,131},{4,36},{5,133},{6,38},{7,135},{8,40}... | collective-permute-start | bytes 786440 | tf_op jit(solution)/shard_map/ppermute | solution.py:447
  52.0 8.9 %collective-permute-start.9 = (f32[64,1024]{1,0:T(8,128)S(1)}, f32[64,1024]{1,0:T(8,128)S(1)}, u32[]{:S(2)}, u32[]{:S(2)}) collective-permute-start(f32[64,1024]{1,0:T(8,128)S(1)} %get-tuple-element.57), channel_id=1, source_target_pairs={{0,16},{1,65},{2,18},{3,67},{4,20},{5,69},{6,22},{7,71},{8,24},{9,... | collective-permute-start | bytes 786440 | tf_op jit(solution)/shard_map/ppermute | solution.py:447
  53.8 7.8 %collective-permute-start.10 = (f32[64,1024]{1,0:T(8,128)S(1)}, f32[64,1024]{1,0:T(8,128)S(1)}, u32[]{:S(2)}, u32[]{:S(2)}) collective-permute-start(f32[64,1024]{1,0:T(8,128)S(1)} %get-tuple-element.58), channel_id=1, source_target_pairs={{0,48},{1,193},{2,50},{3,195},{4,52},{5,197},{6,54},{7,199},{8,56}... | collective-permute-start | bytes 786440 | tf_op jit(solution)/shard_map/ppermute | solution.py:447

commit v5 on v4

--- a/solution.py
+++ b/solution.py
@@ -41,7 +41,7 @@
 
 
 def logistic(value):
-    return 0.5 * jnp.tanh(0.5 * value) + 0.5
+    return 1.0 / (1.0 + jnp.exp(-value))
 
 
 def gates_kernel(

time: 81.1 us -> 81.2 us (level)
  no operation moved by 1% of the time
where the time goes in v5:
time: 81.2 us; the launch traced here: 81 us
  blocking collectives  33 us (41%)
  waiting for transfers between devices  20.6 us (25%)
  Pallas kernels  14.3 us (18%)
  starting transfers between devices  11.7 us (14%)
    all_to_all x1, blocking collectives, per_device(): lax.all_to_all(by_chip, 'dp', 0, 0, axis_index_groups=same_core, tiled=True)  18.7 us
    ppermute x9, waiting for transfers between devices, move(): return lax.ppermute(value, ('ctx', 'dp'), pairs_of)  18.6 us
    all_to_all x1, blocking collectives, per_device(): slabs = lax.all_to_all(summary, 'ctx', 0, 0, tiled=True)  14.3 us
    ppermute x9, starting transfers between devices, move(): return lax.ppermute(value, ('ctx', 'dp'), pairs_of)  11.2 us
    pallas_call x1, Pallas kernels, gates(): pl.pallas_call(gates_kernel, grid=(blocks,), in_specs=[full(segment_start...  6.56 us
    pallas_call x1, Pallas kernels, gradients(): pl.pallas_call(grads_kernel, grid=(model // BLOCK,), in_specs=[near] * 4,...  2.92 us
    pallas_call x1, Pallas kernels, input_gradient(): pl.pallas_call(lambda *refs: inputs_kernel(steps, *refs), grid=(model //...  2.6 us
    ppermute x1, waiting for transfers between devices, per_device(): received = lax.ppermute(sent, 'dp', swap)  1.94 us
  transfers between devices with their start and end apart: 11, of which 8 were waited for; matrix products, arithmetic and copies ran while one was open for 0% of the time, Pallas kernels for 8%

profile of v5, /device:TPU:8, one launch (start us, length us, event | category | flops | bytes accessed | tf_op | source)
XLA Modules:
  0.0 81.0 jit_solution(9609045045809297228)
XLA Ops:
  0.6 6.6 %gates.1 = (f32[16,4,1024]{2,1,0:T(4,128)S(1)}, f32[48,1024]{1,0:T(8,128)S(1)}, f32[7,256,1024]{2,1,0:T(8,128)S(1)}, f32[256,1024]{1,0:T(8,128)S(1)}) custom-call(s32[2,3]{1,0:T(2,128)} %starts.1, bf16[256,1024]{1,0:T(8,128)(2,1)} %bitcast.7, bf16[256,1024]{1,0:T(8,128)(2,1)} %bitcast.8, bf16[256,1024]{1,0:T(8,128)(2,1)} %bitcast.9, s32[2,128]{1,0:T(2,128)} %mask.1, ...), custom_call_target="tpu_custom_call" | custom-call | tf_op jit(solution)/shard_map/gates/pallas_call | solution.py:329
  7.2 14.3 %all_to_all.10.slabs = f32[16,4,1024]{2,1,0:T(4,128)S(1)} all-to-all(f32[16,4,1024]{2,1,0:T(4,128)S(1)} %get-tuple-element.31), channel_id=1, replica_groups=mesh['ctx'=16,'dp'=16] {'ctx'}, dimensions={0} | all-to-all | bytes 524288 | tf_op jit(solution)/shard_map/all_to_all | solution.py:411
  21.5 2.9 %grads.1 = (bf16[256,1024]{1,0:T(8,128)(2,1)}, bf16[2,256,1024]{2,1,0:T(8,128)(2,1)S(1)}, f32[2,256,512]{2,1,0:T(8,128)S(1)}, f32[256,1024]{1,0:T(8,128)S(1)}) custom-call(f32[16,4,1024]{2,1,0:T(4,128)S(1)} %all_to_all.10.slabs, f32[48,1024]{1,0:T(8,128)S(1)} %get-tuple-element.35.grouped, f32[7,256,1024]{2,1,0:T(8,128)S(1)} %get-tuple-element.36.middle, ...), custom_call_target="tpu_custom_call" | custom-call | tf_op jit(solution)/shard_map/grads/pallas_call | solution.py:367
  24.4 0.5 collective-permute-start.1
  24.9 0.3 turn.1.x_turned
  25.3 1.9 %collective-permute-done.1.received = f32[2,256,512]{2,1,0:T(8,128)S(1)} collective-permute-done((f32[2,256,512]{2,1,0:T(8,128)S(1)}, f32[2,256,512]{2,1,0:T(8,128)S(1)}, u32[]{:S(2)}, u32[]{:S(2)}) %collective-permute-start.1) | collective-permute-done | bytes 1048608 | tf_op jit(solution)/shard_map/ppermute | solution.py:417
  27.2 0.6 first_weights.1
  27.8 1.2 %collective-permute-start.4 = (f32[2,64,1024]{2,1,0:T(8,128)S(1)}, f32[2,64,1024]{2,1,0:T(8,128)S(1)}, u32[]{:S(2)}, u32[]{:S(2)}) collective-permute-start(f32[2,64,1024]{2,1,0:T(8,128)S(1)} %get-tuple-element.43), channel_id=1, source_target_pairs={{0,192},{1,49},{2,194},{3,51},{4,196},{5,53},{6,198},{7,55},{8,200... | collective-permute-start | bytes 1572872 | tf_op jit(solution)/shard_map/ppermute | solution.py:447
  29.0 0.9 %collective-permute-start.2 = (f32[2,64,1024]{2,1,0:T(8,128)S(1)}, f32[2,64,1024]{2,1,0:T(8,128)S(1)}, u32[]{:S(2)}, u32[]{:S(2)}) collective-permute-start(f32[2,64,1024]{2,1,0:T(8,128)S(1)} %get-tuple-element.41), channel_id=1, source_target_pairs={{0,64},{1,17},{2,66},{3,19},{4,68},{5,21},{6,70},{7,23},{8,72},{9,... | collective-permute-start | bytes 1572872 | tf_op jit(solution)/shard_map/ppermute | solution.py:447
  29.9 1.0 %more_weights.1 = (f32[2,64,1024]{2,1,0:T(8,128)S(1)}, f32[2,64,1024]{2,1,0:T(8,128)S(1)}, f32[2,64,1024]{2,1,0:T(8,128)S(1)}, f32[2,64,1024]{2,1,0:T(8,128)S(1)}, f32[4,64,1024]{2,1,0:T(8,128)S(1)}) custom-call(bf16[1024,512]{1,0:T(8,128)(2,1)S(1)} %turn.1.x_turned, bf16[512,1024]{1,0:T(8,128)(2,1)S(1)} %get-tuple-element.39.held), custom_call_target="tpu_custom_call" | custom-call | tf_op jit(solution)/shard_map/more_weights/pallas_call | solution.py:431
  31.2 3.1 %collective-permute-start.7 = (f32[2,64,1024]{2,1,0:T(8,128)S(1)}, f32[2,64,1024]{2,1,0:T(8,128)S(1)}, u32[]{:S(2)}, u32[]{:S(2)}) collective-permute-start(f32[2,64,1024]{2,1,0:T(8,128)S(1)} %get-tuple-element.45), channel_id=1, source_target_pairs={{0,192},{1,49},{2,194},{3,51},{4,196},{5,53},{6,198},{7,55},{8,200... | collective-permute-start | bytes 1572872 | tf_op jit(solution)/shard_map/ppermute | solution.py:447
  34.3 2.8 %collective-permute-done.4 = f32[2,64,1024]{2,1,0:T(8,128)S(1)} collective-permute-done((f32[2,64,1024]{2,1,0:T(8,128)S(1)}, f32[2,64,1024]{2,1,0:T(8,128)S(1)}, u32[]{:S(2)}, u32[]{:S(2)}) %collective-permute-start.4) | collective-permute-done | bytes 524320 | tf_op jit(solution)/shard_map/ppermute | solution.py:447
  37.2 2.4 %collective-permute-start.5 = (f32[2,64,1024]{2,1,0:T(8,128)S(1)}, f32[2,64,1024]{2,1,0:T(8,128)S(1)}, u32[]{:S(2)}, u32[]{:S(2)}) collective-permute-start(f32[2,64,1024]{2,1,0:T(8,128)S(1)} %add.7), channel_id=1, source_target_pairs={{0,192},{1,49},{2,194},{3,51},{4,196},{5,53},{6,198},{7,55},{8,200... | collective-permute-start | bytes 1572872 | tf_op jit(solution)/shard_map/ppermute | solution.py:447
  39.7 5.3 %collective-permute-done.6.high = f32[2,64,1024]{2,1,0:T(8,128)S(1)} collective-permute-done((f32[2,64,1024]{2,1,0:T(8,128)S(1)}, f32[2,64,1024]{2,1,0:T(8,128)S(1)}, u32[]{:S(2)}, u32[]{:S(2)}) %collective-permute-start.6) | collective-permute-done | bytes 524320 | tf_op jit(solution)/shard_map/ppermute | solution.py:447
  45.0 2.6 %inputs.1 = bf16[256,1024]{1,0:T(8,128)(2,1)} custom-call(bf16[2,256,1024]{2,1,0:T(8,128)(2,1)S(1)} %get-tuple-element.37.grads.refs_0_, f32[256,1024]{1,0:T(8,128)S(1)} %get-tuple-element.47.refs_1_, bf16[1024,2048]{1,0:T(8,128)(2,1)S(1)} %copy-done), custom_call_target="tpu_custom_call" | custom-call | flops 1073741824 | bytes 6291456 | tf_op jit(solution)/shard_map/inputs/pallas_call | solution.py:387
  47.6 0.7 collective-permute-done.5.high_more
  48.3 2.3 %collective-permute-done.3.low_more = f32[2,64,1024]{2,1,0:T(8,128)S(1)} collective-permute-done((f32[2,64,1024]{2,1,0:T(8,128)S(1)}, f32[2,64,1024]{2,1,0:T(8,128)S(1)}, u32[]{:S(2)}, u32[]{:S(2)}) %collective-permute-start.3) | collective-permute-done | bytes 524320 | tf_op jit(solution)/shard_map/ppermute | solution.py:447
  50.8 1.3 %collective-permute-start.8 = (f32[64,1024]{1,0:T(8,128)S(1)}, f32[64,1024]{1,0:T(8,128)S(1)}, u32[]{:S(2)}, u32[]{:S(2)}) collective-permute-start(f32[64,1024]{1,0:T(8,128)S(1)} %get-tuple-element.56), channel_id=1, source_target_pairs={{0,32},{1,129},{2,34},{3,131},{4,36},{5,133},{6,38},{7,135},{8,40}... | collective-permute-start | bytes 786440 | tf_op jit(solution)/shard_map/ppermute | solution.py:447
  52.1 1.8 %collective-permute-start.9 = (f32[64,1024]{1,0:T(8,128)S(1)}, f32[64,1024]{1,0:T(8,128)S(1)}, u32[]{:S(2)}, u32[]{:S(2)}) collective-permute-start(f32[64,1024]{1,0:T(8,128)S(1)} %get-tuple-element.57), channel_id=1, source_target_pairs={{0,16},{1,65},{2,18},{3,67},{4,20},{5,69},{6,22},{7,71},{8,24},{9,... | collective-permute-start | bytes 786440 | tf_op jit(solution)/shard_map/ppermute | solution.py:447
  54.1 4.8 %collective-permute-done.8.refs_1_ = f32[64,1024]{1,0:T(8,128)S(1)} collective-permute-done((f32[64,1024]{1,0:T(8,128)S(1)}, f32[64,1024]{1,0:T(8,128)S(1)}, u32[]{:S(2)}, u32[]{:S(2)}) %collective-permute-start.8) | collective-permute-done | bytes 262176 | tf_op jit(solution)/shard_map/ppermute | solution.py:447
  58.9 2.1 %collective-permute-done.9.refs_2_ = f32[64,1024]{1,0:T(8,128)S(1)} collective-permute-done((f32[64,1024]{1,0:T(8,128)S(1)}, f32[64,1024]{1,0:T(8,128)S(1)}, u32[]{:S(2)}, u32[]{:S(2)}) %collective-permute-start.9) | collective-permute-done | bytes 262176 | tf_op jit(solution)/shard_map/ppermute | solution.py:447
  61.0 0.6 collective-permute-done.10.refs_3_
  61.6 18.7 %all_to_all.11 = f32[8,64,128]{2,1,0:T(8,128)S(1)} all-to-all(f32[8,64,128]{2,1,0:T(8,128)S(1)} %slab_sum.1), channel_id=1, replica_groups={{0,2,4,6,8,10,12,14},{1,3,5,7,9,11,13,15},{16,18,20,22,24,26,28,30},{17..., dimensions={0} | all-to-all | bytes 524288 | tf_op jit(solution)/shard_map/all_to_all | solution.py:472
  80.4 0.6 reduce_sum.9
  (13 shorter events, 1.0 us)
Async XLA Ops:
  21.5 3.4 %collective-permute-start = (f32[256,1024]{1,0:T(8,128)S(1)}, f32[256,1024]{1,0:T(8,128)S(1)}, u32[]{:S(2)}, u32[]{:S(2)}) collective-permute-start(f32[256,1024]{1,0:T(8,128)S(1)} %get-tuple-element.33.x_own.xp), channel_id=1, source_target_pairs={{0,1},{1,0},{2,3},{3,2},{4,5},{5,4},{6,7},{7,6},{8,9},{9,8},{10,11... | collective-permute-start | bytes 3145736 | tf_op jit(solution)/shard_map/ppermute | solution.py:414
  24.4 20.6 %copy-start = (bf16[1024,2048]{1,0:T(8,128)(2,1)S(1)}, bf16[1024,2048]{1,0:T(8,128)(2,1)}, u32[]{:S(2)}) copy-start(bf16[1024,2048]{1,0:T(8,128)(2,1)} %refs_2_.1) | copy-start | bytes 12582916
  24.4 2.8 %collective-permute-start.1 = (f32[2,256,512]{2,1,0:T(8,128)S(1)}, f32[2,256,512]{2,1,0:T(8,128)S(1)}, u32[]{:S(2)}, u32[]{:S(2)}) collective-permute-start(f32[2,256,512]{2,1,0:T(8,128)S(1)} %get-tuple-element.38), channel_id=1, source_target_pairs={{0,1},{1,0},{2,3},{3,2},{4,5},{5,4},{6,7},{7,6},{8,9},{9,8},{10,11... | collective-permute-start | bytes 3145736 | tf_op jit(solution)/shard_map/ppermute | solution.py:417
  27.8 9.3 %collective-permute-start.4 = (f32[2,64,1024]{2,1,0:T(8,128)S(1)}, f32[2,64,1024]{2,1,0:T(8,128)S(1)}, u32[]{:S(2)}, u32[]{:S(2)}) collective-permute-start(f32[2,64,1024]{2,1,0:T(8,128)S(1)} %get-tuple-element.43), channel_id=1, source_target_pairs={{0,192},{1,49},{2,194},{3,51},{4,196},{5,53},{6,198},{7,55},{8,200... | collective-permute-start | bytes 1572872 | tf_op jit(solution)/shard_map/ppermute | solution.py:447
  29.0 10.5 %collective-permute-start.2 = (f32[2,64,1024]{2,1,0:T(8,128)S(1)}, f32[2,64,1024]{2,1,0:T(8,128)S(1)}, u32[]{:S(2)}, u32[]{:S(2)}) collective-permute-start(f32[2,64,1024]{2,1,0:T(8,128)S(1)} %get-tuple-element.41), channel_id=1, source_target_pairs={{0,64},{1,17},{2,66},{3,19},{4,68},{5,21},{6,70},{7,23},{8,72},{9,... | collective-permute-start | bytes 1572872 | tf_op jit(solution)/shard_map/ppermute | solution.py:447
  30.9 14.1 %collective-permute-start.6 = (f32[2,64,1024]{2,1,0:T(8,128)S(1)}, f32[2,64,1024]{2,1,0:T(8,128)S(1)}, u32[]{:S(2)}, u32[]{:S(2)}) collective-permute-start(f32[2,64,1024]{2,1,0:T(8,128)S(1)} %get-tuple-element.44), channel_id=1, source_target_pairs={{0,64},{1,17},{2,66},{3,19},{4,68},{5,21},{6,70},{7,23},{8,72},{9,... | collective-permute-start | bytes 1572872 | tf_op jit(solution)/shard_map/ppermute | solution.py:447
  31.2 13.8 %collective-permute-start.7 = (f32[2,64,1024]{2,1,0:T(8,128)S(1)}, f32[2,64,1024]{2,1,0:T(8,128)S(1)}, u32[]{:S(2)}, u32[]{:S(2)}) collective-permute-start(f32[2,64,1024]{2,1,0:T(8,128)S(1)} %get-tuple-element.45), channel_id=1, source_target_pairs={{0,192},{1,49},{2,194},{3,51},{4,196},{5,53},{6,198},{7,55},{8,200... | collective-permute-start | bytes 1572872 | tf_op jit(solution)/shard_map/ppermute | solution.py:447
  37.2 11.2 %collective-permute-start.5 = (f32[2,64,1024]{2,1,0:T(8,128)S(1)}, f32[2,64,1024]{2,1,0:T(8,128)S(1)}, u32[]{:S(2)}, u32[]{:S(2)}) collective-permute-start(f32[2,64,1024]{2,1,0:T(8,128)S(1)} %add.7), channel_id=1, source_target_pairs={{0,192},{1,49},{2,194},{3,51},{4,196},{5,53},{6,198},{7,55},{8,200... | collective-permute-start | bytes 1572872 | tf_op jit(solution)/shard_map/ppermute | solution.py:447
  39.6 11.0 %collective-permute-start.3 = (f32[2,64,1024]{2,1,0:T(8,128)S(1)}, f32[2,64,1024]{2,1,0:T(8,128)S(1)}, u32[]{:S(2)}, u32[]{:S(2)}) collective-permute-start(f32[2,64,1024]{2,1,0:T(8,128)S(1)} %add.6), channel_id=1, source_target_pairs={{0,64},{1,17},{2,66},{3,19},{4,68},{5,21},{6,70},{7,23},{8,72},{9,... | collective-permute-start | bytes 1572872 | tf_op jit(solution)/shard_map/ppermute | solution.py:447
  50.8 8.1 %collective-permute-start.8 = (f32[64,1024]{1,0:T(8,128)S(1)}, f32[64,1024]{1,0:T(8,128)S(1)}, u32[]{:S(2)}, u32[]{:S(2)}) collective-permute-start(f32[64,1024]{1,0:T(8,128)S(1)} %get-tuple-element.56), channel_id=1, source_target_pairs={{0,32},{1,129},{2,34},{3,131},{4,36},{5,133},{6,38},{7,135},{8,40}... | collective-permute-start | bytes 786440 | tf_op jit(solution)/shard_map/ppermute | solution.py:447
  52.1 8.9 %collective-permute-start.9 = (f32[64,1024]{1,0:T(8,128)S(1)}, f32[64,1024]{1,0:T(8,128)S(1)}, u32[]{:S(2)}, u32[]{:S(2)}) collective-permute-start(f32[64,1024]{1,0:T(8,128)S(1)} %get-tuple-element.57), channel_id=1, source_target_pairs={{0,16},{1,65},{2,18},{3,67},{4,20},{5,69},{6,22},{7,71},{8,24},{9,... | collective-permute-start | bytes 786440 | tf_op jit(solution)/shard_map/ppermute | solution.py:447
  53.8 7.7 %collective-permute-start.10 = (f32[64,1024]{1,0:T(8,128)S(1)}, f32[64,1024]{1,0:T(8,128)S(1)}, u32[]{:S(2)}, u32[]{:S(2)}) collective-permute-start(f32[64,1024]{1,0:T(8,128)S(1)} %get-tuple-element.58), channel_id=1, source_target_pairs={{0,48},{1,193},{2,50},{3,195},{4,52},{5,197},{6,54},{7,199},{8,56}... | collective-permute-start | bytes 786440 | tf_op jit(solution)/shard_map/ppermute | solution.py:447

commit v6 on v5

--- a/solution.py
+++ b/solution.py
@@ -17,6 +17,7 @@
 SIDE = 4
 WIDE = 512
 WIDTH = 512
+SPAN = 512
 UNROLL = (16, 16, 16, 16)
 PARAMS = (28, 28)
 PIECES = (8, 10, 6, 12, 4, 14, 0)
@@ -157,7 +158,6 @@
     rows = slabs.shape[1] // 2
     tokens, width = gate_grad.shape
     lanes = pl.ds(pl.multiple_of(pl.program_id(0) * width, width), width)
-    to_send = pl.ds(pl.multiple_of(pl.program_id(0) * LANES, LANES), LANES)
     steps = tokens // rows
     inner = steps // GROUPS
     me = lax.axis_index("ctx")
@@ -219,7 +219,11 @@
     other = lax.axis_index("dp") % 2 == 0
     for half, value in enumerate((gds, gis)):
         grads[half, :, lanes] = value[...].astype(BF16)
-        sent[half, :, to_send] = jnp.where(other, value[:, LANES:], value[:, :LANES])
+        for i in range(width // (2 * LANES)):
+            spot = pl.program_id(0) * (width // 2) + i * LANES
+            to_send = pl.ds(pl.multiple_of(spot, LANES), LANES)
+            low, high = pl.ds(2 * i * LANES, LANES), pl.ds((2 * i + 1) * LANES, LANES)
+            sent[half, :, to_send] = jnp.where(other, value[:, high], value[:, low])
 
 
 def turn_kernel(x_own, x_other, out):
@@ -366,16 +370,16 @@
     near = pl.BlockSpec(memory_space=pltpu.VMEM)
     return pl.pallas_call(
         grads_kernel,
-        grid=(model // BLOCK,),
+        grid=(model // SPAN,),
         in_specs=[near] * 4,
-        out_specs=[columns(tokens), near, near, near],
+        out_specs=[columns(tokens, SPAN), near, near, near],
         out_shape=[
             shaped((tokens, model), BF16),
             pltpu.VMEM((2, tokens, model), BF16),
             pltpu.VMEM((2, tokens, model // 2), F32),
             pltpu.VMEM((tokens, model), F32),
         ],
-        scratch_shapes=[pltpu.VMEM((tokens, BLOCK), F32)] * 4,
+        scratch_shapes=[pltpu.VMEM((tokens, SPAN), F32)] * 4,
         compiler_params=params(PARAMS[1]),
         name="grads",
     )(slabs, grouped, middle, xp)

time: 81.2 us -> 80.6 us (level)
  no operation moved by 1% of the time
where the time goes in v6:
time: 80.6 us; the launch traced here: 80.5 us
  blocking collectives  33 us (41%)
  waiting for transfers between devices  20.6 us (26%)
  Pallas kernels  13.7 us (17%)
  starting transfers between devices  11.7 us (15%)
    all_to_all x1, blocking collectives, per_device(): lax.all_to_all(by_chip, 'dp', 0, 0, axis_index_groups=same_core, tiled=True)  18.7 us
    ppermute x9, waiting for transfers between devices, move(): return lax.ppermute(value, ('ctx', 'dp'), pairs_of)  18.6 us
    all_to_all x1, blocking collectives, per_device(): slabs = lax.all_to_all(summary, 'ctx', 0, 0, tiled=True)  14.3 us
    ppermute x9, starting transfers between devices, move(): return lax.ppermute(value, ('ctx', 'dp'), pairs_of)  11.2 us
    pallas_call x1, Pallas kernels, gates(): pl.pallas_call(gates_kernel, grid=(blocks,), in_specs=[full(segment_start...  6.56 us
    pallas_call x1, Pallas kernels, input_gradient(): pl.pallas_call(lambda *refs: inputs_kernel(steps, *refs), grid=(model //...  2.59 us
    pallas_call x1, Pallas kernels, gradients(): pl.pallas_call(grads_kernel, grid=(model // SPAN,), in_specs=[near] * 4,...  2.36 us
    ppermute x1, waiting for transfers between devices, per_device(): received = lax.ppermute(sent, 'dp', swap)  1.94 us
  transfers between devices with their start and end apart: 11, of which 8 were waited for; matrix products, arithmetic and copies ran while one was open for 0% of the time, Pallas kernels for 8%

profile of v6, /device:TPU:8, one launch (start us, length us, event | category | flops | bytes accessed | tf_op | source)
XLA Modules:
  0.0 80.5 jit_solution(13249665772775554594)
XLA Ops:
  0.6 6.6 %gates.1 = (f32[16,4,1024]{2,1,0:T(4,128)S(1)}, f32[48,1024]{1,0:T(8,128)S(1)}, f32[7,256,1024]{2,1,0:T(8,128)S(1)}, f32[256,1024]{1,0:T(8,128)S(1)}) custom-call(s32[2,3]{1,0:T(2,128)} %starts.1, bf16[256,1024]{1,0:T(8,128)(2,1)} %bitcast.7, bf16[256,1024]{1,0:T(8,128)(2,1)} %bitcast.8, bf16[256,1024]{1,0:T(8,128)(2,1)} %bitcast.9, s32[2,128]{1,0:T(2,128)} %mask.1, ...), custom_call_target="tpu_custom_call" | custom-call | tf_op jit(solution)/shard_map/gates/pallas_call | solution.py:333
  7.2 14.3 %all_to_all.10.slabs = f32[16,4,1024]{2,1,0:T(4,128)S(1)} all-to-all(f32[16,4,1024]{2,1,0:T(4,128)S(1)} %get-tuple-element.31), channel_id=1, replica_groups=mesh['ctx'=16,'dp'=16] {'ctx'}, dimensions={0} | all-to-all | bytes 524288 | tf_op jit(solution)/shard_map/all_to_all | solution.py:415
  21.5 2.4 %grads.1 = (bf16[256,1024]{1,0:T(8,128)(2,1)}, bf16[2,256,1024]{2,1,0:T(8,128)(2,1)S(1)}, f32[2,256,512]{2,1,0:T(8,128)S(1)}, f32[256,1024]{1,0:T(8,128)S(1)}) custom-call(f32[16,4,1024]{2,1,0:T(4,128)S(1)} %all_to_all.10.slabs, f32[48,1024]{1,0:T(8,128)S(1)} %get-tuple-element.35.grouped, f32[7,256,1024]{2,1,0:T(8,128)S(1)} %get-tuple-element.36.middle, ...), custom_call_target="tpu_custom_call" | custom-call | tf_op jit(solution)/shard_map/grads/pallas_call | solution.py:371
  23.8 0.5 collective-permute-start.1
  24.3 0.3 turn.1.x_turned
  24.7 1.9 %collective-permute-done.1.received = f32[2,256,512]{2,1,0:T(8,128)S(1)} collective-permute-done((f32[2,256,512]{2,1,0:T(8,128)S(1)}, f32[2,256,512]{2,1,0:T(8,128)S(1)}, u32[]{:S(2)}, u32[]{:S(2)}) %collective-permute-start.1) | collective-permute-done | bytes 1048608 | tf_op jit(solution)/shard_map/ppermute | solution.py:421
  26.6 0.6 first_weights.1
  27.3 1.2 %collective-permute-start.4 = (f32[2,64,1024]{2,1,0:T(8,128)S(1)}, f32[2,64,1024]{2,1,0:T(8,128)S(1)}, u32[]{:S(2)}, u32[]{:S(2)}) collective-permute-start(f32[2,64,1024]{2,1,0:T(8,128)S(1)} %get-tuple-element.43), channel_id=1, source_target_pairs={{0,192},{1,49},{2,194},{3,51},{4,196},{5,53},{6,198},{7,55},{8,200... | collective-permute-start | bytes 1572872 | tf_op jit(solution)/shard_map/ppermute | solution.py:451
  28.5 0.9 %collective-permute-start.2 = (f32[2,64,1024]{2,1,0:T(8,128)S(1)}, f32[2,64,1024]{2,1,0:T(8,128)S(1)}, u32[]{:S(2)}, u32[]{:S(2)}) collective-permute-start(f32[2,64,1024]{2,1,0:T(8,128)S(1)} %get-tuple-element.41), channel_id=1, source_target_pairs={{0,64},{1,17},{2,66},{3,19},{4,68},{5,21},{6,70},{7,23},{8,72},{9,... | collective-permute-start | bytes 1572872 | tf_op jit(solution)/shard_map/ppermute | solution.py:451
  29.4 1.0 %more_weights.1 = (f32[2,64,1024]{2,1,0:T(8,128)S(1)}, f32[2,64,1024]{2,1,0:T(8,128)S(1)}, f32[2,64,1024]{2,1,0:T(8,128)S(1)}, f32[2,64,1024]{2,1,0:T(8,128)S(1)}, f32[4,64,1024]{2,1,0:T(8,128)S(1)}) custom-call(bf16[1024,512]{1,0:T(8,128)(2,1)S(1)} %turn.1.x_turned, bf16[512,1024]{1,0:T(8,128)(2,1)S(1)} %get-tuple-element.39.held), custom_call_target="tpu_custom_call" | custom-call | tf_op jit(solution)/shard_map/more_weights/pallas_call | solution.py:435
  30.6 3.0 %collective-permute-start.7 = (f32[2,64,1024]{2,1,0:T(8,128)S(1)}, f32[2,64,1024]{2,1,0:T(8,128)S(1)}, u32[]{:S(2)}, u32[]{:S(2)}) collective-permute-start(f32[2,64,1024]{2,1,0:T(8,128)S(1)} %get-tuple-element.45), channel_id=1, source_target_pairs={{0,192},{1,49},{2,194},{3,51},{4,196},{5,53},{6,198},{7,55},{8,200... | collective-permute-start | bytes 1572872 | tf_op jit(solution)/shard_map/ppermute | solution.py:451
  33.7 2.8 %collective-permute-done.4 = f32[2,64,1024]{2,1,0:T(8,128)S(1)} collective-permute-done((f32[2,64,1024]{2,1,0:T(8,128)S(1)}, f32[2,64,1024]{2,1,0:T(8,128)S(1)}, u32[]{:S(2)}, u32[]{:S(2)}) %collective-permute-start.4) | collective-permute-done | bytes 524320 | tf_op jit(solution)/shard_map/ppermute | solution.py:451
  36.6 2.4 %collective-permute-start.5 = (f32[2,64,1024]{2,1,0:T(8,128)S(1)}, f32[2,64,1024]{2,1,0:T(8,128)S(1)}, u32[]{:S(2)}, u32[]{:S(2)}) collective-permute-start(f32[2,64,1024]{2,1,0:T(8,128)S(1)} %add.7), channel_id=1, source_target_pairs={{0,192},{1,49},{2,194},{3,51},{4,196},{5,53},{6,198},{7,55},{8,200... | collective-permute-start | bytes 1572872 | tf_op jit(solution)/shard_map/ppermute | solution.py:451
  39.2 5.3 %collective-permute-done.6.high = f32[2,64,1024]{2,1,0:T(8,128)S(1)} collective-permute-done((f32[2,64,1024]{2,1,0:T(8,128)S(1)}, f32[2,64,1024]{2,1,0:T(8,128)S(1)}, u32[]{:S(2)}, u32[]{:S(2)}) %collective-permute-start.6) | collective-permute-done | bytes 524320 | tf_op jit(solution)/shard_map/ppermute | solution.py:451
  44.5 2.6 %inputs.1 = bf16[256,1024]{1,0:T(8,128)(2,1)} custom-call(bf16[2,256,1024]{2,1,0:T(8,128)(2,1)S(1)} %get-tuple-element.37.grads.refs_0_, f32[256,1024]{1,0:T(8,128)S(1)} %get-tuple-element.47.refs_1_, bf16[1024,2048]{1,0:T(8,128)(2,1)S(1)} %copy-done), custom_call_target="tpu_custom_call" | custom-call | flops 1073741824 | bytes 6291456 | tf_op jit(solution)/shard_map/inputs/pallas_call | solution.py:391
  47.1 0.7 collective-permute-done.5.high_more
  47.8 2.3 %collective-permute-done.3.low_more = f32[2,64,1024]{2,1,0:T(8,128)S(1)} collective-permute-done((f32[2,64,1024]{2,1,0:T(8,128)S(1)}, f32[2,64,1024]{2,1,0:T(8,128)S(1)}, u32[]{:S(2)}, u32[]{:S(2)}) %collective-permute-start.3) | collective-permute-done | bytes 524320 | tf_op jit(solution)/shard_map/ppermute | solution.py:451
  50.2 1.3 %collective-permute-start.8 = (f32[64,1024]{1,0:T(8,128)S(1)}, f32[64,1024]{1,0:T(8,128)S(1)}, u32[]{:S(2)}, u32[]{:S(2)}) collective-permute-start(f32[64,1024]{1,0:T(8,128)S(1)} %get-tuple-element.56), channel_id=1, source_target_pairs={{0,32},{1,129},{2,34},{3,131},{4,36},{5,133},{6,38},{7,135},{8,40}... | collective-permute-start | bytes 786440 | tf_op jit(solution)/shard_map/ppermute | solution.py:451
  51.5 1.8 %collective-permute-start.9 = (f32[64,1024]{1,0:T(8,128)S(1)}, f32[64,1024]{1,0:T(8,128)S(1)}, u32[]{:S(2)}, u32[]{:S(2)}) collective-permute-start(f32[64,1024]{1,0:T(8,128)S(1)} %get-tuple-element.57), channel_id=1, source_target_pairs={{0,16},{1,65},{2,18},{3,67},{4,20},{5,69},{6,22},{7,71},{8,24},{9,... | collective-permute-start | bytes 786440 | tf_op jit(solution)/shard_map/ppermute | solution.py:451
  53.5 4.8 %collective-permute-done.8.refs_1_ = f32[64,1024]{1,0:T(8,128)S(1)} collective-permute-done((f32[64,1024]{1,0:T(8,128)S(1)}, f32[64,1024]{1,0:T(8,128)S(1)}, u32[]{:S(2)}, u32[]{:S(2)}) %collective-permute-start.8) | collective-permute-done | bytes 262176 | tf_op jit(solution)/shard_map/ppermute | solution.py:451
  58.3 2.1 %collective-permute-done.9.refs_2_ = f32[64,1024]{1,0:T(8,128)S(1)} collective-permute-done((f32[64,1024]{1,0:T(8,128)S(1)}, f32[64,1024]{1,0:T(8,128)S(1)}, u32[]{:S(2)}, u32[]{:S(2)}) %collective-permute-start.9) | collective-permute-done | bytes 262176 | tf_op jit(solution)/shard_map/ppermute | solution.py:451
  60.4 0.6 collective-permute-done.10.refs_3_
  61.1 18.7 %all_to_all.11 = f32[8,64,128]{2,1,0:T(8,128)S(1)} all-to-all(f32[8,64,128]{2,1,0:T(8,128)S(1)} %slab_sum.1), channel_id=1, replica_groups={{0,2,4,6,8,10,12,14},{1,3,5,7,9,11,13,15},{16,18,20,22,24,26,28,30},{17..., dimensions={0} | all-to-all | bytes 524288 | tf_op jit(solution)/shard_map/all_to_all | solution.py:476
  79.8 0.6 reduce_sum.9
  (13 shorter events, 1.0 us)
Async XLA Ops:
  21.5 2.9 %collective-permute-start = (f32[256,1024]{1,0:T(8,128)S(1)}, f32[256,1024]{1,0:T(8,128)S(1)}, u32[]{:S(2)}, u32[]{:S(2)}) collective-permute-start(f32[256,1024]{1,0:T(8,128)S(1)} %get-tuple-element.33.x_own.xp), channel_id=1, source_target_pairs={{0,1},{1,0},{2,3},{3,2},{4,5},{5,4},{6,7},{7,6},{8,9},{9,8},{10,11... | collective-permute-start | bytes 3145736 | tf_op jit(solution)/shard_map/ppermute | solution.py:418
  23.8 20.6 %copy-start = (bf16[1024,2048]{1,0:T(8,128)(2,1)S(1)}, bf16[1024,2048]{1,0:T(8,128)(2,1)}, u32[]{:S(2)}) copy-start(bf16[1024,2048]{1,0:T(8,128)(2,1)} %refs_2_.1) | copy-start | bytes 12582916
  23.8 2.8 %collective-permute-start.1 = (f32[2,256,512]{2,1,0:T(8,128)S(1)}, f32[2,256,512]{2,1,0:T(8,128)S(1)}, u32[]{:S(2)}, u32[]{:S(2)}) collective-permute-start(f32[2,256,512]{2,1,0:T(8,128)S(1)} %get-tuple-element.38), channel_id=1, source_target_pairs={{0,1},{1,0},{2,3},{3,2},{4,5},{5,4},{6,7},{7,6},{8,9},{9,8},{10,11... | collective-permute-start | bytes 3145736 | tf_op jit(solution)/shard_map/ppermute | solution.py:421
  27.3 9.3 %collective-permute-start.4 = (f32[2,64,1024]{2,1,0:T(8,128)S(1)}, f32[2,64,1024]{2,1,0:T(8,128)S(1)}, u32[]{:S(2)}, u32[]{:S(2)}) collective-permute-start(f32[2,64,1024]{2,1,0:T(8,128)S(1)} %get-tuple-element.43), channel_id=1, source_target_pairs={{0,192},{1,49},{2,194},{3,51},{4,196},{5,53},{6,198},{7,55},{8,200... | collective-permute-start | bytes 1572872 | tf_op jit(solution)/shard_map/ppermute | solution.py:451
  28.5 10.5 %collective-permute-start.2 = (f32[2,64,1024]{2,1,0:T(8,128)S(1)}, f32[2,64,1024]{2,1,0:T(8,128)S(1)}, u32[]{:S(2)}, u32[]{:S(2)}) collective-permute-start(f32[2,64,1024]{2,1,0:T(8,128)S(1)} %get-tuple-element.41), channel_id=1, source_target_pairs={{0,64},{1,17},{2,66},{3,19},{4,68},{5,21},{6,70},{7,23},{8,72},{9,... | collective-permute-start | bytes 1572872 | tf_op jit(solution)/shard_map/ppermute | solution.py:451
  30.4 14.1 %collective-permute-start.6 = (f32[2,64,1024]{2,1,0:T(8,128)S(1)}, f32[2,64,1024]{2,1,0:T(8,128)S(1)}, u32[]{:S(2)}, u32[]{:S(2)}) collective-permute-start(f32[2,64,1024]{2,1,0:T(8,128)S(1)} %get-tuple-element.44), channel_id=1, source_target_pairs={{0,64},{1,17},{2,66},{3,19},{4,68},{5,21},{6,70},{7,23},{8,72},{9,... | collective-permute-start | bytes 1572872 | tf_op jit(solution)/shard_map/ppermute | solution.py:451
  30.6 13.8 %collective-permute-start.7 = (f32[2,64,1024]{2,1,0:T(8,128)S(1)}, f32[2,64,1024]{2,1,0:T(8,128)S(1)}, u32[]{:S(2)}, u32[]{:S(2)}) collective-permute-start(f32[2,64,1024]{2,1,0:T(8,128)S(1)} %get-tuple-element.45), channel_id=1, source_target_pairs={{0,192},{1,49},{2,194},{3,51},{4,196},{5,53},{6,198},{7,55},{8,200... | collective-permute-start | bytes 1572872 | tf_op jit(solution)/shard_map/ppermute | solution.py:451
  36.6 11.2 %collective-permute-start.5 = (f32[2,64,1024]{2,1,0:T(8,128)S(1)}, f32[2,64,1024]{2,1,0:T(8,128)S(1)}, u32[]{:S(2)}, u32[]{:S(2)}) collective-permute-start(f32[2,64,1024]{2,1,0:T(8,128)S(1)} %add.7), channel_id=1, source_target_pairs={{0,192},{1,49},{2,194},{3,51},{4,196},{5,53},{6,198},{7,55},{8,200... | collective-permute-start | bytes 1572872 | tf_op jit(solution)/shard_map/ppermute | solution.py:451
  39.1 11.0 %collective-permute-start.3 = (f32[2,64,1024]{2,1,0:T(8,128)S(1)}, f32[2,64,1024]{2,1,0:T(8,128)S(1)}, u32[]{:S(2)}, u32[]{:S(2)}) collective-permute-start(f32[2,64,1024]{2,1,0:T(8,128)S(1)} %add.6), channel_id=1, source_target_pairs={{0,64},{1,17},{2,66},{3,19},{4,68},{5,21},{6,70},{7,23},{8,72},{9,... | collective-permute-start | bytes 1572872 | tf_op jit(solution)/shard_map/ppermute | solution.py:451
  50.2 8.1 %collective-permute-start.8 = (f32[64,1024]{1,0:T(8,128)S(1)}, f32[64,1024]{1,0:T(8,128)S(1)}, u32[]{:S(2)}, u32[]{:S(2)}) collective-permute-start(f32[64,1024]{1,0:T(8,128)S(1)} %get-tuple-element.56), channel_id=1, source_target_pairs={{0,32},{1,129},{2,34},{3,131},{4,36},{5,133},{6,38},{7,135},{8,40}... | collective-permute-start | bytes 786440 | tf_op jit(solution)/shard_map/ppermute | solution.py:451
  51.5 8.9 %collective-permute-start.9 = (f32[64,1024]{1,0:T(8,128)S(1)}, f32[64,1024]{1,0:T(8,128)S(1)}, u32[]{:S(2)}, u32[]{:S(2)}) collective-permute-start(f32[64,1024]{1,0:T(8,128)S(1)} %get-tuple-element.57), channel_id=1, source_target_pairs={{0,16},{1,65},{2,18},{3,67},{4,20},{5,69},{6,22},{7,71},{8,24},{9,... | collective-permute-start | bytes 786440 | tf_op jit(solution)/shard_map/ppermute | solution.py:451
  53.3 7.8 %collective-permute-start.10 = (f32[64,1024]{1,0:T(8,128)S(1)}, f32[64,1024]{1,0:T(8,128)S(1)}, u32[]{:S(2)}, u32[]{:S(2)}) collective-permute-start(f32[64,1024]{1,0:T(8,128)S(1)} %get-tuple-element.58), channel_id=1, source_target_pairs={{0,48},{1,193},{2,50},{3,195},{4,52},{5,197},{6,54},{7,199},{8,56}... | collective-permute-start | bytes 786440 | tf_op jit(solution)/shard_map/ppermute | solution.py:451

commit v7 on v6

--- a/solution.py
+++ b/solution.py
@@ -226,7 +226,7 @@
             sent[half, :, to_send] = jnp.where(other, value[:, high], value[:, low])
 
 
-def turn_kernel(x_own, x_other, out):
+def turn_kernel(x_own, x_other, grads, out, held):
     tokens, model = x_own.shape
     part = model // (SIDE * SIDE)
     core = lax.axis_index("dp") % 2
@@ -239,18 +239,6 @@
                 block = jnp.where(core == 0, dx * SIDE + dy, dy * SIDE + dx)
                 to = pl.ds(pl.multiple_of(block * part, part), part)
                 out[to, pl.ds(s * tokens, tokens)] = turned[by * part : (by + 1) * part]
-
-
-def pieces(x_turned, held, outs, starts):
-    part = outs[0].shape[1]
-    for out, start in zip(outs, starts):
-        value = dot(x_turned[pl.ds(start * part, out.shape[0] * part), :], held[...])
-        out[...] = value.reshape(out.shape)
-
-
-def first_weights_kernel(x_turned, grads, received, held, *outs):
-    tokens = grads.shape[1]
-    core = lax.axis_index("dp") % 2
     parts = grads.shape[2] // (2 * LANES)
     for half in range(2):
         for z in range(parts):
@@ -261,6 +249,21 @@
                 grads[half, :, pl.ds((2 * z + 1) * LANES, LANES)].astype(F32),
             )
             held[pl.ds(0, tokens), to] = own.astype(BF16)
+
+
+def pieces(x_turned, held, outs, starts):
+    part = outs[0].shape[1]
+    for out, start in zip(outs, starts):
+        value = dot(x_turned[pl.ds(start * part, out.shape[0] * part), :], held[...])
+        out[...] = value.reshape(out.shape)
+
+
+def first_weights_kernel(x_turned, received, held_own, held, *outs):
+    tokens = received.shape[1]
+    parts = received.shape[2] // LANES
+    for half in range(2):
+        for z in range(parts):
+            to = pl.ds((half * parts + z) * LANES, LANES)
             held[pl.ds(tokens, tokens), to] = received[
                 half, :, pl.ds(z * LANES, LANES)
             ].astype(BF16)
@@ -419,19 +422,20 @@
     part = model // peers
     gate_grad, grads, sent, direct = gradients(slabs, grouped, middle, xp)
     received = lax.ppermute(sent, "dp", swap)
-    x_turned = pl.pallas_call(
+    x_turned, held = pl.pallas_call(
         turn_kernel,
-        out_shape=shaped((model, 2 * tokens), BF16),
+        out_shape=[shaped((model, 2 * tokens), BF16), shaped((2 * tokens, model), BF16)],
         compiler_params=params(8),
         name="turn",
-    )(xp, x_other)
+    )(xp, x_other, grads)
     piece = shaped((2, part, model))
     held, on2, back2 = pl.pallas_call(
         first_weights_kernel,
         out_shape=[shaped((2 * tokens, model), BF16), piece, piece],
         compiler_params=params(12),
+        input_output_aliases={2: 0},
         name="first_weights",
-    )(x_turned, grads, received)
+    )(x_turned, received, held)
     on1, back1, on_last, back_last, stay = pl.pallas_call(
         more_weights_kernel,
         out_shape=[piece] * 4 + [shaped((SIDE, part, model))],

time: 80.6 us -> 80.4 us (level)
  no operation moved by 1% of the time
where the time goes in v7:
time: 80.4 us; the launch traced here: 80.3 us
  blocking collectives  33 us (41%)
  waiting for transfers between devices  20.4 us (25%)
  Pallas kernels  13.8 us (17%)
  starting transfers between devices  11.7 us (15%)
    all_to_all x1, blocking collectives, per_device(): lax.all_to_all(by_chip, 'dp', 0, 0, axis_index_groups=same_core, tiled=True)  18.7 us
    ppermute x9, waiting for transfers between devices, move(): return lax.ppermute(value, ('ctx', 'dp'), pairs_of)  18.6 us
    all_to_all x1, blocking collectives, per_device(): slabs = lax.all_to_all(summary, 'ctx', 0, 0, tiled=True)  14.3 us
    ppermute x9, starting transfers between devices, move(): return lax.ppermute(value, ('ctx', 'dp'), pairs_of)  11.2 us
    pallas_call x1, Pallas kernels, gates(): pl.pallas_call(gates_kernel, grid=(blocks,), in_specs=[full(segment_start...  6.56 us
    pallas_call x1, Pallas kernels, input_gradient(): pl.pallas_call(lambda *refs: inputs_kernel(steps, *refs), grid=(model //...  2.6 us
    pallas_call x1, Pallas kernels, gradients(): pl.pallas_call(grads_kernel, grid=(model // SPAN,), in_specs=[near] * 4,...  2.36 us
    ppermute x1, waiting for transfers between devices, per_device(): received = lax.ppermute(sent, 'dp', swap)  1.71 us
  transfers between devices with their start and end apart: 11, of which 8 were waited for; matrix products, arithmetic and copies ran while one was open for 0% of the time, Pallas kernels for 8%

profile of v7, /device:TPU:8, one launch (start us, length us, event | category | flops | bytes accessed | tf_op | source)
XLA Modules:
  0.0 80.3 jit_solution(6538074354773427348)
XLA Ops:
  0.6 6.6 %gates.1 = (f32[16,4,1024]{2,1,0:T(4,128)S(1)}, f32[48,1024]{1,0:T(8,128)S(1)}, f32[7,256,1024]{2,1,0:T(8,128)S(1)}, f32[256,1024]{1,0:T(8,128)S(1)}) custom-call(s32[2,3]{1,0:T(2,128)} %starts.1, bf16[256,1024]{1,0:T(8,128)(2,1)} %bitcast.7, bf16[256,1024]{1,0:T(8,128)(2,1)} %bitcast.8, bf16[256,1024]{1,0:T(8,128)(2,1)} %bitcast.9, s32[2,128]{1,0:T(2,128)} %mask.1, ...), custom_call_target="tpu_custom_call" | custom-call | tf_op jit(solution)/shard_map/gates/pallas_call | solution.py:336
  7.2 14.3 %all_to_all.10.slabs = f32[16,4,1024]{2,1,0:T(4,128)S(1)} all-to-all(f32[16,4,1024]{2,1,0:T(4,128)S(1)} %get-tuple-element.33), channel_id=1, replica_groups=mesh['ctx'=16,'dp'=16] {'ctx'}, dimensions={0} | all-to-all | bytes 524288 | tf_op jit(solution)/shard_map/all_to_all | solution.py:418
  21.5 2.4 %grads.1 = (bf16[256,1024]{1,0:T(8,128)(2,1)}, bf16[2,256,1024]{2,1,0:T(8,128)(2,1)S(1)}, f32[2,256,512]{2,1,0:T(8,128)S(1)}, f32[256,1024]{1,0:T(8,128)S(1)}) custom-call(f32[16,4,1024]{2,1,0:T(4,128)S(1)} %all_to_all.10.slabs, f32[48,1024]{1,0:T(8,128)S(1)} %get-tuple-element.37.grouped, f32[7,256,1024]{2,1,0:T(8,128)S(1)} %get-tuple-element.38.middle, ...), custom_call_target="tpu_custom_call" | custom-call | tf_op jit(solution)/shard_map/grads/pallas_call | solution.py:374
  23.8 0.5 collective-permute-start.1
  24.3 0.6 turn.1
  24.9 1.7 %collective-permute-done.1.received = f32[2,256,512]{2,1,0:T(8,128)S(1)} collective-permute-done((f32[2,256,512]{2,1,0:T(8,128)S(1)}, f32[2,256,512]{2,1,0:T(8,128)S(1)}, u32[]{:S(2)}, u32[]{:S(2)}) %collective-permute-start.1) | collective-permute-done | bytes 1048608 | tf_op jit(solution)/shard_map/ppermute | solution.py:424
  26.6 0.5 first_weights.1
  27.1 1.2 %collective-permute-start.4 = (f32[2,64,1024]{2,1,0:T(8,128)S(1)}, f32[2,64,1024]{2,1,0:T(8,128)S(1)}, u32[]{:S(2)}, u32[]{:S(2)}) collective-permute-start(f32[2,64,1024]{2,1,0:T(8,128)S(1)} %get-tuple-element.47), channel_id=1, source_target_pairs={{0,192},{1,49},{2,194},{3,51},{4,196},{5,53},{6,198},{7,55},{8,200... | collective-permute-start | bytes 1572872 | tf_op jit(solution)/shard_map/ppermute | solution.py:455
  28.3 0.9 %collective-permute-start.2 = (f32[2,64,1024]{2,1,0:T(8,128)S(1)}, f32[2,64,1024]{2,1,0:T(8,128)S(1)}, u32[]{:S(2)}, u32[]{:S(2)}) collective-permute-start(f32[2,64,1024]{2,1,0:T(8,128)S(1)} %get-tuple-element.45), channel_id=1, source_target_pairs={{0,64},{1,17},{2,66},{3,19},{4,68},{5,21},{6,70},{7,23},{8,72},{9,... | collective-permute-start | bytes 1572872 | tf_op jit(solution)/shard_map/ppermute | solution.py:455
  29.2 1.0 %more_weights.1 = (f32[2,64,1024]{2,1,0:T(8,128)S(1)}, f32[2,64,1024]{2,1,0:T(8,128)S(1)}, f32[2,64,1024]{2,1,0:T(8,128)S(1)}, f32[2,64,1024]{2,1,0:T(8,128)S(1)}, f32[4,64,1024]{2,1,0:T(8,128)S(1)}) custom-call(bf16[1024,512]{1,0:T(8,128)(2,1)S(1)} %get-tuple-element.40.x_turned, bf16[512,1024]{1,0:T(8,128)(2,1)S(1)} %get-tuple-element.43.held), custom_call_target="tpu_custom_call" | custom-call | tf_op jit(solution)/shard_map/more_weights/pallas_call | solution.py:439
  30.5 3.0 %collective-permute-start.7 = (f32[2,64,1024]{2,1,0:T(8,128)S(1)}, f32[2,64,1024]{2,1,0:T(8,128)S(1)}, u32[]{:S(2)}, u32[]{:S(2)}) collective-permute-start(f32[2,64,1024]{2,1,0:T(8,128)S(1)} %get-tuple-element.49), channel_id=1, source_target_pairs={{0,192},{1,49},{2,194},{3,51},{4,196},{5,53},{6,198},{7,55},{8,200... | collective-permute-start | bytes 1572872 | tf_op jit(solution)/shard_map/ppermute | solution.py:455
  33.5 2.8 %collective-permute-done.4 = f32[2,64,1024]{2,1,0:T(8,128)S(1)} collective-permute-done((f32[2,64,1024]{2,1,0:T(8,128)S(1)}, f32[2,64,1024]{2,1,0:T(8,128)S(1)}, u32[]{:S(2)}, u32[]{:S(2)}) %collective-permute-start.4) | collective-permute-done | bytes 524320 | tf_op jit(solution)/shard_map/ppermute | solution.py:455
  36.4 2.4 %collective-permute-start.5 = (f32[2,64,1024]{2,1,0:T(8,128)S(1)}, f32[2,64,1024]{2,1,0:T(8,128)S(1)}, u32[]{:S(2)}, u32[]{:S(2)}) collective-permute-start(f32[2,64,1024]{2,1,0:T(8,128)S(1)} %add.7), channel_id=1, source_target_pairs={{0,192},{1,49},{2,194},{3,51},{4,196},{5,53},{6,198},{7,55},{8,200... | collective-permute-start | bytes 1572872 | tf_op jit(solution)/shard_map/ppermute | solution.py:455
  39.0 5.3 %collective-permute-done.6.high = f32[2,64,1024]{2,1,0:T(8,128)S(1)} collective-permute-done((f32[2,64,1024]{2,1,0:T(8,128)S(1)}, f32[2,64,1024]{2,1,0:T(8,128)S(1)}, u32[]{:S(2)}, u32[]{:S(2)}) %collective-permute-start.6) | collective-permute-done | bytes 524320 | tf_op jit(solution)/shard_map/ppermute | solution.py:455
  44.3 2.6 %inputs.1 = bf16[256,1024]{1,0:T(8,128)(2,1)} custom-call(bf16[2,256,1024]{2,1,0:T(8,128)(2,1)S(1)} %get-tuple-element.39.grads.refs_0_, f32[256,1024]{1,0:T(8,128)S(1)} %get-tuple-element.51.refs_1_, bf16[1024,2048]{1,0:T(8,128)(2,1)S(1)} %copy-done), custom_call_target="tpu_custom_call" | custom-call | flops 1073741824 | bytes 6291456 | tf_op jit(solution)/shard_map/inputs/pallas_call | solution.py:394
  46.9 0.7 collective-permute-done.5.high_more
  47.6 2.3 %collective-permute-done.3.low_more = f32[2,64,1024]{2,1,0:T(8,128)S(1)} collective-permute-done((f32[2,64,1024]{2,1,0:T(8,128)S(1)}, f32[2,64,1024]{2,1,0:T(8,128)S(1)}, u32[]{:S(2)}, u32[]{:S(2)}) %collective-permute-start.3) | collective-permute-done | bytes 524320 | tf_op jit(solution)/shard_map/ppermute | solution.py:455
  50.1 1.3 %collective-permute-start.8 = (f32[64,1024]{1,0:T(8,128)S(1)}, f32[64,1024]{1,0:T(8,128)S(1)}, u32[]{:S(2)}, u32[]{:S(2)}) collective-permute-start(f32[64,1024]{1,0:T(8,128)S(1)} %get-tuple-element.60), channel_id=1, source_target_pairs={{0,32},{1,129},{2,34},{3,131},{4,36},{5,133},{6,38},{7,135},{8,40}... | collective-permute-start | bytes 786440 | tf_op jit(solution)/shard_map/ppermute | solution.py:455
  51.3 1.8 %collective-permute-start.9 = (f32[64,1024]{1,0:T(8,128)S(1)}, f32[64,1024]{1,0:T(8,128)S(1)}, u32[]{:S(2)}, u32[]{:S(2)}) collective-permute-start(f32[64,1024]{1,0:T(8,128)S(1)} %get-tuple-element.61), channel_id=1, source_target_pairs={{0,16},{1,65},{2,18},{3,67},{4,20},{5,69},{6,22},{7,71},{8,24},{9,... | collective-permute-start | bytes 786440 | tf_op jit(solution)/shard_map/ppermute | solution.py:455
  53.3 4.8 %collective-permute-done.8.refs_1_ = f32[64,1024]{1,0:T(8,128)S(1)} collective-permute-done((f32[64,1024]{1,0:T(8,128)S(1)}, f32[64,1024]{1,0:T(8,128)S(1)}, u32[]{:S(2)}, u32[]{:S(2)}) %collective-permute-start.8) | collective-permute-done | bytes 262176 | tf_op jit(solution)/shard_map/ppermute | solution.py:455
  58.1 2.1 %collective-permute-done.9.refs_2_ = f32[64,1024]{1,0:T(8,128)S(1)} collective-permute-done((f32[64,1024]{1,0:T(8,128)S(1)}, f32[64,1024]{1,0:T(8,128)S(1)}, u32[]{:S(2)}, u32[]{:S(2)}) %collective-permute-start.9) | collective-permute-done | bytes 262176 | tf_op jit(solution)/shard_map/ppermute | solution.py:455
  60.2 0.6 collective-permute-done.10.refs_3_
  60.9 18.7 %all_to_all.11 = f32[8,64,128]{2,1,0:T(8,128)S(1)} all-to-all(f32[8,64,128]{2,1,0:T(8,128)S(1)} %slab_sum.1), channel_id=1, replica_groups={{0,2,4,6,8,10,12,14},{1,3,5,7,9,11,13,15},{16,18,20,22,24,26,28,30},{17..., dimensions={0} | all-to-all | bytes 524288 | tf_op jit(solution)/shard_map/all_to_all | solution.py:480
  79.6 0.6 reduce_sum.9
  (13 shorter events, 1.0 us)
Async XLA Ops:
  21.5 2.9 %collective-permute-start = (f32[256,1024]{1,0:T(8,128)S(1)}, f32[256,1024]{1,0:T(8,128)S(1)}, u32[]{:S(2)}, u32[]{:S(2)}) collective-permute-start(f32[256,1024]{1,0:T(8,128)S(1)} %get-tuple-element.35.xp.x_own), channel_id=1, source_target_pairs={{0,1},{1,0},{2,3},{3,2},{4,5},{5,4},{6,7},{7,6},{8,9},{9,8},{10,11... | collective-permute-start | bytes 3145736 | tf_op jit(solution)/shard_map/ppermute | solution.py:421
  23.8 20.5 %copy-start = (bf16[1024,2048]{1,0:T(8,128)(2,1)S(1)}, bf16[1024,2048]{1,0:T(8,128)(2,1)}, u32[]{:S(2)}) copy-start(bf16[1024,2048]{1,0:T(8,128)(2,1)} %refs_2_.1) | copy-start | bytes 12582916
  23.8 2.8 %collective-permute-start.1 = (f32[2,256,512]{2,1,0:T(8,128)S(1)}, f32[2,256,512]{2,1,0:T(8,128)S(1)}, u32[]{:S(2)}, u32[]{:S(2)}) collective-permute-start(f32[2,256,512]{2,1,0:T(8,128)S(1)} %get-tuple-element.41), channel_id=1, source_target_pairs={{0,1},{1,0},{2,3},{3,2},{4,5},{5,4},{6,7},{7,6},{8,9},{9,8},{10,11... | collective-permute-start | bytes 3145736 | tf_op jit(solution)/shard_map/ppermute | solution.py:424
  27.1 9.3 %collective-permute-start.4 = (f32[2,64,1024]{2,1,0:T(8,128)S(1)}, f32[2,64,1024]{2,1,0:T(8,128)S(1)}, u32[]{:S(2)}, u32[]{:S(2)}) collective-permute-start(f32[2,64,1024]{2,1,0:T(8,128)S(1)} %get-tuple-element.47), channel_id=1, source_target_pairs={{0,192},{1,49},{2,194},{3,51},{4,196},{5,53},{6,198},{7,55},{8,200... | collective-permute-start | bytes 1572872 | tf_op jit(solution)/shard_map/ppermute | solution.py:455
  28.3 10.5 %collective-permute-start.2 = (f32[2,64,1024]{2,1,0:T(8,128)S(1)}, f32[2,64,1024]{2,1,0:T(8,128)S(1)}, u32[]{:S(2)}, u32[]{:S(2)}) collective-permute-start(f32[2,64,1024]{2,1,0:T(8,128)S(1)} %get-tuple-element.45), channel_id=1, source_target_pairs={{0,64},{1,17},{2,66},{3,19},{4,68},{5,21},{6,70},{7,23},{8,72},{9,... | collective-permute-start | bytes 1572872 | tf_op jit(solution)/shard_map/ppermute | solution.py:455
  30.2 14.1 %collective-permute-start.6 = (f32[2,64,1024]{2,1,0:T(8,128)S(1)}, f32[2,64,1024]{2,1,0:T(8,128)S(1)}, u32[]{:S(2)}, u32[]{:S(2)}) collective-permute-start(f32[2,64,1024]{2,1,0:T(8,128)S(1)} %get-tuple-element.48), channel_id=1, source_target_pairs={{0,64},{1,17},{2,66},{3,19},{4,68},{5,21},{6,70},{7,23},{8,72},{9,... | collective-permute-start | bytes 1572872 | tf_op jit(solution)/shard_map/ppermute | solution.py:455
  30.5 13.8 %collective-permute-start.7 = (f32[2,64,1024]{2,1,0:T(8,128)S(1)}, f32[2,64,1024]{2,1,0:T(8,128)S(1)}, u32[]{:S(2)}, u32[]{:S(2)}) collective-permute-start(f32[2,64,1024]{2,1,0:T(8,128)S(1)} %get-tuple-element.49), channel_id=1, source_target_pairs={{0,192},{1,49},{2,194},{3,51},{4,196},{5,53},{6,198},{7,55},{8,200... | collective-permute-start | bytes 1572872 | tf_op jit(solution)/shard_map/ppermute | solution.py:455
  36.4 11.2 %collective-permute-start.5 = (f32[2,64,1024]{2,1,0:T(8,128)S(1)}, f32[2,64,1024]{2,1,0:T(8,128)S(1)}, u32[]{:S(2)}, u32[]{:S(2)}) collective-permute-start(f32[2,64,1024]{2,1,0:T(8,128)S(1)} %add.7), channel_id=1, source_target_pairs={{0,192},{1,49},{2,194},{3,51},{4,196},{5,53},{6,198},{7,55},{8,200... | collective-permute-start | bytes 1572872 | tf_op jit(solution)/shard_map/ppermute | solution.py:455
  38.9 11.0 %collective-permute-start.3 = (f32[2,64,1024]{2,1,0:T(8,128)S(1)}, f32[2,64,1024]{2,1,0:T(8,128)S(1)}, u32[]{:S(2)}, u32[]{:S(2)}) collective-permute-start(f32[2,64,1024]{2,1,0:T(8,128)S(1)} %add.6), channel_id=1, source_target_pairs={{0,64},{1,17},{2,66},{3,19},{4,68},{5,21},{6,70},{7,23},{8,72},{9,... | collective-permute-start | bytes 1572872 | tf_op jit(solution)/shard_map/ppermute | solution.py:455
  50.1 8.1 %collective-permute-start.8 = (f32[64,1024]{1,0:T(8,128)S(1)}, f32[64,1024]{1,0:T(8,128)S(1)}, u32[]{:S(2)}, u32[]{:S(2)}) collective-permute-start(f32[64,1024]{1,0:T(8,128)S(1)} %get-tuple-element.60), channel_id=1, source_target_pairs={{0,32},{1,129},{2,34},{3,131},{4,36},{5,133},{6,38},{7,135},{8,40}... | collective-permute-start | bytes 786440 | tf_op jit(solution)/shard_map/ppermute | solution.py:455
  51.3 8.9 %collective-permute-start.9 = (f32[64,1024]{1,0:T(8,128)S(1)}, f32[64,1024]{1,0:T(8,128)S(1)}, u32[]{:S(2)}, u32[]{:S(2)}) collective-permute-start(f32[64,1024]{1,0:T(8,128)S(1)} %get-tuple-element.61), channel_id=1, source_target_pairs={{0,16},{1,65},{2,18},{3,67},{4,20},{5,69},{6,22},{7,71},{8,24},{9,... | collective-permute-start | bytes 786440 | tf_op jit(solution)/shard_map/ppermute | solution.py:455
  53.1 7.8 %collective-permute-start.10 = (f32[64,1024]{1,0:T(8,128)S(1)}, f32[64,1024]{1,0:T(8,128)S(1)}, u32[]{:S(2)}, u32[]{:S(2)}) collective-permute-start(f32[64,1024]{1,0:T(8,128)S(1)} %get-tuple-element.62), channel_id=1, source_target_pairs={{0,48},{1,193},{2,50},{3,195},{4,52},{5,197},{6,54},{7,199},{8,56}... | collective-permute-start | bytes 786440 | tf_op jit(solution)/shard_map/ppermute | solution.py:455
